TPU v7x, 32 devices: a whole 2x2x4 slice. The times are simulated.
32 devices in a mesh: dp: 8 (over z, x), mp: 4 (over y, core).
Axes of the slice: x: 2, y: 2, z: 4, core: 2. Of those that a mesh axis runs over, the one named last changes fastest.
Arguments:
- tokens: bfloat16 [4096, 1536], P(('dp', 'mp')), may hold values from -6 to 6
- caption: bfloat16 [8, 256, 4096], P('dp'), may hold values from -6 to 6
- condition: float32 [8, 1536], P('dp'), may hold values from -6 to 6
- cotangent: bfloat16 [4096, 1536], P(('dp', 'mp')), may hold values from -6 to 6
- qkv_weight: bfloat16 [3, 1536, 1536], P(None, 'dp', 'mp'), may hold values from -0.15625 to 0.15625
- proj_weight: bfloat16 [1536, 1536], P('mp', 'dp'), may hold values from -0.15625 to 0.15625
- text_weight: bfloat16 [2, 4096, 1536], P(None, 'dp', 'mp'), may hold values from -0.09375 to 0.09375
- ffn_weight: bfloat16 [2, 1536, 4096], P(None, 'dp', 'mp'), may hold values from -0.15625 to 0.15625
- down_weight: bfloat16 [4096, 1536], P('mp', 'dp'), may hold values from -0.09375 to 0.09375
- ada_weight: bfloat16 [1536, 6144], P('dp', 'mp'), may hold values from -0.15625 to 0.15625
- norm_gains: float32 [4, 1536], replicated, may hold values from 0.5 to 1.5
- head_gains: float32 [3, 1536], replicated, may hold values from 0.5 to 1.5
- ada_bias: float32 [6144], replicated, may hold values from -3 to 3
- cross_gate: float32 [24], replicated, may hold values from -1.5 to 1.5
- group_map: int32 [8], replicated, may hold values from 0 to 7, as said below
- grid_width: int32 [8], replicated, may hold values from 32 to 64, as said below
- caption_len: int32 [8], replicated, may hold values from 1 to 256, as said below
Outputs:
- block_out: bfloat16 [4096, 1536], P(('dp', 'mp'))
- grad_tokens: float32 [4096, 1536], P(('dp', 'mp'))
- grad_caption: float32 [8, 256, 4096], P('dp', None, 'mp')
- grad_condition: float32 [8, 1536], P('dp', 'mp')
- grad_qkv: float32 [3, 1536, 1536], P(None, 'dp', 'mp')
- grad_proj: float32 [1536, 1536], P('mp', 'dp')
- grad_text: float32 [2, 4096, 1536], P(None, 'dp', 'mp')
- grad_ffn: float32 [2, 1536, 4096], P(None, 'dp', 'mp')
- grad_down: float32 [4096, 1536], P('mp', 'dp')
- grad_ada: float32 [1536, 6144], P('dp', 'mp')
- grad_norms: float32 [4, 1536], replicated
- grad_heads: float32 [3, 1536], replicated
- grad_bias: float32 [6144], replicated
- grad_gate: float32 [24], replicated
Inputs may be any that keep to these rules, and one draw needn't show every extreme that they name: `group_map`: entry i is the first data index of the group holding index i; groups are runs of 1 to 4 consecutive indices, and some group has exactly 4. `grid_width`: equal within a group; either 32 or 64. `caption_len`: some index has 256.
All inputs are finite; a program needn't handle non-finite values.
Results may differ from a plain program's by a relative error of at most 0.022.
Values may be sent and summed in bfloat16 or wider, within the bound.
No kernel may reach another device: no remote copies, remote signals or barrier semaphores. Data moves between devices by JAX's collectives and lax.ppermute only.
A program may use at most 192 MiB of HBM per device.

v0:
```python
import math

import jax
import jax.numpy as jnp
from jax import lax
from jax.sharding import PartitionSpec as P

HEADS = 24
HD = 64
GMAX = 4


EPS = 1e-06
NEG = -1e30


def passed_along(value, axis, steps):
    count = lax.axis_size(axis)
    initial, last = (max(0, -steps), min(count, count - steps))
    return lax.ppermute(value, axis, [(source, source + steps) for source in range(initial, last)])


def norm_rows(values, weights):
    return values * lax.rsqrt(jnp.mean(values * values, axis=-1, keepdims=True) + EPS) * weights


def angle_tables(positions, widths):
    quarter = HD // 4
    freqs = jnp.exp(jnp.arange(quarter).astype(jnp.float32) * (-math.log(10000.0) / quarter))
    row_pos = (positions // widths).astype(jnp.float32)
    col_pos = (positions % widths).astype(jnp.float32)
    return (row_pos[..., None] * freqs, col_pos[..., None] * freqs)


def rotate(values, row_ang, col_ang):
    quarter = values.shape[-1] // 4
    cos_row = jnp.cos(row_ang)[..., None, :]
    sin_row = jnp.sin(row_ang)[..., None, :]
    cos_col = jnp.cos(col_ang)[..., None, :]
    sin_col = jnp.sin(col_ang)[..., None, :]
    first_a = values[..., :quarter]
    first_b = values[..., quarter : 2 * quarter]
    second_a = values[..., 2 * quarter : 3 * quarter]
    second_b = values[..., 3 * quarter :]
    return jnp.concatenate(
        [
            first_a * cos_row - first_b * sin_row,
            first_a * sin_row + first_b * cos_row,
            second_a * cos_col - second_b * sin_col,
            second_a * sin_col + second_b * cos_col,
        ],
        axis=-1,
    )


def modulate(values, weights, scales):
    return norm_rows(values, weights) * (1.0 + scales)


def gated_add(branch, weights, gates, resid):
    return resid + jnp.tanh(gates) * norm_rows(branch, weights)


def head_norm(values, weights):
    count = values.shape[0]
    return norm_rows(values.reshape(count, -1, HD), weights.reshape(-1, HD))


def swiglu(gate_pre, up_pre):
    return jax.nn.silu(gate_pre) * up_pre


def masked_scores(queries, keys_in, mask_row):
    logits = jnp.einsum(
        "qhe,khe->hqk", queries, keys_in, preferred_element_type=jnp.float32
    ) * HD ** (-0.5)
    if mask_row is None:
        return logits
    return jnp.where(mask_row[None, None, :], logits, NEG)


def keep_state(running):
    return running


def gather_rows(values):
    return lax.all_gather(values, "mp", axis=0, tiled=True)


def sum_rows(values):
    return lax.psum_scatter(
        values.astype(jnp.bfloat16), "mp", scatter_dimension=0, tiled=True
    ).astype(jnp.float32)


def gather_grads(values):
    return lax.all_gather(values, "mp", axis=0, tiled=True)


def sum_input_grads(values):
    return lax.psum_scatter(
        values.astype(jnp.bfloat16), "mp", scatter_dimension=0, tiled=True
    ).astype(jnp.float32)


def local(
    tokens,
    caption,
    condition,
    cotangent,
    qkv_weight,
    proj_weight,
    text_weight,
    ffn_weight,
    down_weight,
    ada_weight,
    norm_gains,
    head_gains,
    ada_bias,
    cross_gate,
    group_map,
    grid_width,
    caption_len,
):
    dp_count = lax.axis_size("dp")
    dp_index = lax.axis_index("dp")
    mp_index = lax.axis_index("mp")
    row_count = tokens.shape[0]
    model_width = tokens.shape[1]
    seq_len = row_count * lax.axis_size("mp")
    local_width = qkv_weight.shape[2]
    local_heads = local_width // HD
    text_len = caption.shape[1]
    score_scale = HD ** (-0.5)
    weight_scale = 1.0 / math.sqrt(seq_len * dp_count)
    query_block = min(512, seq_len)
    query_count = seq_len // query_block
    gathered = (
        lax.all_gather(qkv_weight, "dp", axis=1, tiled=True),
        lax.all_gather(proj_weight, "dp", axis=1, tiled=True),
        lax.all_gather(text_weight, "dp", axis=1, tiled=True),
        lax.all_gather(ffn_weight, "dp", axis=1, tiled=True),
        lax.all_gather(down_weight, "dp", axis=1, tiled=True),
        lax.all_gather(ada_weight, "dp", axis=0, tiled=True),
    )
    qkv_full, proj_full, text_full, ffn_full, down_full, ada_full = gathered
    cond_low = jax.nn.silu(condition).astype(jnp.bfloat16)
    bias_part = lax.dynamic_slice_in_dim(ada_bias, mp_index * model_width, model_width)
    mod_part = jnp.dot(cond_low, ada_full, preferred_element_type=jnp.float32) + bias_part[None, :]
    modulation = lax.all_gather(mod_part, "mp", axis=0, tiled=True)
    scale_attn = modulation[0]
    gate_attn = modulation[1]
    scale_ffn = modulation[2]
    gate_ffn = modulation[3]
    act_rows = tokens.astype(jnp.float32)
    first_in, first_pull = jax.vjp(modulate, act_rows, norm_gains[0], scale_attn)
    first_low = gather_rows(first_in.astype(jnp.bfloat16))
    qkv_pre = jnp.einsum("td,kde->kte", first_low, qkv_full, preferred_element_type=jnp.float32)
    local_gains = lax.dynamic_slice_in_dim(head_gains, mp_index * local_width, local_width, axis=1)
    first_slot = group_map[dp_index]
    positions = (dp_index - first_slot) * seq_len + jnp.arange(seq_len, dtype=jnp.int32)
    row_ang, col_ang = angle_tables(positions, grid_width[dp_index])

    def prep_heads(values, weights):
        return rotate(head_norm(values, weights), row_ang, col_ang)

    query_f, query_pull = jax.vjp(prep_heads, qkv_pre[0], local_gains[0])
    key_f, key_pull = jax.vjp(prep_heads, qkv_pre[1], local_gains[1])
    query_b = query_f.astype(jnp.bfloat16)
    key_b = key_f.astype(jnp.bfloat16)
    value_b = qkv_pre[2].astype(jnp.bfloat16).reshape(seq_len, local_heads, HD)
    text_low = caption[0]
    text_pre = jnp.einsum("cd,kde->kce", text_low, text_full, preferred_element_type=jnp.float32)
    text_key_f, text_key_pull = jax.vjp(head_norm, text_pre[0], local_gains[2])
    text_key_b = text_key_f.astype(jnp.bfloat16)
    text_value_b = text_pre[1].astype(jnp.bfloat16).reshape(text_len, local_heads, HD)
    offsets = list(range(1, GMAX)) + [-offset for offset in range(1, GMAX)]
    key_sets = [(key_b, value_b, text_key_b, text_value_b)]
    sources = [dp_index]
    for offset in offsets:
        key_sets.append(passed_along((key_b, value_b, text_key_b, text_value_b), "dp", offset))
        sources.append(dp_index - offset)
    text_slots = jnp.arange(text_len, dtype=jnp.int32)
    block_live = []
    text_masks = []
    for source in sources:
        clipped = jnp.clip(source, 0, dp_count - 1)
        inside = (source >= 0) & (source < dp_count) & (group_map[clipped] == first_slot)
        block_live.append(inside)
        text_masks.append(text_slots < caption_len[clipped])
    tanh_gate = jnp.tanh(lax.dynamic_slice_in_dim(cross_gate, mp_index * local_heads, local_heads))

    def attend_forward(queries):
        totals = []
        for key_slot, use_mask in ((0, False), (2, True)):
            state = (
                jnp.full((local_heads, query_block), NEG, jnp.float32),
                jnp.zeros((local_heads, query_block), jnp.float32),
            )
            for key_set, live_flag, text_mask in zip(key_sets, block_live, text_masks):

                def update(
                    running,
                    key_set=key_set,
                    text_mask=text_mask,
                    key_slot=key_slot,
                    use_mask=use_mask,
                ):
                    logits = masked_scores(
                        queries, key_set[key_slot], text_mask if use_mask else None
                    )
                    largest = jnp.maximum(running[0], jnp.max(logits, axis=-1))
                    summed = running[1] * jnp.exp(running[0] - largest) + jnp.sum(
                        jnp.exp(logits - largest[..., None]), axis=-1
                    )
                    return (largest, summed)

                state = lax.cond(live_flag, update, keep_state, state)
            totals.append(state[0] + jnp.log(state[1]))
        results = []
        for key_slot, use_mask, log_total in ((0, False, totals[0]), (2, True, totals[1])):
            accum = jnp.zeros((query_block, local_heads, HD), jnp.float32)
            for key_set, live_flag, text_mask in zip(key_sets, block_live, text_masks):

                def add_block(
                    running,
                    key_set=key_set,
                    text_mask=text_mask,
                    key_slot=key_slot,
                    use_mask=use_mask,
                    log_total=log_total,
                ):
                    logits = masked_scores(
                        queries, key_set[key_slot], text_mask if use_mask else None
                    )
                    probs = jnp.exp(logits - log_total[..., None]).astype(jnp.bfloat16)
                    return running + jnp.einsum(
                        "hqk,khe->qhe",
                        probs,
                        key_set[key_slot + 1],
                        preferred_element_type=jnp.float32,
                    )

                accum = lax.cond(live_flag, add_block, keep_state, accum)
            results.append(accum)
        return (results[0], results[1], totals[0], totals[1])

    query_blocks = query_b.reshape(query_count, query_block, local_heads, HD)
    out_self, out_text, total_self, total_text = lax.map(attend_forward, query_blocks)
    combined = out_self + tanh_gate[None, None, :, None] * out_text
    attn_low = combined.reshape(seq_len, local_width).astype(jnp.bfloat16)
    attn_rows = sum_rows(jnp.dot(attn_low, proj_full, preferred_element_type=jnp.float32))
    middle, middle_pull = jax.vjp(gated_add, attn_rows, norm_gains[1], gate_attn, act_rows)
    second_in, second_pull = jax.vjp(modulate, middle, norm_gains[2], scale_ffn)
    second_low = gather_rows(second_in.astype(jnp.bfloat16))
    ffn_pre = jnp.einsum("td,kdf->ktf", second_low, ffn_full, preferred_element_type=jnp.float32)
    hidden_f, swiglu_pull = jax.vjp(swiglu, ffn_pre[0], ffn_pre[1])
    hidden_low = hidden_f.astype(jnp.bfloat16)
    ffn_rows = sum_rows(jnp.dot(hidden_low, down_full, preferred_element_type=jnp.float32))
    result, result_pull = jax.vjp(gated_add, ffn_rows, norm_gains[3], gate_ffn, middle)
    grad_ffn_rows, grad_gain_four, grad_gate_ffn, grad_middle_a = result_pull(
        cotangent.astype(jnp.float32)
    )
    grad_ffn_all = gather_grads(grad_ffn_rows.astype(jnp.bfloat16))
    grad_down = jnp.einsum(
        "tf,td->fd", hidden_low, grad_ffn_all, preferred_element_type=jnp.float32
    )
    grad_hidden = jnp.einsum(
        "td,fd->tf", grad_ffn_all, down_full, preferred_element_type=jnp.float32
    )
    grad_gate_pre, grad_up_pre = swiglu_pull(grad_hidden)
    grad_pre_low = jnp.stack([grad_gate_pre, grad_up_pre]).astype(jnp.bfloat16)
    grad_ffn = jnp.einsum(
        "td,ktf->kdf", second_low, grad_pre_low, preferred_element_type=jnp.float32
    )
    grad_second = sum_input_grads(
        jnp.einsum("ktf,kdf->td", grad_pre_low, ffn_full, preferred_element_type=jnp.float32)
    )
    grad_middle_b, grad_gain_three, grad_scale_ffn = second_pull(grad_second)
    grad_middle = grad_middle_a + grad_middle_b
    grad_attn_rows, grad_gain_two, grad_gate_attn, grad_act_a = middle_pull(grad_middle)
    grad_attn_all = gather_grads(grad_attn_rows.astype(jnp.bfloat16))
    grad_proj = jnp.einsum("te,td->ed", attn_low, grad_attn_all, preferred_element_type=jnp.float32)
    grad_attn = jnp.einsum(
        "td,ed->te", grad_attn_all, proj_full, preferred_element_type=jnp.float32
    )
    grad_attn_blocks = grad_attn.astype(jnp.bfloat16).reshape(
        query_count, query_block, local_heads, HD
    )

    def attend_back(running, inputs):
        grad_sets, gate_sum = running
        queries, grad_out, self_part, text_part, self_total, text_total = inputs
        grad_wide = grad_out.astype(jnp.float32)
        delta_self = jnp.sum(grad_wide * self_part, axis=-1).T
        text_dot = jnp.sum(grad_wide * text_part, axis=-1).T
        delta_text = tanh_gate[:, None] * text_dot
        gate_sum = gate_sum + jnp.sum(text_dot, axis=1)
        grad_query = jnp.zeros((query_block, local_heads, HD), jnp.float32)
        new_sets = []
        for key_set, live_flag, text_mask, grad_set in zip(
            key_sets, block_live, text_masks, grad_sets
        ):

            def back_block(state, key_set=key_set, text_mask=text_mask):
                grad_query_in, (grad_key, grad_value, grad_text_key, grad_text_value) = state
                probs = jnp.exp(masked_scores(queries, key_set[0], None) - self_total[..., None])
                grad_value = grad_value + jnp.einsum(
                    "hqk,qhe->khe",
                    probs.astype(jnp.bfloat16),
                    grad_out,
                    preferred_element_type=jnp.float32,
                )
                grad_probs = jnp.einsum(
                    "qhe,khe->hqk", grad_out, key_set[1], preferred_element_type=jnp.float32
                )
                grad_logits = (probs * (grad_probs - delta_self[..., None])).astype(jnp.bfloat16)
                grad_query_in = (
                    grad_query_in
                    + jnp.einsum(
                        "hqk,khe->qhe", grad_logits, key_set[0], preferred_element_type=jnp.float32
                    )
                    * score_scale
                )
                grad_key = (
                    grad_key
                    + jnp.einsum(
                        "hqk,qhe->khe", grad_logits, queries, preferred_element_type=jnp.float32
                    )
                    * score_scale
                )
                probs = jnp.exp(
                    masked_scores(queries, key_set[2], text_mask) - text_total[..., None]
                )
                grad_text_value = grad_text_value + tanh_gate[None, :, None] * jnp.einsum(
                    "hqk,qhe->khe",
                    probs.astype(jnp.bfloat16),
                    grad_out,
                    preferred_element_type=jnp.float32,
                )
                grad_probs = tanh_gate[:, None, None] * jnp.einsum(
                    "qhe,khe->hqk", grad_out, key_set[3], preferred_element_type=jnp.float32
                )
                grad_logits = (probs * (grad_probs - delta_text[..., None])).astype(jnp.bfloat16)
                grad_query_in = (
                    grad_query_in
                    + jnp.einsum(
                        "hqk,khe->qhe", grad_logits, key_set[2], preferred_element_type=jnp.float32
                    )
                    * score_scale
                )
                grad_text_key = (
                    grad_text_key
                    + jnp.einsum(
                        "hqk,qhe->khe", grad_logits, queries, preferred_element_type=jnp.float32
                    )
                    * score_scale
                )
                return (grad_query_in, (grad_key, grad_value, grad_text_key, grad_text_value))

            grad_query, grad_set = lax.cond(
                live_flag, back_block, keep_state, (grad_query, grad_set)
            )
            new_sets.append(grad_set)
        return ((tuple(new_sets), gate_sum), grad_query)

    zero_set = (
        jnp.zeros((seq_len, local_heads, HD), jnp.float32),
        jnp.zeros((seq_len, local_heads, HD), jnp.float32),
        jnp.zeros((text_len, local_heads, HD), jnp.float32),
        jnp.zeros((text_len, local_heads, HD), jnp.float32),
    )
    start_sets = tuple((zero_set for source in sources))
    (final_sets, gate_sum), grad_query_blocks = lax.scan(
        attend_back,
        (start_sets, jnp.zeros((local_heads,), jnp.float32)),
        (query_blocks, grad_attn_blocks, out_self, out_text, total_self, total_text),
    )
    own_grads = final_sets[0]
    for offset, grad_set in zip(offsets, final_sets[1:]):
        returned = (
            passed_along(grad_set[0].astype(jnp.bfloat16), "dp", -offset).astype(jnp.float32),
            passed_along(grad_set[1].astype(jnp.bfloat16), "dp", -offset).astype(jnp.float32),
            passed_along(grad_set[2].astype(jnp.bfloat16), "dp", -offset).astype(jnp.float32),
            passed_along(grad_set[3].astype(jnp.bfloat16), "dp", -offset).astype(jnp.float32),
        )
        own_grads = tuple(
            (base_item + extra_item for base_item, extra_item in zip(own_grads, returned))
        )
    grad_key_f, grad_value_f, grad_text_key_f, grad_text_value_f = own_grads
    grad_query_pre, grad_head_query = query_pull(
        grad_query_blocks.reshape(seq_len, local_heads, HD)
    )
    grad_key_pre, grad_head_key = key_pull(grad_key_f)
    grad_qkv_low = jnp.stack(
        [grad_query_pre, grad_key_pre, grad_value_f.reshape(seq_len, local_width)]
    ).astype(jnp.bfloat16)
    grad_qkv = jnp.einsum(
        "td,kte->kde", first_low, grad_qkv_low, preferred_element_type=jnp.float32
    )
    grad_first = sum_input_grads(
        jnp.einsum("kte,kde->td", grad_qkv_low, qkv_full, preferred_element_type=jnp.float32)
    )
    grad_act_b, grad_gain_one, grad_scale_attn = first_pull(grad_first)
    grad_tokens = grad_act_a + grad_act_b
    grad_text_key_pre, grad_head_text = text_key_pull(grad_text_key_f)
    grad_text_low = jnp.stack(
        [grad_text_key_pre, grad_text_value_f.reshape(text_len, local_width)]
    ).astype(jnp.bfloat16)
    grad_text = jnp.einsum(
        "cd,kce->kde", text_low, grad_text_low, preferred_element_type=jnp.float32
    )
    grad_text_part = jnp.einsum(
        "kce,kde->cd", grad_text_low, text_full, preferred_element_type=jnp.float32
    )
    mod_grad_part = jnp.stack([grad_scale_attn, grad_gate_attn, grad_scale_ffn, grad_gate_ffn])
    grad_mod = lax.psum_scatter(mod_grad_part, "mp", scatter_dimension=0, tiled=True)
    grad_mod_low = grad_mod.astype(jnp.bfloat16)
    grad_ada = jnp.einsum("od,oe->de", cond_low, grad_mod_low, preferred_element_type=jnp.float32)
    grad_cond_part = jnp.einsum(
        "oe,de->od", grad_mod_low, ada_full, preferred_element_type=jnp.float32
    )
    caption_sum, cond_sum = (
        lax.psum_scatter(
            grad_text_part.astype(jnp.bfloat16), "mp", scatter_dimension=1, tiled=True
        ).astype(jnp.float32),
        lax.psum_scatter(
            grad_cond_part.astype(jnp.bfloat16), "mp", scatter_dimension=1, tiled=True
        ).astype(jnp.float32),
    )
    cond_width = cond_sum.shape[1]
    cond_cols = lax.dynamic_slice_in_dim(condition, mp_index * cond_width, cond_width, axis=1)
    silu_vals, silu_pull = jax.vjp(jax.nn.silu, cond_cols)
    grad_condition = silu_pull(cond_sum)[0] * (1.0 / math.sqrt(seq_len))
    big_grads = (
        lax.psum_scatter(
            (grad_qkv * weight_scale).astype(jnp.bfloat16), "dp", scatter_dimension=1, tiled=True
        ).astype(jnp.float32),
        lax.psum_scatter(
            (grad_proj * weight_scale).astype(jnp.bfloat16), "dp", scatter_dimension=1, tiled=True
        ).astype(jnp.float32),
        lax.psum_scatter(
            (grad_text * weight_scale).astype(jnp.bfloat16), "dp", scatter_dimension=1, tiled=True
        ).astype(jnp.float32),
        lax.psum_scatter(
            (grad_ffn * weight_scale).astype(jnp.bfloat16), "dp", scatter_dimension=1, tiled=True
        ).astype(jnp.float32),
        lax.psum_scatter(
            (grad_down * weight_scale).astype(jnp.bfloat16), "dp", scatter_dimension=1, tiled=True
        ).astype(jnp.float32),
        lax.psum_scatter(
            (grad_ada * weight_scale).astype(jnp.bfloat16), "dp", scatter_dimension=0, tiled=True
        ).astype(jnp.float32),
    )
    norm_grad = (
        jnp.stack([grad_gain_one, grad_gain_two, grad_gain_three, grad_gain_four]) * weight_scale
    )
    head_local = jnp.stack([grad_head_query, grad_head_key, grad_head_text])
    head_grad = (
        lax.dynamic_update_slice_in_dim(
            jnp.zeros((3, model_width), jnp.float32), head_local, mp_index * local_width, 1
        )
        * weight_scale
    )
    bias_grad = (
        lax.dynamic_update_slice_in_dim(
            jnp.zeros((4 * model_width,), jnp.float32),
            grad_mod_low.astype(jnp.float32)[0],
            mp_index * model_width,
            0,
        )
        * weight_scale
    )
    gate_grad = (
        lax.dynamic_update_slice_in_dim(
            jnp.zeros((HEADS,), jnp.float32),
            gate_sum * (1.0 - tanh_gate * tanh_gate),
            mp_index * local_heads,
            0,
        )
        * weight_scale
    )
    small_sums = lax.psum((norm_grad, head_grad, bias_grad, gate_grad), ("dp", "mp"))
    return (
        result.astype(jnp.bfloat16),
        grad_tokens,
        caption_sum[None],
        grad_condition,
        big_grads[0],
        big_grads[1],
        big_grads[2],
        big_grads[3],
        big_grads[4],
        big_grads[5],
        small_sums[0],
        small_sums[1],
        small_sums[2],
        small_sums[3],
    )


def solution(mesh):
    return jax.shard_map(
        local,
        mesh=mesh,
        in_specs=(
            P(("dp", "mp"), None),
            P("dp", None, None),
            P("dp", None),
            P(("dp", "mp"), None),
            P(None, "dp", "mp"),
            P("mp", "dp"),
            P(None, "dp", "mp"),
            P(None, "dp", "mp"),
            P("mp", "dp"),
            P("dp", "mp"),
            P(),
            P(),
            P(),
            P(),
            P(),
            P(),
            P(),
        ),
        out_specs=(
            P(("dp", "mp"), None),
            P(("dp", "mp"), None),
            P("dp", None, "mp"),
            P("dp", "mp"),
            P(None, "dp", "mp"),
            P("mp", "dp"),
            P(None, "dp", "mp"),
            P(None, "dp", "mp"),
            P("mp", "dp"),
            P("dp", "mp"),
            P(),
            P(),
            P(),
            P(),
        ),
        check_vma=False,
    )
```

profile of v0, /device:TPU:0, one launch (start us, length us, event | category | flops | bytes accessed | tf_op | source)
XLA Modules:
  0.0 1946.2 jit_solution(686348161310275932)
XLA Ops:
  12.0 80.8 %all-gather.13.cloned.1.call-done = bf16[1536,1536]{1,0:T(8,128)(2,1)} async-done(((bf16[192,1536]{1,0:T(8,128)(2,1)}), bf16[1536,1536]{1,0:T(8,128)(2,1)}) %all-gather.13.cloned.1.call-update) | async-done | bytes 4718608 | tf_op jit(solution)/shard_map/all_gather | solution.py:144
  131.6 26.8 %all-gather.17.cloned.1.call-done = bf16[3,1536,384]{2,1,0:T(8,128)(2,1)} async-done(((bf16[3,192,384]{2,1,0:T(8,128)(2,1)}), bf16[3,1536,384]{2,1,0:T(8,128)(2,1)}) %all-gather.17.cloned.1.call-update) | async-done | bytes 3538960 | tf_op jit(solution)/shard_map/all_gather | solution.py:139
  158.4 20.4 %all-gather.15.cloned.1.call-done = bf16[512,1536]{1,0:T(8,128)(2,1)} async-done(((bf16[128,1536]{1,0:T(8,128)(2,1)}), bf16[512,1536]{1,0:T(8,128)(2,1)}) %all-gather.15.cloned.1.call-update) | async-done | bytes 1572880 | tf_op jit(solution)/shard_map/all_gather | solution.py:87
  192.8 14.9 collective-permute-done.11
  212.4 16.4 collective-permute-start.2
  228.8 105.7 %all-gather.19.cloned.1.call-done = bf16[2,4096,384]{1,2,0:T(8,128)(2,1)} async-done(((bf16[2,512,384]{1,2,0:T(8,128)(2,1)}), bf16[2,4096,384]{1,2,0:T(8,128)(2,1)}) %all-gather.19.cloned.1.call-update) | async-done | bytes 6291472 | tf_op jit(solution)/shard_map/all_gather | solution.py:141
  387.6 19.6 %collective-permute-start.14 = (bf16[256,6,64]{0,2,1:T(8,128)(2,1)S(1)}, bf16[256,6,64]{0,2,1:T(8,128)(2,1)}, u32[]{:S(2)}, u32[]{:S(2)}) collective-permute-start(bf16[256,6,64]{0,2,1:T(8,128)(2,1)S(1)} %multiply_convert_fusion.22), channel_id=1, source_target_pairs={{0,12},{4,16},{8,20},{12,24},{16,28},{1,13},{5,17},{9,21},{13,25},... | collective-permute-start | bytes 589832 | tf_op jit(solution)/shard_map/ppermute | solution.py:20
  494.8 28.9 %reduce-scatter.16.cloned.1.call-done = bf16[128,1536]{1,0:T(8,128)(2,1)} async-done(((bf16[512,1536]{1,0:T(8,128)(2,1)}), bf16[128,1536]{1,0:T(8,128)(2,1)}) %reduce-scatter.16.cloned.1.call-update) | async-done | bytes 393232 | tf_op jit(solution)/shard_map/reduce_scatter | solution.py:91
  529.7 95.5 %all-gather.25.cloned.1.call-done = bf16[2,1536,1024]{2,1,0:T(8,128)(2,1)} async-done(((bf16[2,192,1024]{2,1,0:T(8,128)(2,1)}), bf16[2,1536,1024]{2,1,0:T(8,128)(2,1)}) %all-gather.25.cloned.1.call-update) | async-done | bytes 6291472 | tf_op jit(solution)/shard_map/all_gather | solution.py:142
  625.2 20.1 %all-gather.23.cloned.1.call-done = bf16[512,1536]{1,0:T(8,128)(2,1)} async-done(((bf16[128,1536]{1,0:T(8,128)(2,1)}), bf16[512,1536]{1,0:T(8,128)(2,1)}) %all-gather.23.cloned.1.call-update) | async-done | bytes 1572880 | tf_op jit(solution)/shard_map/all_gather | solution.py:87
  654.9 53.3 %all-gather.27.cloned.1.call-done = bf16[1024,1536]{0,1:T(8,128)(2,1)} async-done(((bf16[1024,192]{0,1:T(8,128)(2,1)}), bf16[1024,1536]{0,1:T(8,128)(2,1)}) %all-gather.27.cloned.1.call-update) | async-done | bytes 3145744 | tf_op jit(solution)/shard_map/all_gather | solution.py:143
  713.4 26.9 %reduce-scatter.18.cloned.1.call-done = bf16[128,1536]{1,0:T(8,128)(2,1)} async-done(((bf16[512,1536]{1,0:T(8,128)(2,1)}), bf16[128,1536]{1,0:T(8,128)(2,1)}) %reduce-scatter.18.cloned.1.call-update) | async-done | bytes 393232 | tf_op jit(solution)/shard_map/reduce_scatter | solution.py:91
  746.4 19.3 all-gather.29.cloned.1.call-done
  780.7 28.3 %reduce-scatter.20.cloned.1.call-done = bf16[128,1536]{1,0:T(8,128)(2,1)} async-done(((bf16[512,1536]{1,0:T(8,128)(2,1)}), bf16[128,1536]{1,0:T(8,128)(2,1)}) %reduce-scatter.20.cloned.1.call-update) | async-done | bytes 393232 | tf_op jit(solution)/shard_map/reduce_scatter | solution.py:101
  818.3 18.9 all-gather.31.cloned.1.call-done
  871.9 16.7 conditional.67
  890.4 17.7 collective-permute-start.33
  908.1 15.5 conditional.68
  924.8 15.8 conditional.69
  944.4 22.9 %collective-permute-start.35 = (bf16[512,6,64]{0,2,1:T(8,128)(2,1)S(1)}, bf16[512,6,64]{0,2,1:T(8,128)(2,1)S(1)}, u32[]{:S(2)}, u32[]{:S(2)}) collective-permute-start(bf16[512,6,64]{0,2,1:T(8,128)(2,1)S(1)} %convert_element_type.554), channel_id=1, source_target_pairs={{0,12},{4,16},{8,20},{12,24},{16,28},{1,13},{5,17},{9,21},{13,25},... | collective-permute-start | bytes 1179656 | tf_op jit(solution)/shard_map/ppermute | solution.py:20
  1019.4 16.5 copy.123
  1064.4 18.8 collective-permute-start.46
  1103.9 30.2 %collective-permute-start.39 = (bf16[256,6,64]{0,2,1:T(8,128)(2,1)}, bf16[256,6,64]{0,2,1:T(8,128)(2,1)}, u32[]{:S(2)}, u32[]{:S(2)}) collective-permute-start(bf16[256,6,64]{0,2,1:T(8,128)(2,1)} %convert_element_type.564), channel_id=1, source_target_pairs={{0,4},{4,8},{8,12},{12,16},{16,20},{20,24},{24,28},{1,5},{5,9},{9,... | collective-permute-start | bytes 589832 | tf_op jit(solution)/shard_map/ppermute | solution.py:20
  1207.7 96.1 %all-reduce.14.cloned.1.call-done = bf16[2,1536,1024]{2,0,1:T(2,128)(2,1)} async-done(((bf16[2,1536,1024]{2,0,1:T(2,128)(2,1)}), bf16[2,1536,1024]{2,0,1:T(2,128)(2,1)}) %all-reduce.14.cloned.1.call-update) | async-done | bytes 6291472
  1307.2 74.0 %reduce-scatter.30.cloned.1.call-done = bf16[1024,192]{0,1:T(8,128)(2,1)} async-done(((bf16[1024,1536]{0,1:T(8,128)(2,1)}), bf16[1024,192]{0,1:T(8,128)(2,1)}) %reduce-scatter.30.cloned.1.call-update) | async-done | bytes 393232 | tf_op jit(solution)/shard_map/reduce_scatter | solution.py:448
  1383.1 65.6 %reduce-scatter.26.cloned.1.call-done = bf16[384,192]{0,1:T(8,128)(2,1)} async-done(((bf16[384,1536]{0,1:T(8,128)(2,1)}), bf16[384,192]{0,1:T(8,128)(2,1)}) %reduce-scatter.26.cloned.1.call-update) | async-done | bytes 147472 | tf_op jit(solution)/shard_map/reduce_scatter | solution.py:439
  1454.0 17.6 reduce-scatter.34.cloned.1.call-done
  1473.2 32.6 %reduce-scatter.24.cloned.1.call-done = bf16[256,1024]{1,0:T(8,128)(2,1)} async-done(((bf16[256,4096]{1,0:T(8,128)(2,1)}), bf16[256,1024]{1,0:T(8,128)(2,1)}) %reduce-scatter.24.cloned.1.call-update) | async-done | bytes 524304 | tf_op jit(solution)/shard_map/reduce_scatter | solution.py:424
  1507.9 80.5 %reduce-scatter.36.cloned.1.call-done = bf16[192,1152]{1,0:T(8,128)(2,1)} async-done(((bf16[1536,1152]{1,0:T(8,128)(2,1)}), bf16[192,1152]{1,0:T(8,128)(2,1)}) %reduce-scatter.36.cloned.1.call-update) | async-done | bytes 442384
  1593.3 116.6 %reduce-scatter.28.cloned.1.call-done = bf16[2,512,384]{1,2,0:T(8,128)(2,1)} async-done(((bf16[2,4096,384]{1,2,0:T(8,128)(2,1)}), bf16[2,512,384]{1,2,0:T(8,128)(2,1)}) %reduce-scatter.28.cloned.1.call-update) | async-done | bytes 786448 | tf_op jit(solution)/shard_map/reduce_scatter | solution.py:442
  1712.5 95.5 %reduce-scatter.32.cloned.1.call-done = bf16[192,1536]{1,0:T(8,128)(2,1)} async-done(((bf16[1536,1536]{1,0:T(8,128)(2,1)}), bf16[192,1536]{1,0:T(8,128)(2,1)}) %reduce-scatter.32.cloned.1.call-update) | async-done | bytes 589840 | tf_op jit(solution)/shard_map/reduce_scatter | solution.py:451
  1810.2 123.8 %all-reduce.16.cloned.1.call-done = (f32[4,1536]{1,0:T(4,128)}, f32[3,1536]{1,0:T(4,128)}, f32[6144]{0:T(1024)}, f32[24]{0:T(128)}) async-done(((f32[4,1536]{1,0:T(4,128)}, f32[3,1536]{1,0:T(4,128)}, f32[6144]{0:T(1024)}, f32[24]{0:T(128)}), (f32[4,1536]{1,0:T(4,128)}, f32[3,1536]{1,0:T(4,128)}, f32[6144]{0:T(1024)}, f32[24]{0:T(128)})) %all-reduce.16.cloned.1.call-update) | async-done | bytes 67696 | tf_op jit(solution)/shard_map/psum | solution.py:483
  (764 shorter events, 617.5 us)
Async XLA Ops:
  7.2 85.6 %all-gather.13.cloned.1.call-start = ((), (), s32[]{:S(2)}) async-start(), calls=%async_computation.11 | async-start | bytes 5308416 | tf_op jit(solution)/shard_map/all_gather | solution.py:144
  7.9 150.4 %all-gather.17.cloned.1.call-start = ((), (), s32[]{:S(2)}) async-start(), calls=%async_computation.13 | async-start | bytes 3981312 | tf_op jit(solution)/shard_map/all_gather | solution.py:139
  8.7 170.1 %all-gather.15.cloned.1.call-start = ((), (), s32[]{:S(2)}) async-start(), calls=%async_computation.12 | async-start | bytes 1966080 | tf_op jit(solution)/shard_map/all_gather | solution.py:87
  103.6 231.0 %all-gather.19.cloned.1.call-start = ((), (), s32[]{:S(2)}) async-start(), calls=%async_computation.14 | async-start | bytes 7077888 | tf_op jit(solution)/shard_map/all_gather | solution.py:141
  106.0 384.4 %all-gather.21.cloned.1.call-start = ((), (), s32[]{:S(2)}) async-start(), calls=%async_computation.15 | async-start | bytes 1327104 | tf_op jit(solution)/shard_map/all_gather | solution.py:140
  106.5 417.2 %reduce-scatter.16.cloned.1.call-start = ((), (), s32[]{:S(2)}) async-start(), calls=%async_computation.16 | async-start | bytes 1966080 | tf_op jit(solution)/shard_map/reduce_scatter | solution.py:91
  186.9 152.5 %collective-permute-start.9 = (bf16[512,6,64]{0,2,1:T(8,128)(2,1)}, bf16[512,6,64]{0,2,1:T(8,128)(2,1)}, u32[]{:S(2)}, u32[]{:S(2)}) collective-permute-start(bf16[512,6,64]{0,2,1:T(8,128)(2,1)} %bitcast.68), channel_id=1, source_target_pairs={{4,0},{8,4},{12,8},{16,12},{20,16},{24,20},{28,24},{5,1},{9,5},{13... | collective-permute-start | bytes 1179656 | tf_op jit(solution)/shard_map/ppermute | solution.py:20
  189.0 151.7 %collective-permute-start.5 = (bf16[512,6,64]{0,2,1:T(8,128)(2,1)S(1)}, bf16[512,6,64]{0,2,1:T(8,128)(2,1)}, u32[]{:S(2)}, u32[]{:S(2)}) collective-permute-start(bf16[512,6,64]{0,2,1:T(8,128)(2,1)S(1)} %pad_maximum_fusion.7), channel_id=1, source_target_pairs={{12,0},{16,4},{20,8},{24,12},{28,16},{13,1},{17,5},{21,9},{25,13},... | collective-permute-start | bytes 1179656 | tf_op jit(solution)/shard_map/ppermute | solution.py:20
  190.3 151.7 %collective-permute-start.4 = (bf16[512,6,64]{0,2,1:T(8,128)(2,1)S(1)}, bf16[512,6,64]{0,2,1:T(8,128)(2,1)}, u32[]{:S(2)}, u32[]{:S(2)}) collective-permute-start(bf16[512,6,64]{0,2,1:T(8,128)(2,1)S(1)} %pad_maximum_fusion.7), channel_id=1, source_target_pairs={{8,0},{12,4},{16,8},{20,12},{24,16},{28,20},{9,1},{13,5},{17,9},{2... | collective-permute-start | bytes 1179656 | tf_op jit(solution)/shard_map/ppermute | solution.py:20
  207.7 139.1 %collective-permute-start.3 = (bf16[512,6,64]{0,2,1:T(8,128)(2,1)S(1)}, bf16[512,6,64]{0,2,1:T(8,128)(2,1)}, u32[]{:S(2)}, u32[]{:S(2)}) collective-permute-start(bf16[512,6,64]{0,2,1:T(8,128)(2,1)S(1)} %pad_maximum_fusion.7), channel_id=1, source_target_pairs={{4,0},{8,4},{12,8},{16,12},{20,16},{24,20},{28,24},{5,1},{9,5},{13... | collective-permute-start | bytes 1179656 | tf_op jit(solution)/shard_map/ppermute | solution.py:20
  212.4 136.5 %collective-permute-start.2 = (bf16[512,6,64]{0,2,1:T(8,128)(2,1)S(1)}, bf16[512,6,64]{0,2,1:T(8,128)(2,1)}, u32[]{:S(2)}, u32[]{:S(2)}) collective-permute-start(bf16[512,6,64]{0,2,1:T(8,128)(2,1)S(1)} %pad_maximum_fusion.7), channel_id=1, source_target_pairs={{0,12},{4,16},{8,20},{12,24},{16,28},{1,13},{5,17},{9,21},{13,25},... | collective-permute-start | bytes 1179656 | tf_op jit(solution)/shard_map/ppermute | solution.py:20
  383.7 64.4 %collective-permute-start.17 = (bf16[256,6,64]{0,2,1:T(8,128)(2,1)S(1)}, bf16[256,6,64]{0,2,1:T(8,128)(2,1)}, u32[]{:S(2)}, u32[]{:S(2)}) collective-permute-start(bf16[256,6,64]{0,2,1:T(8,128)(2,1)S(1)} %multiply_convert_fusion.22), channel_id=1, source_target_pairs={{12,0},{16,4},{20,8},{24,12},{28,16},{13,1},{17,5},{21,9},{25,13},... | collective-permute-start | bytes 589832 | tf_op jit(solution)/shard_map/ppermute | solution.py:20
  494.0 131.2 %all-gather.25.cloned.1.call-start = ((), (), s32[]{:S(2)}) async-start(), calls=%async_computation.18 | async-start | bytes 7077888 | tf_op jit(solution)/shard_map/all_gather | solution.py:142
  494.7 150.5 %all-gather.23.cloned.1.call-start = ((), (), s32[]{:S(2)}) async-start(), calls=%async_computation.17 | async-start | bytes 1966080 | tf_op jit(solution)/shard_map/all_gather | solution.py:87
  528.9 179.2 %all-gather.27.cloned.1.call-start = ((), (), s32[]{:S(2)}) async-start(), calls=%async_computation.19 | async-start | bytes 3538944 | tf_op jit(solution)/shard_map/all_gather | solution.py:143
  529.7 210.7 %reduce-scatter.18.cloned.1.call-start = ((), (), s32[]{:S(2)}) async-start(), calls=%async_computation.20 | async-start | bytes 1966080 | tf_op jit(solution)/shard_map/reduce_scatter | solution.py:91
  817.3 333.3 %reduce-scatter.22.cloned.1.call-start = ((), (), s32[]{:S(2)}) async-start(), calls=%async_computation.24 | async-start | bytes 1966080 | tf_op jit(solution)/shard_map/reduce_scatter | solution.py:101
  857.8 85.1 %collective-permute-start.30 = (bf16[512,6,64]{0,2,1:T(8,128)(2,1)}, bf16[512,6,64]{0,2,1:T(8,128)(2,1)}, u32[]{:S(2)}, u32[]{:S(2)}) collective-permute-start(bf16[512,6,64]{0,2,1:T(8,128)(2,1)} %convert_element_type.544), channel_id=1, source_target_pairs={{4,0},{8,4},{12,8},{16,12},{20,16},{24,20},{28,24},{5,1},{9,5},{13... | collective-permute-start | bytes 1179656 | tf_op jit(solution)/shard_map/ppermute | solution.py:20
  859.9 84.5 %collective-permute-start.24 = (bf16[512,6,64]{0,2,1:T(8,128)(2,1)}, bf16[512,6,64]{0,2,1:T(8,128)(2,1)}, u32[]{:S(2)}, u32[]{:S(2)}) collective-permute-start(bf16[512,6,64]{0,2,1:T(8,128)(2,1)} %convert_element_type.532), channel_id=1, source_target_pairs={{4,0},{8,4},{12,8},{16,12},{20,16},{24,20},{28,24},{5,1},{9,5},{13... | collective-permute-start | bytes 1179656 | tf_op jit(solution)/shard_map/ppermute | solution.py:20
  865.4 102.3 %collective-permute-start.31 = (bf16[512,6,64]{0,2,1:T(8,128)(2,1)}, bf16[512,6,64]{0,2,1:T(8,128)(2,1)}, u32[]{:S(2)}, u32[]{:S(2)}) collective-permute-start(bf16[512,6,64]{0,2,1:T(8,128)(2,1)} %convert_element_type.546), channel_id=1, source_target_pairs={{8,0},{12,4},{16,8},{20,12},{24,16},{28,20},{9,1},{13,5},{17,9},{2... | collective-permute-start | bytes 1179656 | tf_op jit(solution)/shard_map/ppermute | solution.py:20
  870.6 98.4 %collective-permute-start.32 = (bf16[512,6,64]{0,2,1:T(8,128)(2,1)}, bf16[512,6,64]{0,2,1:T(8,128)(2,1)}, u32[]{:S(2)}, u32[]{:S(2)}) collective-permute-start(bf16[512,6,64]{0,2,1:T(8,128)(2,1)} %convert_element_type.548), channel_id=1, source_target_pairs={{12,0},{16,4},{20,8},{24,12},{28,16},{13,1},{17,5},{21,9},{25,13},... | collective-permute-start | bytes 1179656 | tf_op jit(solution)/shard_map/ppermute | solution.py:20
  890.4 79.9 %collective-permute-start.33 = (bf16[512,6,64]{0,2,1:T(8,128)(2,1)}, bf16[512,6,64]{0,2,1:T(8,128)(2,1)}, u32[]{:S(2)}, u32[]{:S(2)}) collective-permute-start(bf16[512,6,64]{0,2,1:T(8,128)(2,1)} %convert_element_type.550), channel_id=1, source_target_pairs={{0,4},{4,8},{8,12},{12,16},{16,20},{20,24},{24,28},{1,5},{5,9},{9,... | collective-permute-start | bytes 1179656 | tf_op jit(solution)/shard_map/ppermute | solution.py:20
  1011.3 292.5 %all-reduce.14.cloned.1.call-start = ((), (), s32[]{:S(2)}) async-start(), calls=%async_computation.32 | async-start | bytes 12582912
  1035.9 345.3 %reduce-scatter.30.cloned.1.call-start = ((), (), s32[]{:S(2)}) async-start(), calls=%async_computation.28 | async-start | bytes 3538944 | tf_op jit(solution)/shard_map/reduce_scatter | solution.py:448
  1042.1 406.6 %reduce-scatter.26.cloned.1.call-start = ((), (), s32[]{:S(2)}) async-start(), calls=%async_computation.26 | async-start | bytes 1327104 | tf_op jit(solution)/shard_map/reduce_scatter | solution.py:439
  1050.9 420.7 %reduce-scatter.34.cloned.1.call-start = ((), (), s32[]{:S(2)}) async-start(), calls=%async_computation.30 | async-start | bytes 491520
  1064.4 69.7 %collective-permute-start.46 = (bf16[256,6,64]{0,2,1:T(8,128)(2,1)S(1)}, bf16[256,6,64]{0,2,1:T(8,128)(2,1)S(1)}, u32[]{:S(2)}, u32[]{:S(2)}) collective-permute-start(bf16[256,6,64]{0,2,1:T(8,128)(2,1)S(1)} %convert_element_type.578), channel_id=1, source_target_pairs={{0,8},{4,12},{8,16},{12,20},{16,24},{20,28},{1,9},{5,13},{9,17},{1... | collective-permute-start | bytes 589832 | tf_op jit(solution)/shard_map/ppermute | solution.py:20
  1169.5 336.2 %reduce-scatter.24.cloned.1.call-start = ((), (), s32[]{:S(2)}) async-start(), calls=%async_computation.25 | async-start | bytes 2621440 | tf_op jit(solution)/shard_map/reduce_scatter | solution.py:424
  1175.8 412.5 %reduce-scatter.36.cloned.1.call-start = ((), (), s32[]{:S(2)}) async-start(), calls=%async_computation.31 | async-start | bytes 3981312
  1194.3 515.6 %reduce-scatter.28.cloned.1.call-start = ((), (), s32[]{:S(2)}) async-start(), calls=%async_computation.27 | async-start | bytes 7077888 | tf_op jit(solution)/shard_map/reduce_scatter | solution.py:442
  1199.7 608.3 %reduce-scatter.32.cloned.1.call-start = ((), (), s32[]{:S(2)}) async-start(), calls=%async_computation.29 | async-start | bytes 5308416 | tf_op jit(solution)/shard_map/reduce_scatter | solution.py:451
  1204.2 729.8 %all-reduce.16.cloned.1.call-start = ((), (), s32[]{:S(2)}) async-start(), calls=%async_computation.33 | async-start | bytes 148480 | tf_op jit(solution)/shard_map/psum | solution.py:483
  (197 other events, 6962.4 us)
Sparse Core Ops, SparseCore 0:
  10.2 82.5 all-gather.12
  95.0 63.3 all-gather.16
  160.5 18.1 all-gather.14
  181.2 153.2 all-gather.18
  336.6 42.1 all-gather.20
  494.1 29.5 reduce-scatter.15
  526.2 99.0 all-gather.24
  627.4 17.8 all-gather.22
  647.7 60.4 all-gather.26
  713.5 26.8 reduce-scatter.17
  746.1 19.6 all-gather.28
  780.7 28.1 reduce-scatter.19
  817.5 19.6 all-gather.30
  1011.5 44.7 reduce-scatter.21
  1059.9 243.9 all-reduce.13
  1307.7 73.3 reduce-scatter.29
  1385.4 63.3 reduce-scatter.25
  1451.8 19.7 reduce-scatter.33
  1474.3 31.4 reduce-scatter.23
  1509.2 79.1 reduce-scatter.35
  1592.0 117.8 reduce-scatter.27
  1713.6 94.3 reduce-scatter.31
  1814.7 119.2 all-reduce.15
where the time goes:
time: 1950 us
  waiting for transfers between devices  1260 us (65%)
  starting transfers between devices  246 us (13%)
  matrix products  190 us (10%)
  other arithmetic  110 us (6%)
  local copies, waits for them, and re-layouts  88.5 us (5%)
  between operations  29.3 us (2%)
    ppermute x48, starting transfers between devices, passed_along(): lax.ppermute(value, axis, [(source, source + steps) for source in range(i...  244 us
    unnamed x26, waiting for transfers between devices  198 us
    psum x1, waiting for transfers between devices, local(): lax.psum((norm_grad, head_grad, bias_grad, gate_grad), ('dp', 'mp'))  124 us
    reduce_scatter x1, waiting for transfers between devices, local(): lax.psum_scatter((grad_text * weight_scale).astype(jnp.bfloat16), 'dp', s...  117 us
    all_gather x1, waiting for transfers between devices, local(): lax.all_gather(text_weight, 'dp', axis=1, tiled=True)  106 us
    reduce_scatter x1, waiting for transfers between devices, local(): lax.psum_scatter((grad_ada * weight_scale).astype(jnp.bfloat16), 'dp', sc...  95.5 us
    all_gather x1, waiting for transfers between devices, local(): lax.all_gather(ffn_weight, 'dp', axis=1, tiled=True)  95.5 us
    all_gather x1, waiting for transfers between devices, local(): lax.all_gather(ada_weight, 'dp', axis=0, tiled=True)  80.8 us
  transfers between devices with their start and end apart: 71, of which 27 were waited for; matrix products, arithmetic and copies ran while one was open for 16% of the time, Pallas kernels for 0%

commit v1 on v0

v1 whole, which is shorter than its diff:
```python
import functools
import math

import jax
import jax.numpy as jnp
from jax import lax
from jax.experimental import pallas as pl
from jax.experimental.pallas import tpu as pltpu
from jax.sharding import PartitionSpec as P

HEADS = 24
HD = 64
PAIR = 2 * HD
EPS = 1e-06
NEG = -1e30
SCALE = HD ** (-0.5)
BF = jnp.bfloat16
F32 = jnp.float32
NN = (((1,), (0,)), ((), ()))
NT = (((1,), (1,)), ((), ()))
TN = (((0,), (0,)), ((), ()))


def mm(left, right, dims):
    return lax.dot_general(left, right, dims, preferred_element_type=F32)


def exact(left, right, dims):
    return lax.dot_general(
        left, right, dims, preferred_element_type=F32, precision=lax.Precision.HIGHEST
    )


def ring_order(count):
    return list(range(0, count, 2)) + list(range(1, count, 2))[::-1]


def ring_pairs(count, step):
    order = ring_order(count)
    return [(order[k], order[(k + step) % count]) for k in range(count)]


def ring_gather(shard):
    count = lax.axis_size("dp")
    half = shard.shape[0] // 2
    first, second = [shard[:half]], [shard[half:]]
    for _ in range(count - 1):
        first.append(lax.ppermute(first[-1], "dp", ring_pairs(count, 1)))
        second.append(lax.ppermute(second[-1], "dp", ring_pairs(count, -1)))
    return first, second


def ring_scatter(first, second):
    count = lax.axis_size("dp")
    sums = []
    for own, step in ((first, 1), (second, -1)):
        total = own(1)
        for k in range(2, count + 1):
            moved = lax.ppermute(total.astype(BF), "dp", ring_pairs(count, step))
            total = moved.astype(F32) + own(k % count).astype(F32)
        sums.append(total)
    return sums


def swap(value, axis, bit):
    count = lax.axis_size(axis)
    return lax.ppermute(value, axis, [(i, i ^ bit) for i in range(count)])


def sum_all(value, axis):
    bit = 1
    while bit < lax.axis_size(axis):
        value = value + swap(value, axis, bit)
        bit *= 2
    return value


def gather_in_order(value, axis, index):
    bit = 1
    while bit < lax.axis_size(axis):
        other = swap(value, axis, bit)
        high = (index & bit) != 0
        value = jnp.concatenate(
            [jnp.where(high, other, value), jnp.where(high, value, other)], axis=0
        )
        bit *= 2
    return value


def rows_from_mp(value):
    far = swap(value, "mp", 2)
    near = swap(value, "mp", 1)
    return jnp.concatenate([value, near, far, swap(far, "mp", 1)], axis=0)


def sum_to_mp(value):
    count = value.shape[0] // 4
    blocks = [value[k * count : (k + 1) * count] for k in range(4)]
    far = blocks[2].astype(F32) + swap(blocks[3].astype(BF), "mp", 1).astype(F32)
    near = blocks[0].astype(F32) + swap(blocks[1].astype(BF), "mp", 1).astype(F32)
    return near + swap(far.astype(BF), "mp", 2).astype(F32)


def shifted(steps, keep=lambda i: True):
    count = lax.axis_size("dp")
    return [(i, i + steps) for i in range(count) if keep(i) and 0 <= i + steps < count]


def even(i):
    return i % 2 == 0


def odd(i):
    return i % 2 == 1


def send_sets(own, is_odd):
    beside = swap(own, "dp", 1)
    low = lax.ppermute(own, "dp", shifted(2))
    high = lax.ppermute(own, "dp", shifted(-2))
    across = swap(jnp.where(is_odd, low, high), "dp", 1)
    third = lax.ppermute(beside, "dp", shifted(-2, even) + shifted(2, odd))
    fourth = lax.ppermute(across, "dp", shifted(2, even) + shifted(-2, odd))
    return [own, beside, low, high, across, third, fourth]


def set_offsets(is_odd):
    sign = jnp.where(is_odd, -1, 1)
    return [0 * sign, sign, 0 * sign - 2, 0 * sign + 2, -sign, 3 * sign, -3 * sign]


def return_sets(grads, is_odd):
    own, beside, low, high, across, third, fourth = [grad.astype(F32) for grad in grads]
    across = across + lax.ppermute(
        fourth.astype(BF), "dp", shifted(-2, even) + shifted(2, odd)
    ).astype(F32)
    beside = beside + lax.ppermute(
        third.astype(BF), "dp", shifted(2, even) + shifted(-2, odd)
    ).astype(F32)
    crossed = swap(across.astype(BF), "dp", 1).astype(F32)
    low = low + jnp.where(is_odd, crossed, 0.0)
    high = high + jnp.where(is_odd, 0.0, crossed)
    return (
        own
        + swap(beside.astype(BF), "dp", 1).astype(F32)
        + lax.ppermute(low.astype(BF), "dp", shifted(-2)).astype(F32)
        + lax.ppermute(high.astype(BF), "dp", shifted(2)).astype(F32)
    )


def norm_rows(values, weights):
    return values * lax.rsqrt(jnp.mean(values * values, axis=-1, keepdims=True) + EPS) * weights


def modulate(values, weights, scales):
    return norm_rows(values, weights) * (1.0 + scales)


def gated_add(branch, weights, gates, resid):
    return resid + jnp.tanh(gates) * norm_rows(branch, weights)


def swiglu(gate_pre, up_pre):
    return jax.nn.silu(gate_pre) * up_pre


def lanes(rows):
    return lax.broadcasted_iota(jnp.int32, (rows, PAIR), 1)


def head_sum(values):
    low = lanes(values.shape[0]) < HD
    first = jnp.sum(jnp.where(low, values, 0.0), axis=-1, keepdims=True)
    second = jnp.sum(jnp.where(low, 0.0, values), axis=-1, keepdims=True)
    return jnp.where(low, first, second)


def partner(values):
    quarter = HD // 4
    first = (lanes(values.shape[0]) % (2 * quarter)) < quarter
    return jnp.where(
        first, pltpu.roll(values, PAIR - quarter, 1), pltpu.roll(values, quarter, 1)
    )


def normed(values):
    return values * lax.rsqrt(head_sum(values * values) / HD + EPS)


def prep_kernel(pre_ref, gains_ref, cos_ref, sin_ref, out_ref):
    width = out_ref.shape[1]
    rows = pre_ref.shape[0]
    cos, sin = cos_ref[...], sin_ref[...]
    for part in range(2):
        for start in range(0, width, PAIR):
            here = pl.ds(part * width + start, PAIR)
            turned = normed(pre_ref[:, here]) * gains_ref[part : part + 1, pl.ds(start, PAIR)]
            if part == 0:
                turned = turned * cos + partner(turned) * sin
                out_ref[pl.ds(0, rows), pl.ds(start, PAIR)] = turned.astype(BF)
            else:
                turned = turned * cos + partner(turned) * sin
                out_ref[pl.ds(rows, rows), pl.ds(start, PAIR)] = turned.astype(BF)
    out_ref[pl.ds(2 * rows, rows), :] = pre_ref[:, pl.ds(2 * width, width)].astype(BF)


def text_prep_kernel(pre_ref, gains_ref, out_ref):
    rows, width = pre_ref.shape[0], out_ref.shape[1]
    for start in range(0, width, PAIR):
        here = pl.ds(start, PAIR)
        value = normed(pre_ref[:, here]) * gains_ref[2:3, here]
        out_ref[pl.ds(0, rows), here] = value.astype(BF)
    out_ref[pl.ds(rows, rows), :] = pre_ref[:, pl.ds(width, width)].astype(BF)


def norm_back(pre, gains, grad):
    ratio = lax.rsqrt(head_sum(pre * pre) / HD + EPS)
    scaled = grad * gains
    grad_pre = ratio * scaled - pre * (ratio * ratio * ratio) * (head_sum(pre * scaled) / HD)
    return grad_pre, jnp.sum(grad * pre * ratio, axis=0, keepdims=True)


def prep_back_kernel(pre_ref, gains_ref, cos_ref, sin_ref, query_ref, set_ref, out_ref, head_ref):
    rows, width = query_ref.shape
    cos, sin = cos_ref[...], sin_ref[...]
    head_ref[...] = jnp.zeros_like(head_ref)
    for part in range(2):
        for start in range(0, width, PAIR):
            here = pl.ds(start, PAIR)
            there = pl.ds(part * width + start, PAIR)
            grad = query_ref[:, here] if part == 0 else set_ref[pl.ds(0, rows), here]
            grad = grad * cos - partner(grad) * sin
            grad_pre, grad_gain = norm_back(pre_ref[:, there], gains_ref[part : part + 1, here], grad)
            out_ref[:, there] = grad_pre.astype(BF)
            head_ref[part : part + 1, here] = grad_gain
    out_ref[:, pl.ds(2 * width, width)] = set_ref[pl.ds(rows, rows), :].astype(BF)


def text_back_kernel(pre_ref, gains_ref, set_ref, out_ref, head_ref):
    rows, width = pre_ref.shape[0], set_ref.shape[1]
    head_ref[...] = jnp.zeros_like(head_ref)
    for start in range(0, width, PAIR):
        here = pl.ds(start, PAIR)
        grad_pre, grad_gain = norm_back(
            pre_ref[:, here], gains_ref[2:3, here], set_ref[pl.ds(0, rows), here]
        )
        out_ref[:, here] = grad_pre.astype(BF)
        head_ref[0:1, here] = grad_gain
    out_ref[:, pl.ds(width, width)] = set_ref[pl.ds(rows, rows), :].astype(BF)


def split_pair(values):
    low = lanes(values.shape[0]) < HD
    zero = jnp.zeros_like(values)
    return jnp.where(low, values, zero), jnp.where(low, zero, values)


def forward_kernel(live_ref, gate_ref, query_ref, bias_ref, *refs):
    count = (len(refs) - 9) // 2
    self_refs, text_refs = refs[:count], refs[count : 2 * count]
    attn_ref, self_ref, text_ref, self_sum_ref, text_sum_ref = refs[2 * count : 2 * count + 5]
    totals = refs[2 * count + 5 :]
    rows = query_ref.shape[0]
    low = lanes(rows) < HD
    for total in totals:
        total[...] = jnp.zeros_like(total)

    for index in range(count):

        @pl.when(live_ref[index] > 0)
        def _(index=index):
            queries = split_pair(query_ref[...] * jnp.asarray(SCALE, BF))
            for slot, source in ((0, self_refs[index]), (1, text_refs[index])):
                depth = source.shape[0] // 2
                keys, values = source[pl.ds(0, depth), :], source[pl.ds(depth, depth), :]
                outs, sums = [], []
                for query in queries:
                    logits = mm(query, keys, NT)
                    if slot:
                        logits = logits + bias_ref[index : index + 1, :]
                    probs = jnp.exp(logits)
                    sums.append(jnp.sum(probs, axis=-1, keepdims=True))
                    outs.append(mm(probs.astype(BF), values, NN))
                totals[slot][...] += jnp.where(low, outs[0], outs[1])
                totals[2 + slot][...] += jnp.where(low, sums[0], sums[1])

    pair = pl.program_id(0)
    gate = jnp.where(low, gate_ref[2 * pair], gate_ref[2 * pair + 1])
    out_self = totals[0][...] / totals[2][...]
    out_text = totals[1][...] / totals[3][...]
    attn_ref[...] = (out_self + gate * out_text).astype(BF)
    self_ref[...] = out_self
    text_ref[...] = out_text
    self_sum_ref[...] = totals[2][...]
    text_sum_ref[...] = totals[3][...]


def backward_kernel(
    live_ref,
    gate_ref,
    query_ref,
    grad_ref,
    self_ref,
    text_ref,
    self_sum_ref,
    text_sum_ref,
    bias_ref,
    *refs,
):
    count = (len(refs) - 3) // 3
    self_refs, text_refs = refs[:count], refs[count : 2 * count]
    set_refs = refs[2 * count : 3 * count]
    query_grad_ref, gate_grad_ref, total = refs[3 * count :]
    rows = query_ref.shape[0]
    low = lanes(rows) < HD
    pair = pl.program_id(0)
    gates = (gate_ref[2 * pair], gate_ref[2 * pair + 1])
    wide = grad_ref[...].astype(F32)
    text_dot = head_sum(wide * text_ref[...])
    gate_grad_ref[...] = jnp.broadcast_to(
        jnp.sum(text_dot, axis=0, keepdims=True), gate_grad_ref.shape
    )
    delta_self = jnp.transpose(head_sum(wide * self_ref[...]))
    delta_text = jnp.transpose(jnp.where(low, gates[0], gates[1]) * text_dot)
    log_self = jnp.transpose(jnp.log(self_sum_ref[...]))
    log_text = jnp.transpose(jnp.log(text_sum_ref[...]))
    total[...] = jnp.zeros_like(total)

    for index in range(count):

        @pl.when(live_ref[index] > 0)
        def _(index=index):
            queries = split_pair(query_ref[...] * jnp.asarray(SCALE, BF))
            grads = split_pair(grad_ref[...])
            start = 0
            for slot, source in ((0, self_refs[index]), (1, text_refs[index])):
                depth = source.shape[0] // 2
                keys, values = source[pl.ds(0, depth), :], source[pl.ds(depth, depth), :]
                grad_query, grad_key, grad_value = [], [], []
                for head in range(2):
                    row = head * HD
                    logs = (log_text if slot else log_self)[row : row + 1, :]
                    delta = (delta_text if slot else delta_self)[row : row + 1, :]
                    logits = mm(keys, queries[head], NT)
                    if slot:
                        logits = logits + bias_ref[:, index : index + 1]
                    probs = jnp.exp(logits - logs)
                    value_part = mm(probs.astype(BF), grads[head], NN)
                    grad_probs = mm(values, grads[head], NT)
                    if slot:
                        value_part = value_part * gates[head]
                        grad_probs = grad_probs * gates[head]
                    grad_logits = (probs * (grad_probs - delta)).astype(BF)
                    grad_value.append(value_part)
                    grad_key.append(mm(grad_logits, queries[head], NN))
                    grad_query.append(mm(grad_logits, keys, TN))
                total[...] += jnp.where(low, grad_query[0], grad_query[1])
                set_refs[index][pl.ds(start, depth), :] = (grad_key[0] + grad_key[1]).astype(BF)
                set_refs[index][pl.ds(start + depth, depth), :] = (
                    grad_value[0] + grad_value[1]
                ).astype(BF)
                start += 2 * depth

        @pl.when(live_ref[index] == 0)
        def _(index=index):
            set_refs[index][...] = jnp.zeros_like(set_refs[index])

    query_grad_ref[...] = total[...] * SCALE


def params(limit=40):
    return pltpu.CompilerParams(vmem_limit_bytes=limit * 2**20)


def whole(kernel, outs, cost, *args):
    shapes = [jax.ShapeDtypeStruct(shape, dtype) for shape, dtype in outs]
    return pl.pallas_call(
        kernel,
        out_shape=shapes if len(shapes) > 1 else shapes[0],
        compiler_params=params(),
        cost_estimate=pl.CostEstimate(flops=cost, bytes_accessed=2 * cost // 10, transcendentals=0),
    )(*args)


def column(rows):
    return pl.BlockSpec((rows, PAIR), lambda pair: (0, pair))


def fixed(shape):
    return pl.BlockSpec(shape, lambda pair: (0, 0))


def attend_forward(live, gates, query, bias, self_sets, text_sets):
    rows, width = query.shape
    smem = pl.BlockSpec(memory_space=pltpu.SMEM)
    keys = self_sets[0].shape[0] // 2 + text_sets[0].shape[0] // 2
    return pl.pallas_call(
        forward_kernel,
        grid=(width // PAIR,),
        in_specs=[smem, smem, column(rows), fixed(bias.shape)]
        + [column(value.shape[0]) for value in self_sets + text_sets],
        out_specs=[column(rows)] * 5,
        out_shape=[jax.ShapeDtypeStruct((rows, width), BF)]
        + [jax.ShapeDtypeStruct((rows, width), F32)] * 4,
        scratch_shapes=[pltpu.VMEM((rows, PAIR), F32)] * 4,
        compiler_params=params(),
        cost_estimate=pl.CostEstimate(
            flops=4 * 4 * rows * keys * width * 4,
            bytes_accessed=20 * rows * width * 4,
            transcendentals=4 * rows * keys * width // HD,
        ),
    )(live, gates, query, bias, *self_sets, *text_sets)


def attend_backward(live, gates, query, grad, saved, bias, self_sets, text_sets):
    rows, width = query.shape
    smem = pl.BlockSpec(memory_space=pltpu.SMEM)
    depth = self_sets[0].shape[0] + text_sets[0].shape[0]
    outs = pl.pallas_call(
        backward_kernel,
        grid=(width // PAIR,),
        in_specs=[smem, smem]
        + [column(rows)] * 6
        + [fixed(bias.shape)]
        + [column(value.shape[0]) for value in self_sets + text_sets],
        out_specs=[column(depth)] * len(self_sets) + [column(rows), column(8)],
        out_shape=[jax.ShapeDtypeStruct((depth, width), BF)] * len(self_sets)
        + [jax.ShapeDtypeStruct((rows, width), F32), jax.ShapeDtypeStruct((8, width), F32)],
        scratch_shapes=[pltpu.VMEM((rows, PAIR), F32)],
        compiler_params=params(),
        cost_estimate=pl.CostEstimate(
            flops=10 * 4 * rows * depth // 2 * width * 4,
            bytes_accessed=40 * rows * width * 4,
            transcendentals=4 * rows * depth // 2 * width // HD,
        ),
    )(live, gates, query, grad, *saved, bias, *self_sets, *text_sets)
    return outs[: len(self_sets)], outs[-2], outs[-1]


def local(
    tokens,
    caption,
    condition,
    cotangent,
    qkv_weight,
    proj_weight,
    text_weight,
    ffn_weight,
    down_weight,
    ada_weight,
    norm_gains,
    head_gains,
    ada_bias,
    cross_gate,
    group_map,
    grid_width,
    caption_len,
):
    dp_count = lax.axis_size("dp")
    mp_count = lax.axis_size("mp")
    dp_index = lax.axis_index("dp")
    mp_index = lax.axis_index("mp")
    row_count, width = tokens.shape
    seq_len = row_count * mp_count
    local_width = qkv_weight.shape[2]
    local_heads = local_width // HD
    text_len, text_dim = caption.shape[1:]
    units = ffn_weight.shape[2]
    shard = qkv_weight.shape[1]
    weight_scale = 1.0 / math.sqrt(seq_len * dp_count)
    is_odd = (dp_index % 2) == 1
    ring_pos = jnp.where(is_odd, dp_count - 1 - dp_index // 2, dp_index // 2)
    order = jnp.asarray(ring_order(dp_count) * 2, jnp.int32)
    ahead = lax.dynamic_slice_in_dim(order, ring_pos, dp_count)
    behind = lax.dynamic_slice_in_dim(order[::-1], dp_count - 1 - ring_pos, dp_count)

    half = shard // 2
    inner = jnp.arange(half, dtype=jnp.int32)
    source = jnp.concatenate(
        [
            (behind[:, None] * shard + inner[None, :]).reshape(-1),
            (ahead[:, None] * shard + half + inner[None, :]).reshape(-1),
        ]
    )
    places = (lax.broadcasted_iota(jnp.int32, (width, width), 0) == source[None, :]).astype(BF)

    qkv_shard = jnp.transpose(qkv_weight, (1, 0, 2)).reshape(shard, 3 * local_width)
    rest_shard = jnp.concatenate(
        [proj_weight.T, jnp.transpose(ffn_weight, (1, 0, 2)).reshape(shard, 2 * units), down_weight.T],
        axis=1,
    )

    cond_low = jax.nn.silu(condition).astype(BF)
    cond_all = gather_in_order(cond_low, "dp", dp_index)
    cond_mine = lax.dynamic_slice_in_dim(cond_all, dp_index * shard, shard, axis=1)
    mod_all = sum_all(mm(cond_mine, ada_weight, NN), "dp")
    bias_part = lax.dynamic_slice_in_dim(ada_bias, mp_index * width, width)
    mod_part = lax.dynamic_slice_in_dim(mod_all, dp_index, 1, axis=0) + bias_part[None, :]
    vectors = jnp.concatenate([gather_in_order(mod_part, "mp", mp_index), norm_gains], axis=0)
    vectors = exact(vectors, places.astype(F32), NN)
    scale_attn, gate_attn, scale_ffn, gate_ffn = [vectors[k] for k in range(4)]
    gains = [vectors[4 + k] for k in range(4)]

    qkv_first, qkv_second = ring_gather(qkv_shard)
    qkv_full = jnp.concatenate(qkv_first + qkv_second, axis=0)

    act_rows = mm(tokens, places, NN)
    first_in, first_pull = jax.vjp(modulate, act_rows, gains[0], scale_attn)
    first_low = rows_from_mp(first_in.astype(BF))
    qkv_pre = mm(first_low, qkv_full, NN)

    text_shard = text_weight.shape[1]
    quarter_rows = text_len // mp_count
    my_rows = lax.dynamic_slice_in_dim(caption[0], mp_index * quarter_rows, quarter_rows, axis=0)
    pieces = []
    for step in range(dp_count):
        piece = lax.dynamic_slice_in_dim(my_rows, ahead[step] * text_shard, text_shard, axis=1)
        if step:
            piece = lax.ppermute(piece, "dp", ring_pairs(dp_count, step))
        pieces.append(piece[None])
    mine = jnp.concatenate(pieces, axis=0)
    far = swap(mine, "mp", 2)
    near = swap(mine, "mp", 1)
    last = swap(far, "mp", 1)
    text_all = jnp.concatenate([mine, near, far, last], axis=1).reshape(
        dp_count * text_len, text_shard
    )
    text_matrix = jnp.transpose(text_weight, (1, 0, 2)).reshape(text_shard, 2 * local_width)
    text_part = mm(text_all, text_matrix, NN).astype(BF).reshape(dp_count, text_len, 2 * local_width)
    text_pre = jnp.concatenate(
        ring_scatter(
            lambda k: text_part[k, :, :local_width],
            lambda k: text_part[(dp_count - k) % dp_count, :, local_width:],
        ),
        axis=1,
    )

    blocks = mp_index ^ jnp.arange(mp_count, dtype=jnp.int32)
    token_ids = (blocks[:, None] * row_count + jnp.arange(row_count, dtype=jnp.int32)).reshape(-1)
    text_ids = (blocks[:, None] * quarter_rows + jnp.arange(quarter_rows, dtype=jnp.int32)).reshape(-1)
    first_slot = group_map[dp_index]
    positions = (dp_index - first_slot) * seq_len + token_ids
    quarter = HD // 4
    lane = jnp.arange(PAIR, dtype=jnp.int32)
    freqs = jnp.exp((lane % quarter).astype(F32) * (-math.log(10000.0) / quarter))
    grid = grid_width[dp_index]
    place = jnp.where((lane % HD < HD // 2)[None, :], (positions // grid)[:, None], (positions % grid)[:, None])
    angles = place.astype(F32) * freqs[None, :]
    cos = jnp.cos(angles)
    sin = jnp.sin(angles) * jnp.where((lane % (2 * quarter)) < quarter, -1.0, 1.0)[None, :]
    local_gains = lax.dynamic_slice_in_dim(head_gains, mp_index * local_width, local_width, axis=1)
    tanh_gate = jnp.tanh(lax.dynamic_slice_in_dim(cross_gate, mp_index * local_heads, local_heads))

    live, biases = [], []
    for offset in set_offsets(is_odd):
        origin = dp_index + offset
        clipped = jnp.clip(origin, 0, dp_count - 1)
        live.append((origin == clipped) & (group_map[clipped] == first_slot))
        biases.append(jnp.where(text_ids < caption_len[clipped], 0.0, NEG))
    live = jnp.stack(live).astype(jnp.int32)
    bias = jnp.stack(biases + biases[:1]).astype(F32)

    prepared = whole(
        prep_kernel,
        [((3 * seq_len, local_width), BF)],
        20 * seq_len * 3 * local_width,
        qkv_pre,
        local_gains,
        cos,
        sin,
    )
    query = prepared[:seq_len]
    self_sets = send_sets(prepared[seq_len:], is_odd)
    text_set = whole(
        text_prep_kernel,
        [((2 * text_len, local_width), BF)],
        20 * text_len * 2 * local_width,
        text_pre,
        local_gains,
    )
    text_sets = send_sets(text_set, is_odd)
    attn_low, *saved = attend_forward(live, tanh_gate, query, bias, self_sets, text_sets)

    rest_first, rest_second = ring_gather(rest_shard)
    rest = rest_first + rest_second
    cuts = (0, local_width, local_width + 2 * units, local_width + 3 * units)
    proj_full, ffn_full, down_full = [
        jnp.concatenate([piece[:, low:high] for piece in rest], axis=0)
        for low, high in zip(cuts[:-1], cuts[1:])
    ]

    attn_rows = sum_to_mp(mm(attn_low, proj_full, NT))
    middle, middle_pull = jax.vjp(gated_add, attn_rows, gains[1], gate_attn, act_rows)
    second_in, second_pull = jax.vjp(modulate, middle, gains[2], scale_ffn)
    second_low = rows_from_mp(second_in.astype(BF))
    ffn_pre = mm(second_low, ffn_full, NN)
    hidden_f, swiglu_pull = jax.vjp(swiglu, ffn_pre[:, :units], ffn_pre[:, units:])
    hidden_low = hidden_f.astype(BF)
    ffn_rows = sum_to_mp(mm(hidden_low, down_full, NT))
    result, result_pull = jax.vjp(gated_add, ffn_rows, gains[3], gate_ffn, middle)
    result = mm(result.astype(BF), places, NT).astype(BF)

    grad_out = mm(cotangent, places, NN)
    grad_ffn_rows, grad_gain_four, grad_gate_ffn, grad_middle_a = result_pull(grad_out)
    grad_ffn_all = rows_from_mp(grad_ffn_rows.astype(BF))
    grad_hidden = mm(grad_ffn_all, down_full, NN)
    grad_gate_pre, grad_up_pre = swiglu_pull(grad_hidden)
    grad_pre_low = jnp.concatenate([grad_gate_pre, grad_up_pre], axis=1).astype(BF)
    grad_second = sum_to_mp(mm(grad_pre_low, ffn_full, NT))
    grad_down = mm(grad_ffn_all, hidden_low, TN).astype(BF)
    grad_ffn = mm(second_low, grad_pre_low, TN).astype(BF)
    grad_middle_b, grad_gain_three, grad_scale_ffn = second_pull(grad_second)
    grad_attn_rows, grad_gain_two, grad_gate_attn, grad_act_a = middle_pull(
        grad_middle_a + grad_middle_b
    )
    grad_attn_all = rows_from_mp(grad_attn_rows.astype(BF))
    grad_attn_low = mm(grad_attn_all, proj_full, NN).astype(BF)
    grad_proj = mm(grad_attn_all, attn_low, TN).astype(BF)

    def chunk(values, k):
        return values[k * half : (k + 1) * half]

    def scatter(values):
        def first(k):
            return jnp.concatenate([chunk(value, k) for value in values], axis=1)

        def second(k):
            return first(dp_count + k)

        return jnp.concatenate(ring_scatter(first, second), axis=0) * weight_scale

    ffn_sum = scatter([grad_ffn, grad_down])

    grad_sets, grad_query, gate_dots = attend_backward(
        live, tanh_gate, query, grad_attn_low, saved, bias.T, self_sets, text_sets
    )
    own_set = return_sets(grad_sets, is_odd)
    grad_qkv_low, head_two = whole(
        prep_back_kernel,
        [((seq_len, 3 * local_width), BF), ((8, local_width), F32)],
        20 * seq_len * 3 * local_width,
        qkv_pre,
        local_gains,
        cos,
        sin,
        grad_query,
        own_set[: 2 * seq_len],
    )
    grad_text_low, head_one = whole(
        text_back_kernel,
        [((text_len, 2 * local_width), BF), ((8, local_width), F32)],
        20 * text_len * 2 * local_width,
        text_pre,
        local_gains,
        own_set[2 * seq_len :],
    )
    grad_qkv = mm(first_low, grad_qkv_low, TN).astype(BF)
    attn_sum = scatter([grad_qkv, grad_proj])
    grad_first = sum_to_mp(mm(grad_qkv_low, qkv_full, NT))
    grad_act_b, grad_gain_one, grad_scale_attn = first_pull(grad_first)
    grad_tokens = exact(grad_act_a + grad_act_b, places.astype(F32), NT)

    key_rows, value_rows = [grad_text_low[:, :local_width]], [grad_text_low[:, local_width:]]
    for _ in range(dp_count - 1):
        key_rows.append(lax.ppermute(key_rows[-1], "dp", ring_pairs(dp_count, 1)))
        value_rows.append(lax.ppermute(value_rows[-1], "dp", ring_pairs(dp_count, -1)))
    value_rows = value_rows[:1] + value_rows[1:][::-1]
    text_rows = jnp.concatenate(
        [jnp.concatenate(key_rows, axis=0), jnp.concatenate(value_rows, axis=0)], axis=1
    )
    grad_text = mm(text_all, text_rows, TN) * weight_scale
    caption_part = mm(text_rows, text_matrix, NT).reshape(
        dp_count, mp_count, quarter_rows, text_shard
    )
    caption_part = jnp.transpose(caption_part, (1, 0, 2, 3)).reshape(
        mp_count * dp_count * quarter_rows, text_shard
    )
    caption_mine = sum_to_mp(caption_part).astype(BF).reshape(dp_count, quarter_rows, text_shard)
    columns = jnp.zeros((quarter_rows, text_dim), BF)
    for step in range(dp_count):
        piece = caption_mine[step]
        if step:
            piece = lax.ppermute(piece, "dp", ring_pairs(dp_count, -step))
        columns = lax.dynamic_update_slice_in_dim(columns, piece, ahead[step] * text_shard, 1)
    block = text_dim // mp_count
    grad_caption = jnp.zeros((text_len, block), F32)
    for bit in range(mp_count):
        other = mp_index ^ bit
        piece = lax.dynamic_slice_in_dim(columns, other * block, block, axis=1)
        if bit:
            piece = swap(piece, "mp", bit)
        grad_caption = lax.dynamic_update_slice_in_dim(
            grad_caption, piece.astype(F32), other * quarter_rows, 0
        )

    row_grads = jnp.stack(
        [
            grad_gain_one,
            grad_gain_two,
            grad_gain_three,
            grad_gain_four,
            grad_scale_attn,
            grad_gate_attn,
            grad_scale_ffn,
            grad_gate_ffn,
        ]
    )
    row_grads = exact(row_grads, places.astype(F32), NT)
    mod_sum = sum_all(row_grads[4:], "mp")
    grad_mod_low = lax.dynamic_slice_in_dim(mod_sum, mp_index, 1, axis=0).astype(BF)
    grad_mod_all = gather_in_order(grad_mod_low, "dp", dp_index)
    grad_ada = mm(cond_mine, grad_mod_all, TN) * weight_scale
    cond_part = mm(grad_mod_all, ada_weight, NT)
    zeros = functools.partial(jnp.zeros, dtype=F32)
    cond_rows = lax.dynamic_update_slice_in_dim(
        zeros((dp_count, width)), cond_part, dp_index * shard, 1
    )
    head_local = jnp.concatenate([head_two[:2], head_one[:1]], axis=0)
    head_rows = lax.dynamic_update_slice_in_dim(
        zeros((3, width)), head_local, mp_index * local_width, 1
    )
    bias_rows = jnp.where(
        jnp.arange(mp_count)[:, None] == mp_index, grad_mod_low.astype(F32), 0.0
    )
    gate_local = gate_dots[0].reshape(local_heads, HD)[:, 0] * (1.0 - tanh_gate * tanh_gate)
    gate_row = lax.dynamic_update_slice_in_dim(
        zeros((width,)), gate_local, mp_index * local_heads, 0
    )
    small = jnp.concatenate([row_grads[:4], head_rows, bias_rows, gate_row[None], cond_rows], axis=0)
    small = sum_all(sum_all(small, "mp"), "dp")
    cond_width = width // mp_count
    cond_sum = lax.dynamic_slice(small[12:], (dp_index, mp_index * cond_width), (1, cond_width))
    cond_cols = lax.dynamic_slice_in_dim(condition, mp_index * cond_width, cond_width, axis=1)
    silu_vals, silu_pull = jax.vjp(jax.nn.silu, cond_cols)
    grad_condition = silu_pull(cond_sum)[0] * (1.0 / math.sqrt(seq_len))
    scaled = small[:12] * weight_scale

    def parted(values, parts):
        return jnp.transpose(values.reshape(values.shape[0], parts, -1), (1, 0, 2))

    return (
        result,
        grad_tokens,
        grad_caption[None],
        grad_condition,
        parted(attn_sum[:, : 3 * local_width], 3),
        attn_sum[:, 3 * local_width :].T,
        parted(grad_text, 2),
        parted(ffn_sum[:, : 2 * units], 2),
        ffn_sum[:, 2 * units :].T,
        grad_ada,
        scaled[:4],
        scaled[4:7],
        scaled[7:11].reshape(-1),
        scaled[11, :HEADS],
    )


def solution(mesh):
    return jax.shard_map(
        local,
        mesh=mesh,
        in_specs=(
            P(("dp", "mp"), None),
            P("dp", None, None),
            P("dp", None),
            P(("dp", "mp"), None),
            P(None, "dp", "mp"),
            P("mp", "dp"),
            P(None, "dp", "mp"),
            P(None, "dp", "mp"),
            P("mp", "dp"),
            P("dp", "mp"),
            P(),
            P(),
            P(),
            P(),
            P(),
            P(),
            P(),
        ),
        out_specs=(
            P(("dp", "mp"), None),
            P(("dp", "mp"), None),
            P("dp", None, "mp"),
            P("dp", "mp"),
            P(None, "dp", "mp"),
            P("mp", "dp"),
            P(None, "dp", "mp"),
            P(None, "dp", "mp"),
            P("mp", "dp"),
            P("dp", "mp"),
            P(),
            P(),
            P(),
            P(),
        ),
        check_vma=False,
    )
```

time: 1950 us -> 905 us (0.46)
  waiting for transfers between devices: 1260 us -> 421 us
  matrix products: 190 us -> 65.3 us
  other arithmetic: 110 us -> 47.9 us
  Pallas kernels: 0 us -> 58.5 us
  starting transfers between devices: 246 us -> 192 us
    reduce_scatter x9 -> x0, waiting for transfers between devices: 468 us -> none  [the longest x1 117 us: local(): lax.psum_scatter((grad_text * weight_scale).astype(jnp.bfloat16), 'dp', s...]
    all_gather x10 -> x0, waiting for transfers between devices: 441 us -> none  [the longest x1 106 us: local(): lax.all_gather(text_weight, 'dp', axis=1, tiled=True)]
    ppermute x48 -> x167, waiting for transfers between devices: 32.2 us -> 421 us  [the longest x42 206 us: ring_scatter(): moved = lax.ppermute(total.astype(BF), 'dp', ring_pairs(count, step))]
    unnamed x26 -> x0, waiting for transfers between devices: 198 us -> none
    dot_general x73 -> x24, matrix products: 190 us -> 65.3 us  [the longest x21 50.3 us: mm(): return lax.dot_general(left, right, dims, preferred_element_type=F32)]
    psum x1 -> x0, waiting for transfers between devices: 124 us -> none  [local(): lax.psum((norm_grad, head_grad, bias_grad, gate_grad), ('dp', 'mp'))]
    pallas_call x0 -> x6, Pallas kernels: none -> 58.5 us  [the longest x1 36.8 us: attend_backward(): pl.pallas_call(backward_kernel, grid=(width // PAIR,), in_specs=[smem, sm...]
    ppermute x48 -> x167, starting transfers between devices: 244 us -> 192 us  [the longest x57 51.6 us: swap(): return lax.ppermute(value, axis, [(i, i ^ bit) for i in range(count)])]
  transfers between devices with their start and end apart: 71 -> 167, of which waited for: 27 -> 72; matrix products, arithmetic and copies ran while one was open for 16% -> 18% of each run, Pallas kernels for 0% -> 6%
where the time goes in v1:
time: 905 us; the launch traced here: 894 us
  waiting for transfers between devices  421 us (47%)
  starting transfers between devices  192 us (21%)
  local copies, waits for them, and re-layouts  87.9 us (10%)
  matrix products  65.3 us (7%)
  Pallas kernels  58.5 us (6%)
  other arithmetic  47.9 us (5%)
  between operations  21.6 us (2%)
    ppermute x42, waiting for transfers between devices, ring_scatter(): moved = lax.ppermute(total.astype(BF), 'dp', ring_pairs(count, step))  206 us
    ppermute x57, waiting for transfers between devices, swap(): return lax.ppermute(value, axis, [(i, i ^ bit) for i in range(count)])  100 us
    ppermute x57, starting transfers between devices, swap(): return lax.ppermute(value, axis, [(i, i ^ bit) for i in range(count)])  51.6 us
    dot_general x21, matrix products, mm(): return lax.dot_general(left, right, dims, preferred_element_type=F32)  50.3 us
    unnamed x455, local copies, waits for them, and re-layouts  49.3 us
    ppermute x42, starting transfers between devices, ring_scatter(): moved = lax.ppermute(total.astype(BF), 'dp', ring_pairs(count, step))  47.6 us
    pallas_call x1, Pallas kernels, attend_backward(): pl.pallas_call(backward_kernel, grid=(width // PAIR,), in_specs=[smem, sm...  36.8 us
    ppermute x14, waiting for transfers between devices, ring_gather(): first.append(lax.ppermute(first[-1], 'dp', ring_pairs(count, 1)))  28.2 us
  transfers between devices with their start and end apart: 167, of which 72 were waited for; matrix products, arithmetic and copies ran while one was open for 18% of the time, Pallas kernels for 6%

profile of v1, /device:TPU:0, one launch (start us, length us, event | category | flops | bytes accessed | tf_op | source)
XLA Modules:
  0.0 894.1 jit_solution(11553953469375519377)
XLA Ops:
  117.2 6.3 collective-permute-done.14
  125.8 4.9 collective-permute-done.21
  134.9 6.8 collective-permute-done.15
  164.0 13.3 %collective-permute-done.24 = bf16[96,1152]{1,0:T(8,128)(2,1)S(1)} collective-permute-done((bf16[96,1152]{1,0:T(8,128)(2,1)S(1)}, bf16[96,1152]{1,0:T(8,128)(2,1)S(1)}, u32[]{:S(2)}, u32[]{:S(2)}) %collective-permute-start.24) | collective-permute-done | bytes 221216 | tf_op jit(solution)/shard_map/ppermute | solution.py:49
  206.3 11.5 %collective-permute-done.45 = bf16[256,384]{1,0:T(8,128)(2,1)S(1)} collective-permute-done((bf16[256,384]{1,0:T(8,128)(2,1)S(1)}, bf16[256,384]{1,0:T(8,128)(2,1)S(1)}, u32[]{:S(2)}, u32[]{:S(2)}) %collective-permute-start.45) | collective-permute-done | bytes 196640 | tf_op jit(solution)/shard_map/ppermute | solution.py:59
  217.8 5.3 collective-permute-done.52
  225.4 5.7 collective-permute-done.46
  235.4 28.2 %collective-permute-done.47 = bf16[256,384]{1,0:T(8,128)(2,1)S(1)} collective-permute-done((bf16[256,384]{1,0:T(8,128)(2,1)S(1)}, bf16[256,384]{1,0:T(8,128)(2,1)S(1)}, u32[]{:S(2)}, u32[]{:S(2)}) %collective-permute-start.47) | collective-permute-done | bytes 196640 | tf_op jit(solution)/shard_map/ppermute | solution.py:59
  284.7 7.9 collective-permute-done.55.refs_8_
  293.8 15.7 %collective-permute-done.58.refs_11_ = bf16[512,384]{1,0:T(8,128)(2,1)S(1)} collective-permute-done((bf16[512,384]{1,0:T(8,128)(2,1)S(1)}, bf16[512,384]{1,0:T(8,128)(2,1)S(1)}, u32[]{:S(2)}, u32[]{:S(2)}) %collective-permute-start.58) | collective-permute-done | bytes 393248 | tf_op jit(solution)/shard_map/ppermute | solution.py:67
  318.6 18.7 %collective-permute-done.60.refs_13_ = bf16[512,384]{1,0:T(8,128)(2,1)S(1)} collective-permute-done((bf16[512,384]{1,0:T(8,128)(2,1)S(1)}, bf16[512,384]{1,0:T(8,128)(2,1)S(1)}, u32[]{:S(2)}, u32[]{:S(2)}) %collective-permute-start.60) | collective-permute-done | bytes 393248 | tf_op jit(solution)/shard_map/ppermute | solution.py:123
  337.3 16.1 %shard_map.283 = (bf16[512,384]{1,0:T(8,128)(2,1)S(1)}, f32[512,384]{1,0:T(8,128)S(1)}, f32[512,384]{1,0:T(8,128)S(1)}, f32[512,384]{1,0:T(8,128)S(1)}, f32[512,384]{1,0:T(8,128)S(1)}) custom-call(s32[7]{0:T(128)S(1)} %convert_element_type.599.live_ref, f32[6]{0:T(128)S(1)} %dynamic-slice_tanh_fusion.gate_ref, bf16[512,384]{1,0:T(8,128)(2,1)S(1)} %slice.869.query_ref, ...), custom_call_target="tpu_custom_call" | custom-call | flops 9663676416 | bytes 15728640 | tf_op jit(solution)/shard_map/pallas_call | solution.py:397
  358.1 6.9 collective-permute-done.67
  377.4 9.2 %collective-permute-done.77 = bf16[128,1536]{1,0:T(8,128)(2,1)S(1)} collective-permute-done((bf16[128,1536]{1,0:T(8,128)(2,1)S(1)}, bf16[128,1536]{1,0:T(8,128)(2,1)S(1)}, u32[]{:S(2)}, u32[]{:S(2)}) %collective-permute-start.77) | collective-permute-done | bytes 393248 | tf_op jit(solution)/shard_map/ppermute | solution.py:67
  389.0 8.1 collective-permute-done.79
  411.1 9.8 %collective-permute-done.83 = bf16[128,1536]{1,0:T(8,128)(2,1)S(1)} collective-permute-done((bf16[128,1536]{1,0:T(8,128)(2,1)S(1)}, bf16[128,1536]{1,0:T(8,128)(2,1)S(1)}, u32[]{:S(2)}, u32[]{:S(2)}) %collective-permute-start.83) | collective-permute-done | bytes 393248 | tf_op jit(solution)/shard_map/ppermute | solution.py:67
  427.7 8.5 collective-permute-done.85
  438.0 4.9 fusion.14
  442.9 4.8 fusion.21
  466.0 12.0 %collective-permute-done.153 = bf16[96,3072]{1,0:T(8,128)(2,1)S(1)} collective-permute-done((bf16[96,3072]{1,0:T(8,128)(2,1)S(1)}, bf16[96,3072]{1,0:T(8,128)(2,1)S(1)}, u32[]{:S(2)}, u32[]{:S(2)}) %collective-permute-start.153) | collective-permute-done | bytes 589856 | tf_op jit(solution)/shard_map/ppermute | solution.py:59
  487.2 5.9 collective-permute-done.154
  499.2 36.8 %shard_map.284 = (bf16[1536,384]{1,0:T(8,128)(2,1)S(1)}, bf16[1536,384]{1,0:T(8,128)(2,1)}, bf16[1536,384]{1,0:T(8,128)(2,1)}, bf16[1536,384]{1,0:T(8,128)(2,1)}...) custom-call(s32[7]{0:T(128)S(1)} %convert_element_type.599.live_ref,, ...), custom_call_target="tpu_custom_call" | custom-call | flops 24159191040 | bytes 31457280 | tf_op jit(solution)/shard_map/pallas_call | solution.py:419
  553.5 25.3 %collective-permute-done.156 = bf16[96,3072]{1,0:T(8,128)(2,1)S(1)} collective-permute-done((bf16[96,3072]{1,0:T(8,128)(2,1)S(1)}, bf16[96,3072]{1,0:T(8,128)(2,1)S(1)}, u32[]{:S(2)}, u32[]{:S(2)}) %collective-permute-start.156) | collective-permute-done | bytes 589856 | tf_op jit(solution)/shard_map/ppermute | solution.py:59
  590.0 7.0 collective-permute-done.157
  600.6 58.5 %collective-permute-done.158 = bf16[96,3072]{1,0:T(8,128)(2,1)S(1)} collective-permute-done((bf16[96,3072]{1,0:T(8,128)(2,1)S(1)}, bf16[96,3072]{1,0:T(8,128)(2,1)S(1)}, u32[]{:S(2)}, u32[]{:S(2)}) %collective-permute-start.158) | collective-permute-done | bytes 589856 | tf_op jit(solution)/shard_map/ppermute | solution.py:59
  678.9 20.3 %collective-permute-done.97 = bf16[1536,384]{1,0:T(8,128)(2,1)S(1)} collective-permute-done((bf16[1536,384]{1,0:T(8,128)(2,1)S(1)}, bf16[1536,384]{1,0:T(8,128)(2,1)S(1)}, u32[]{:S(2)}, u32[]{:S(2)}) %collective-permute-start.97) | collective-permute-done | bytes 1179680 | tf_op jit(solution)/shard_map/ppermute | solution.py:146
  717.7 6.4 collective-permute-done.139
  749.0 5.1 fusion
  768.1 7.0 fusion.1
  809.8 4.7 collective-permute-done.137
  840.5 5.4 collective-permute-done.144
  857.9 6.5 collective-permute-done.118
  (1002 shorter events, 479.4 us)
Async XLA Ops:
  9.8 52.0 %collective-permute-start.31 = (bf16[64,512]{1,0:T(8,128)(2,1)}, bf16[64,512]{1,0:T(8,128)(2,1)}, u32[]{:S(2)}, u32[]{:S(2)}) collective-permute-start(bf16[64,512]{1,0:T(8,128)(2,1)} %get-tuple-element.184), channel_id=1, source_target_pairs={{0,8},{8,16},{16,24},{24,28},{28,20},{20,12},{12,4},{4,0},{1,9},{9... | collective-permute-start | bytes 196616 | tf_op jit(solution)/shard_map/ppermute | solution.py:519
  12.9 51.0 %collective-permute-start.32 = (bf16[64,512]{1,0:T(8,128)(2,1)}, bf16[64,512]{1,0:T(8,128)(2,1)}, u32[]{:S(2)}, u32[]{:S(2)}) collective-permute-start(bf16[64,512]{1,0:T(8,128)(2,1)} %get-tuple-element.183), channel_id=1, source_target_pairs={{0,16},{8,24},{16,28},{24,20},{28,12},{20,4},{12,0},{4,8},{1,17},{... | collective-permute-start | bytes 196616 | tf_op jit(solution)/shard_map/ppermute | solution.py:519
  15.4 52.1 %collective-permute-start.33 = (bf16[64,512]{1,0:T(8,128)(2,1)}, bf16[64,512]{1,0:T(8,128)(2,1)S(1)}, u32[]{:S(2)}, u32[]{:S(2)}) collective-permute-start(bf16[64,512]{1,0:T(8,128)(2,1)} %get-tuple-element.182), channel_id=1, source_target_pairs={{0,24},{8,28},{16,20},{24,12},{28,4},{20,0},{12,8},{4,16},{1,25},{... | collective-permute-start | bytes 196616 | tf_op jit(solution)/shard_map/ppermute | solution.py:519
  20.9 75.5 %collective-permute-start.11 = (bf16[96,1152]{1,0:T(8,128)(2,1)}, bf16[96,1152]{1,0:T(8,128)(2,1)}, u32[]{:S(2)}, u32[]{:S(2)}) collective-permute-start(bf16[96,1152]{1,0:T(8,128)(2,1)} %bitcast.119), channel_id=1, source_target_pairs={{0,8},{8,16},{16,24},{24,28},{28,20},{20,12},{12,4},{4,0},{1,9},{9... | collective-permute-start | bytes 663560 | tf_op jit(solution)/shard_map/ppermute | solution.py:48
  87.3 66.9 %collective-permute-start.68 = (bf16[96,3456]{1,0:T(8,128)(2,1)}, bf16[96,3456]{1,0:T(8,128)(2,1)S(1)}, u32[]{:S(2)}, u32[]{:S(2)}) collective-permute-start(bf16[96,3456]{1,0:T(8,128)(2,1)} %get-tuple-element.195), channel_id=1, source_target_pairs={{0,4},{8,0},{16,8},{24,16},{28,24},{20,28},{12,20},{4,12},{1,5},{9... | collective-permute-start | bytes 1990664 | tf_op jit(solution)/shard_map/ppermute | solution.py:49
  116.3 34.1 %collective-permute-start.62 = (bf16[96,3456]{1,0:T(8,128)(2,1)S(1)}, bf16[96,3456]{1,0:T(8,128)(2,1)S(1)}, u32[]{:S(2)}, u32[]{:S(2)}) collective-permute-start(bf16[96,3456]{1,0:T(8,128)(2,1)S(1)} %collective-permute-done.61), channel_id=1, source_target_pairs={{0,8},{8,16},{16,24},{24,28},{28,20},{20,12},{12,4},{4,0},{1,9},{9... | collective-permute-start | bytes 1990664 | tf_op jit(solution)/shard_map/ppermute | solution.py:48
  154.1 32.2 %collective-permute-start.8 = (bf16[128,1536]{1,0:T(8,128)(2,1)S(1)}, bf16[128,1536]{1,0:T(8,128)(2,1)S(1)}, u32[]{:S(2)}, u32[]{:S(2)}) collective-permute-start(bf16[128,1536]{1,0:T(8,128)(2,1)S(1)} %multiply_convert_fusion.3), channel_id=1, source_target_pairs={{0,1},{1,0},{2,3},{3,2},{4,5},{5,4},{6,7},{7,6},{8,9},{9,8},{10,11... | collective-permute-start | bytes 1179656 | tf_op jit(solution)/shard_map/ppermute | solution.py:67
  154.1 33.2 %collective-permute-start.10 = (bf16[128,1536]{1,0:T(8,128)(2,1)S(1)}, bf16[128,1536]{1,0:T(8,128)(2,1)S(1)}, u32[]{:S(2)}, u32[]{:S(2)}) collective-permute-start(bf16[128,1536]{1,0:T(8,128)(2,1)S(1)} %collective-permute-done.9), channel_id=1, source_target_pairs={{0,1},{1,0},{2,3},{3,2},{4,5},{5,4},{6,7},{7,6},{8,9},{9,8},{10,11... | collective-permute-start | bytes 1179656 | tf_op jit(solution)/shard_map/ppermute | solution.py:67
  179.5 45.8 %collective-permute-start.70 = (bf16[96,3456]{1,0:T(8,128)(2,1)S(1)}, bf16[96,3456]{1,0:T(8,128)(2,1)S(1)}, u32[]{:S(2)}, u32[]{:S(2)}) collective-permute-start(bf16[96,3456]{1,0:T(8,128)(2,1)S(1)} %collective-permute-done.69), channel_id=1, source_target_pairs={{0,4},{8,0},{16,8},{24,16},{28,24},{20,28},{12,20},{4,12},{1,5},{9... | collective-permute-start | bytes 1990664 | tf_op jit(solution)/shard_map/ppermute | solution.py:49
  191.7 41.5 %collective-permute-start.26 = (bf16[1024,384]{1,0:T(8,128)(2,1)S(1)}, bf16[1024,384]{1,0:T(8,128)(2,1)S(1)}, u32[]{:S(2)}, u32[]{:S(2)}) collective-permute-start(bf16[1024,384]{1,0:T(8,128)(2,1)S(1)} %slice.870.refs_0_), channel_id=1, source_target_pairs={{0,8},{4,12},{8,16},{12,20},{16,24},{20,28},{1,9},{5,13},{9,17},{1... | collective-permute-start | bytes 2359304 | tf_op jit(solution)/shard_map/ppermute | solution.py:119
  199.1 35.8 %collective-permute-start.27 = (bf16[1024,384]{1,0:T(8,128)(2,1)S(1)}, bf16[1024,384]{1,0:T(8,128)(2,1)S(1)}, u32[]{:S(2)}, u32[]{:S(2)}) collective-permute-start(bf16[1024,384]{1,0:T(8,128)(2,1)S(1)} %slice.870.refs_0_), channel_id=1, source_target_pairs={{8,0},{12,4},{16,8},{20,12},{24,16},{28,20},{9,1},{13,5},{17,9},{2... | collective-permute-start | bytes 2359304 | tf_op jit(solution)/shard_map/ppermute | solution.py:120
  225.3 53.0 %collective-permute-start.25 = (bf16[1024,384]{1,0:T(8,128)(2,1)S(1)}, bf16[1024,384]{1,0:T(8,128)(2,1)S(1)}, u32[]{:S(2)}, u32[]{:S(2)}) collective-permute-start(bf16[1024,384]{1,0:T(8,128)(2,1)S(1)} %slice.870.refs_0_), channel_id=1, source_target_pairs={{0,4},{4,0},{8,12},{12,8},{16,20},{20,16},{24,28},{28,24},{1,5},{5... | collective-permute-start | bytes 2359304 | tf_op jit(solution)/shard_map/ppermute | solution.py:67
  231.1 35.0 %collective-permute-start.64 = (bf16[96,3456]{1,0:T(8,128)(2,1)S(1)}, bf16[96,3456]{1,0:T(8,128)(2,1)S(1)}, u32[]{:S(2)}, u32[]{:S(2)}) collective-permute-start(bf16[96,3456]{1,0:T(8,128)(2,1)S(1)} %collective-permute-done.63), channel_id=1, source_target_pairs={{0,8},{8,16},{16,24},{24,28},{28,20},{20,12},{12,4},{4,0},{1,9},{9... | collective-permute-start | bytes 1990664 | tf_op jit(solution)/shard_map/ppermute | solution.py:48
  232.6 50.8 %collective-permute-start.71 = (bf16[96,3456]{1,0:T(8,128)(2,1)S(1)}, bf16[96,3456]{1,0:T(8,128)(2,1)S(1)}, u32[]{:S(2)}, u32[]{:S(2)}) collective-permute-start(bf16[96,3456]{1,0:T(8,128)(2,1)S(1)} %collective-permute-done.70), channel_id=1, source_target_pairs={{0,4},{8,0},{16,8},{24,16},{28,24},{20,28},{12,20},{4,12},{1,5},{9... | collective-permute-start | bytes 1990664 | tf_op jit(solution)/shard_map/ppermute | solution.py:49
  275.8 35.1 %collective-permute-start.65 = (bf16[96,3456]{1,0:T(8,128)(2,1)S(1)}, bf16[96,3456]{1,0:T(8,128)(2,1)S(1)}, u32[]{:S(2)}, u32[]{:S(2)}) collective-permute-start(bf16[96,3456]{1,0:T(8,128)(2,1)S(1)} %collective-permute-done.64), channel_id=1, source_target_pairs={{0,8},{8,16},{16,24},{24,28},{28,20},{20,12},{12,4},{4,0},{1,9},{9... | collective-permute-start | bytes 1990664 | tf_op jit(solution)/shard_map/ppermute | solution.py:48
  313.7 39.8 %collective-permute-start.66 = (bf16[96,3456]{1,0:T(8,128)(2,1)S(1)}, bf16[96,3456]{1,0:T(8,128)(2,1)S(1)}, u32[]{:S(2)}, u32[]{:S(2)}) collective-permute-start(bf16[96,3456]{1,0:T(8,128)(2,1)S(1)} %collective-permute-done.65), channel_id=1, source_target_pairs={{0,8},{8,16},{16,24},{24,28},{28,20},{20,12},{12,4},{4,0},{1,9},{9... | collective-permute-start | bytes 1990664 | tf_op jit(solution)/shard_map/ppermute | solution.py:48
  317.3 38.8 %collective-permute-start.73 = (bf16[96,3456]{1,0:T(8,128)(2,1)S(1)}, bf16[96,3456]{1,0:T(8,128)(2,1)S(1)}, u32[]{:S(2)}, u32[]{:S(2)}) collective-permute-start(bf16[96,3456]{1,0:T(8,128)(2,1)S(1)} %collective-permute-done.72), channel_id=1, source_target_pairs={{0,4},{8,0},{16,8},{24,16},{28,24},{20,28},{12,20},{4,12},{1,5},{9... | collective-permute-start | bytes 1990664 | tf_op jit(solution)/shard_map/ppermute | solution.py:49
  494.0 52.2 %collective-permute-start.155 = (bf16[96,3072]{1,0:T(8,128)(2,1)}, bf16[96,3072]{1,0:T(8,128)(2,1)}, u32[]{:S(2)}, u32[]{:S(2)}) collective-permute-start(bf16[96,3072]{1,0:T(8,128)(2,1)} %add_convert_fusion.12), channel_id=1, source_target_pairs={{0,8},{8,16},{16,24},{24,28},{28,20},{20,12},{12,4},{4,0},{1,9},{9... | collective-permute-start | bytes 1769480 | tf_op jit(solution)/shard_map/ppermute | solution.py:59
  495.7 55.0 %collective-permute-start.162 = (bf16[96,3072]{1,0:T(8,128)(2,1)}, bf16[96,3072]{1,0:T(8,128)(2,1)}, u32[]{:S(2)}, u32[]{:S(2)}) collective-permute-start(bf16[96,3072]{1,0:T(8,128)(2,1)} %add_convert_fusion.6), channel_id=1, source_target_pairs={{0,4},{8,0},{16,8},{24,16},{28,24},{20,28},{12,20},{4,12},{1,5},{9... | collective-permute-start | bytes 1769480 | tf_op jit(solution)/shard_map/ppermute | solution.py:59
  537.9 46.2 %collective-permute-start.93 = (bf16[1536,384]{1,0:T(8,128)(2,1)}, bf16[1536,384]{1,0:T(8,128)(2,1)}, u32[]{:S(2)}, u32[]{:S(2)}) collective-permute-start(bf16[1536,384]{1,0:T(8,128)(2,1)} %get-tuple-element.40), channel_id=1, source_target_pairs={{0,8},{8,16},{16,24},{12,4},{20,12},{28,20},{1,9},{9,17},{17,25},{... | collective-permute-start | bytes 3538952 | tf_op jit(solution)/shard_map/ppermute | solution.py:137
  541.1 47.0 %collective-permute-start.95 = (bf16[1536,384]{1,0:T(8,128)(2,1)}, bf16[1536,384]{1,0:T(8,128)(2,1)}, u32[]{:S(2)}, u32[]{:S(2)}) collective-permute-start(bf16[1536,384]{1,0:T(8,128)(2,1)} %get-tuple-element.43), channel_id=1, source_target_pairs={{8,0},{16,8},{24,16},{4,12},{12,20},{20,28},{9,1},{17,9},{25,17},{... | collective-permute-start | bytes 3538952 | tf_op jit(solution)/shard_map/ppermute | solution.py:134
  551.9 32.0 %collective-permute-start.163 = (bf16[96,3072]{1,0:T(8,128)(2,1)S(1)}, bf16[96,3072]{1,0:T(8,128)(2,1)S(1)}, u32[]{:S(2)}, u32[]{:S(2)}) collective-permute-start(bf16[96,3072]{1,0:T(8,128)(2,1)S(1)} %add_convert_fusion.5), channel_id=1, source_target_pairs={{0,4},{8,0},{16,8},{24,16},{28,24},{20,28},{12,20},{4,12},{1,5},{9... | collective-permute-start | bytes 1769480 | tf_op jit(solution)/shard_map/ppermute | solution.py:59
  585.9 93.0 %collective-permute-start.94 = (bf16[1536,384]{1,0:T(8,128)(2,1)S(1)}, bf16[1536,384]{1,0:T(8,128)(2,1)S(1)}, u32[]{:S(2)}, u32[]{:S(2)}) collective-permute-start(bf16[1536,384]{1,0:T(8,128)(2,1)S(1)} %add_convert_fusion.1), channel_id=1, source_target_pairs={{0,4},{4,0},{8,12},{12,8},{16,20},{20,16},{24,28},{28,24},{1,5},{5... | collective-permute-start | bytes 3538952 | tf_op jit(solution)/shard_map/ppermute | solution.py:67
  589.8 72.6 %collective-permute-start.96 = (bf16[1536,384]{1,0:T(8,128)(2,1)S(1)}, bf16[1536,384]{1,0:T(8,128)(2,1)S(1)}, u32[]{:S(2)}, u32[]{:S(2)}) collective-permute-start(bf16[1536,384]{1,0:T(8,128)(2,1)S(1)} %add_convert_fusion), channel_id=1, source_target_pairs={{0,4},{4,0},{8,12},{12,8},{16,20},{20,16},{24,28},{28,24},{1,5},{5... | collective-permute-start | bytes 3538952 | tf_op jit(solution)/shard_map/ppermute | solution.py:67
  597.1 62.0 %collective-permute-start.158 = (bf16[96,3072]{1,0:T(8,128)(2,1)S(1)}, bf16[96,3072]{1,0:T(8,128)(2,1)S(1)}, u32[]{:S(2)}, u32[]{:S(2)}) collective-permute-start(bf16[96,3072]{1,0:T(8,128)(2,1)S(1)} %add_convert_fusion.9), channel_id=1, source_target_pairs={{0,8},{8,16},{16,24},{24,28},{28,20},{20,12},{12,4},{4,0},{1,9},{9... | collective-permute-start | bytes 1769480 | tf_op jit(solution)/shard_map/ppermute | solution.py:59
  598.9 60.8 %collective-permute-start.165 = (bf16[96,3072]{1,0:T(8,128)(2,1)S(1)}, bf16[96,3072]{1,0:T(8,128)(2,1)S(1)}, u32[]{:S(2)}, u32[]{:S(2)}) collective-permute-start(bf16[96,3072]{1,0:T(8,128)(2,1)S(1)} %add_convert_fusion.3), channel_id=1, source_target_pairs={{0,4},{8,0},{16,8},{24,16},{28,24},{20,28},{12,20},{4,12},{1,5},{9... | collective-permute-start | bytes 1769480 | tf_op jit(solution)/shard_map/ppermute | solution.py:59
  663.2 36.0 %collective-permute-start.97 = (bf16[1536,384]{1,0:T(8,128)(2,1)S(1)}, bf16[1536,384]{1,0:T(8,128)(2,1)S(1)}, u32[]{:S(2)}, u32[]{:S(2)}) collective-permute-start(bf16[1536,384]{1,0:T(8,128)(2,1)S(1)} %get-tuple-element.213), channel_id=1, source_target_pairs={{8,0},{12,4},{16,8},{20,12},{24,16},{28,20},{9,1},{13,5},{17,9},{2... | collective-permute-start | bytes 3538952 | tf_op jit(solution)/shard_map/ppermute | solution.py:146
  664.6 34.6 %collective-permute-start.98 = (bf16[1536,384]{1,0:T(8,128)(2,1)S(1)}, bf16[1536,384]{1,0:T(8,128)(2,1)S(1)}, u32[]{:S(2)}, u32[]{:S(2)}) collective-permute-start(bf16[1536,384]{1,0:T(8,128)(2,1)S(1)} %get-tuple-element.214), channel_id=1, source_target_pairs={{0,8},{4,12},{8,16},{12,20},{16,24},{20,28},{1,9},{5,13},{9,17},{1... | collective-permute-start | bytes 3538952 | tf_op jit(solution)/shard_map/ppermute | solution.py:147
  706.2 37.3 %collective-permute-start.99 = (bf16[128,1536]{1,0:T(8,128)(2,1)S(1)}, bf16[128,1536]{1,0:T(8,128)(2,1)S(1)}, u32[]{:S(2)}, u32[]{:S(2)}) collective-permute-start(bf16[128,1536]{1,0:T(8,128)(2,1)S(1)} %get-tuple-element.187), channel_id=1, source_target_pairs={{0,1},{1,0},{2,3},{3,2},{4,5},{5,4},{6,7},{7,6},{8,9},{9,8},{10,11... | collective-permute-start | bytes 1179656 | tf_op jit(solution)/shard_map/ppermute | solution.py:67
  743.5 41.7 %collective-permute-start.141 = (bf16[96,1536]{1,0:T(8,128)(2,1)}, bf16[96,1536]{1,0:T(8,128)(2,1)}, u32[]{:S(2)}, u32[]{:S(2)}) collective-permute-start(bf16[96,1536]{1,0:T(8,128)(2,1)} %add_convert_fusion.25), channel_id=1, source_target_pairs={{0,8},{8,16},{16,24},{24,28},{28,20},{20,12},{12,4},{4,0},{1,9},{9... | collective-permute-start | bytes 884744 | tf_op jit(solution)/shard_map/ppermute | solution.py:59
  756.0 35.2 %collective-permute-start.148 = (bf16[96,1536]{1,0:T(8,128)(2,1)}, bf16[96,1536]{1,0:T(8,128)(2,1)}, u32[]{:S(2)}, u32[]{:S(2)}) collective-permute-start(bf16[96,1536]{1,0:T(8,128)(2,1)} %add_convert_fusion.19), channel_id=1, source_target_pairs={{0,4},{8,0},{16,8},{24,16},{28,24},{20,28},{12,20},{4,12},{1,5},{9... | collective-permute-start | bytes 884744 | tf_op jit(solution)/shard_map/ppermute | solution.py:59
  756.4 32.5 %collective-permute-start.106 = (bf16[256,384]{1,0:T(8,128)(2,1)}, bf16[256,384]{1,0:T(8,128)(2,1)}, u32[]{:S(2)}, u32[]{:S(2)}) collective-permute-start(bf16[256,384]{1,0:T(8,128)(2,1)} %collective-permute-done.105), channel_id=1, source_target_pairs={{0,8},{8,16},{16,24},{24,28},{28,20},{20,12},{12,4},{4,0},{1,9},{9... | collective-permute-start | bytes 589832 | tf_op jit(solution)/shard_map/ppermute | solution.py:665
  (321 other events, 5508.8 us)

commit v2 on v1

v2 whole, which is shorter than its diff:
```python
import functools
import math

import jax
import jax.numpy as jnp
from jax import lax
from jax.experimental import pallas as pl
from jax.experimental.pallas import tpu as pltpu
from jax.sharding import PartitionSpec as P

HEADS = 24
HD = 64
PAIR = 2 * HD
NEAR_PARTS = 3
EPS = 1e-06
NEG = -1e30
SCALE = HD ** (-0.5)
BF = jnp.bfloat16
F32 = jnp.float32
NN = (((1,), (0,)), ((), ()))
NT = (((1,), (1,)), ((), ()))
TN = (((0,), (0,)), ((), ()))


def mm(left, right, dims):
    return lax.dot_general(left, right, dims, preferred_element_type=F32)


def swap(value, axis, bit):
    count = lax.axis_size(axis)
    return lax.ppermute(value, axis, [(i, i ^ bit) for i in range(count)])


def all_bits(count):
    return [1 << k for k in range(count.bit_length() - 1)]


def after(value, *others):
    return lax.optimization_barrier((value,) + others)[0]


class Chain:
    def __init__(self, steps):
        self.steps, self.result = steps, None
        self.advance(None)

    def advance(self, arrived):
        try:
            self.wanted = self.steps.send(arrived)
        except StopIteration as end:
            self.wanted, self.result = None, end.value


class Links:
    def __init__(self):
        self.last = ()

    def stage(self, *chains, work=None):
        active = [chain for chain in chains if chain.wanted is not None]
        wanted = [item for chain in active for item in chain.wanted]
        values = [value for value, _, _ in wanted]
        if self.last and values:
            values = lax.optimization_barrier(tuple(values) + self.last)[: len(values)]
        moved = [
            lax.ppermute(value, axis, pairs) for value, (_, axis, pairs) in zip(values, wanted)
        ]
        made = work(lambda value: after(value, *self.last)) if work else ()
        moved, made = lax.optimization_barrier((moved, made))
        self.last = tuple(moved[:1]) or tuple(jax.tree.leaves(made)[:1])
        for chain in active:
            count = len(chain.wanted)
            chain.advance(moved[:count])
            moved = moved[count:]
        return made

    def finish_only(self, chain, others):
        while chain.wanted is not None:
            self.stage(chain, *others)

    def finish(self, *chains):
        while any(chain.wanted is not None for chain in chains):
            self.stage(*chains)


def swap_pairs(axis, bit):
    return [(i, i ^ bit) for i in range(lax.axis_size(axis))]


def crossed_bits():
    bits = all_bits(lax.axis_size("dp"))
    return bits, bits[1::-1] + bits[2:]


def bit_axis(bits, bit):
    return sum(other > bit for other in bits)


def in_order(high, own, other, axis):
    return jnp.stack([jnp.where(high, other, own), jnp.where(high, own, other)], axis=axis)


def halves(high, value, axis):
    zero, one = [lax.index_in_dim(value, k, axis, keepdims=False) for k in range(2)]
    return jnp.where(high, zero, one), jnp.where(high, one, zero)


def gather_blocks(pair, index):
    orders = [bits[::-1] for bits in crossed_bits()]
    values, done = list(pair), ([], [])
    for bits in zip(*orders):
        moved = yield [(value, "dp", swap_pairs("dp", bit)) for value, bit in zip(values, bits)]
        for side, bit in enumerate(bits):
            axis = bit_axis(done[side], bit)
            values[side] = in_order((index & bit) != 0, values[side], moved[side], axis)
            done[side].append(bit)
    return [value.reshape((-1,) + own.shape[1:]) for value, own in zip(values, pair)]


def scatter_blocks(pair, index):
    orders = crossed_bits()
    left = [list(bits) for bits in orders]
    values = [value.reshape((2,) * len(orders[0]) + value.shape[1:]) for value in pair]
    for bits in zip(*orders):
        sent, kept = [], []
        for side, bit in enumerate(bits):
            parts = halves((index & bit) != 0, values[side], bit_axis(left[side], bit))
            sent.append((parts[0].astype(BF), "dp", swap_pairs("dp", bit)))
            kept.append(parts[1])
            left[side].remove(bit)
        moved = yield sent
        values = [plus(own, other) for own, other in zip(kept, moved)]
    return values


def exchange_blocks(value, index):
    count = value.shape[0]
    bits, left, done = all_bits(count), all_bits(count), []
    shape = value.shape[1:]
    value = value.reshape((2,) * len(bits) + shape)
    for bit in bits:
        high = (index & bit) != 0
        sent, kept = halves(high, value, bit_axis(left, bit))
        left.remove(bit)
        (moved,) = yield [(sent, "dp", swap_pairs("dp", bit))]
        value = in_order(high, kept, moved, len(left) + bit_axis(done, bit))
        done.append(bit)
    return value.reshape((count,) + shape)


def plus(*values):
    return sum(value.astype(F32) for value in values)


def sum_all(value, axis):
    bit = 1
    while bit < lax.axis_size(axis):
        value = value + swap(value, axis, bit)
        bit *= 2
    return value


def gather_in_order(value, axis, index):
    bit = 1
    while bit < lax.axis_size(axis):
        other = swap(value, axis, bit)
        high = (index & bit) != 0
        value = jnp.concatenate(
            [jnp.where(high, other, value), jnp.where(high, value, other)], axis=0
        )
        bit *= 2
    return value


def rows_from_mp(value, axis=0):
    far = swap(value, "mp", 2)
    near = swap(value, "mp", 1)
    return jnp.concatenate([value, near, far, swap(far, "mp", 1)], axis=axis)


def slots_from_mp(value):
    far, near = yield [(value, "mp", swap_pairs("mp", bit)) for bit in (2, 1)]
    (last,) = yield [(far, "mp", swap_pairs("mp", 1))]
    return [value, near, far, last]


def sum_to_mp(value):
    count = value.shape[0] // 4
    blocks = [value[k * count : (k + 1) * count] for k in range(4)]
    far = blocks[2].astype(F32) + swap(blocks[3].astype(BF), "mp", 1).astype(F32)
    near = blocks[0].astype(F32) + swap(blocks[1].astype(BF), "mp", 1).astype(F32)
    return near + swap(far.astype(BF), "mp", 2).astype(F32)


def shifted(steps, keep=lambda i: True):
    count = lax.axis_size("dp")
    return [(i, i + steps) for i in range(count) if keep(i) and 0 <= i + steps < count]


def even(i):
    return i % 2 == 0


def odd(i):
    return i % 2 == 1


def out_pairs():
    return shifted(-2, even) + shifted(2, odd)


def back_pairs():
    return shifted(2, even) + shifted(-2, odd)


def send_sets(own, is_odd):
    beside, low, high = yield [
        (own, "dp", swap_pairs("dp", 1)),
        (own, "dp", shifted(2)),
        (own, "dp", shifted(-2)),
    ]
    across, third = yield [
        (jnp.where(is_odd, low, high), "dp", swap_pairs("dp", 1)),
        (beside, "dp", out_pairs()),
    ]
    (fourth,) = yield [(across, "dp", back_pairs())]
    return [own, beside, low, high, across, third, fourth]


def set_offsets(is_odd):
    return jnp.where(
        is_odd, jnp.asarray([0, -1, -2, 2, 1, -3, 3]), jnp.asarray([0, 1, -2, 2, -1, 3, -3])
    )


def return_sets(grads, is_odd):
    own, beside, low, high, across, third, fourth = grads
    (fourth,) = yield [(fourth, "dp", out_pairs())]
    across, third = yield [
        (plus(across, fourth).astype(BF), "dp", swap_pairs("dp", 1)),
        (third, "dp", back_pairs()),
    ]
    low = plus(low, jnp.where(is_odd, across, 0)).astype(BF)
    high = plus(high, jnp.where(is_odd, 0, across)).astype(BF)
    beside, low, high = yield [
        (plus(beside, third).astype(BF), "dp", swap_pairs("dp", 1)),
        (low, "dp", shifted(-2)),
        (high, "dp", shifted(2)),
    ]
    return plus(own, beside, low, high)


def norm_rows(values, weights):
    return values * lax.rsqrt(jnp.mean(values * values, axis=-1, keepdims=True) + EPS) * weights


def modulate(values, weights, scales):
    return norm_rows(values, weights) * (1.0 + scales)


def gated_add(branch, weights, gates, resid):
    return resid + jnp.tanh(gates) * norm_rows(branch, weights)


def swiglu(gate_pre, up_pre):
    return jax.nn.silu(gate_pre) * up_pre


def lanes(rows):
    return lax.broadcasted_iota(jnp.int32, (rows, PAIR), 1)


def head_sum(values):
    low = lanes(values.shape[0]) < HD
    first = jnp.sum(jnp.where(low, values, 0.0), axis=-1, keepdims=True)
    second = jnp.sum(jnp.where(low, 0.0, values), axis=-1, keepdims=True)
    return jnp.where(low, first, second)


def partner(values):
    quarter = HD // 4
    first = (lanes(values.shape[0]) % (2 * quarter)) < quarter
    return jnp.where(
        first, pltpu.roll(values, PAIR - quarter, 1), pltpu.roll(values, quarter, 1)
    )


def normed(values):
    return values * lax.rsqrt(head_sum(values * values) / HD + EPS)


def prep_kernel(pre_ref, gains_ref, cos_ref, sin_ref, out_ref):
    width = out_ref.shape[1]
    rows = pre_ref.shape[0]
    cos, sin = cos_ref[...], sin_ref[...]
    for part in range(2):
        for start in range(0, width, PAIR):
            here = pl.ds(part * width + start, PAIR)
            turned = normed(pre_ref[:, here]) * gains_ref[part : part + 1, pl.ds(start, PAIR)]
            if part == 0:
                turned = turned * cos + partner(turned) * sin
                out_ref[pl.ds(0, rows), pl.ds(start, PAIR)] = turned.astype(BF)
            else:
                turned = turned * cos + partner(turned) * sin
                out_ref[pl.ds(rows, rows), pl.ds(start, PAIR)] = turned.astype(BF)
    out_ref[pl.ds(2 * rows, rows), :] = pre_ref[:, pl.ds(2 * width, width)].astype(BF)


def near_prep_kernel(gains_ref, cos_ref, sin_ref, *refs):
    *pre_refs, out_ref = refs
    rows, width = pre_refs[0].shape[0], out_ref.shape[1]
    depth = rows * len(pre_refs)
    for slot, pre_ref in enumerate(pre_refs):
        there = pl.ds(slot * rows, rows)
        cos, sin = cos_ref[there, :], sin_ref[there, :]
        for start in range(0, width, PAIR):
            here = pl.ds(start, PAIR)
            turned = normed(pre_ref[:, here]) * gains_ref[1:2, here]
            turned = turned * cos + partner(turned) * sin
            out_ref[there, here] = turned.astype(BF)
        out_ref[pl.ds(depth + slot * rows, rows), :] = pre_ref[:, pl.ds(width, width)].astype(BF)


def text_prep_kernel(pre_ref, gains_ref, out_ref):
    rows, width = pre_ref.shape[0], out_ref.shape[1]
    for start in range(0, width, PAIR):
        here = pl.ds(start, PAIR)
        value = normed(pre_ref[:, here]) * gains_ref[2:3, here]
        out_ref[pl.ds(0, rows), here] = value.astype(BF)
    out_ref[pl.ds(rows, rows), :] = pre_ref[:, pl.ds(width, width)].astype(BF)


def norm_back(pre, gains, grad):
    ratio = lax.rsqrt(head_sum(pre * pre) / HD + EPS)
    scaled = grad * gains
    grad_pre = ratio * scaled - pre * (ratio * ratio * ratio) * (head_sum(pre * scaled) / HD)
    return grad_pre, jnp.sum(grad * pre * ratio, axis=0, keepdims=True)


def query_back_kernel(pre_ref, gains_ref, cos_ref, sin_ref, self_ref, text_ref, out_ref, head_ref):
    cos, sin = cos_ref[...], sin_ref[...]
    head_ref[...] = jnp.zeros_like(head_ref)
    for start in range(0, out_ref.shape[1], PAIR):
        here = pl.ds(start, PAIR)
        grad = self_ref[:, here] + text_ref[:, here]
        grad = grad * cos - partner(grad) * sin
        grad_pre, grad_gain = norm_back(pre_ref[:, here], gains_ref[0:1, here], grad)
        out_ref[:, here] = grad_pre.astype(BF)
        head_ref[0:1, here] = grad_gain


def key_back_kernel(pre_ref, gains_ref, cos_ref, sin_ref, set_ref, out_ref, head_ref):
    rows, width = pre_ref.shape[0], set_ref.shape[1]
    cos, sin = cos_ref[...], sin_ref[...]
    head_ref[...] = jnp.zeros_like(head_ref)
    for start in range(0, width, PAIR):
        here = pl.ds(start, PAIR)
        grad = set_ref[pl.ds(0, rows), here]
        grad = grad * cos - partner(grad) * sin
        grad_pre, grad_gain = norm_back(
            pre_ref[:, pl.ds(width + start, PAIR)], gains_ref[1:2, here], grad
        )
        out_ref[:, here] = grad_pre.astype(BF)
        head_ref[0:1, here] = grad_gain
    out_ref[:, pl.ds(width, width)] = set_ref[pl.ds(rows, rows), :].astype(BF)


def text_back_kernel(pre_ref, gains_ref, set_ref, out_ref, head_ref):
    rows, width = pre_ref.shape[0], set_ref.shape[1]
    head_ref[...] = jnp.zeros_like(head_ref)
    for start in range(0, width, PAIR):
        here = pl.ds(start, PAIR)
        grad_pre, grad_gain = norm_back(
            pre_ref[:, here], gains_ref[2:3, here], set_ref[pl.ds(0, rows), here]
        )
        out_ref[:, here] = grad_pre.astype(BF)
        head_ref[0:1, here] = grad_gain
    out_ref[:, pl.ds(width, width)] = set_ref[pl.ds(rows, rows), :].astype(BF)


def split_pair(values):
    low = lanes(values.shape[0]) < HD
    zero = jnp.zeros_like(values)
    return jnp.where(low, values, zero), jnp.where(low, zero, values)


def forward_sums(live_ref, query_ref, set_refs, bias_ref, total, weight):
    low = lanes(query_ref.shape[0]) < HD
    total[...] = jnp.zeros_like(total)
    weight[...] = jnp.zeros_like(weight)
    for index, source in enumerate(set_refs):

        @pl.when(live_ref[index] > 0)
        def _(index=index, source=source):
            depth = source.shape[0] // 2
            keys, values = source[pl.ds(0, depth), :], source[pl.ds(depth, depth), :]
            outs, sums = [], []
            for query in split_pair(query_ref[...] * jnp.asarray(SCALE, BF)):
                logits = mm(query, keys, NT)
                if bias_ref is not None:
                    logits = logits + bias_ref[index : index + 1, :]
                probs = jnp.exp(logits)
                sums.append(jnp.sum(probs, axis=-1, keepdims=True))
                outs.append(mm(probs.astype(BF), values, NN))
            total[...] += jnp.where(low, outs[0], outs[1])
            weight[...] += jnp.where(low, sums[0], sums[1])


def views(own_ref, near_refs):
    depth = own_ref.shape[0]
    return [own_ref] + [
        near_ref.at[pl.ds(start, depth), :]
        for near_ref in near_refs
        for start in range(0, near_ref.shape[0], depth)
    ]


def self_forward_kernel(live_ref, query_ref, own_ref, *refs):
    *near_refs, out_ref, log_ref, total, weight = refs
    set_refs = views(own_ref, near_refs)
    forward_sums(live_ref, query_ref, set_refs, None, total, weight)
    out_ref[...] = total[...] / weight[...]
    log_ref[...] = jnp.log(weight[...])


def text_forward_kernel(live_ref, gate_ref, query_ref, self_ref, bias_ref, *refs):
    *set_refs, attn_ref, out_ref, log_ref, total, weight = refs
    forward_sums(live_ref, query_ref, set_refs, bias_ref, total, weight)
    low = lanes(query_ref.shape[0]) < HD
    pair = pl.program_id(0)
    gate = jnp.where(low, gate_ref[2 * pair], gate_ref[2 * pair + 1])
    out = total[...] / weight[...]
    attn_ref[...] = (self_ref[...] + gate * out).astype(BF)
    out_ref[...] = out
    log_ref[...] = jnp.log(weight[...])


def backward_sums(live_ref, query_ref, grad_ref, log_ref, delta, bias_ref, gates, refs, total):
    count = len(refs) // 2
    low = lanes(query_ref.shape[0]) < HD
    logs_all, delta_all = jnp.transpose(log_ref[...]), jnp.transpose(delta)
    total[...] = jnp.zeros_like(total)
    for index, (source, out_ref) in enumerate(zip(refs[:count], refs[count:])):

        @pl.when(live_ref[index] > 0)
        def _(index=index, source=source, out_ref=out_ref):
            queries = split_pair(query_ref[...] * jnp.asarray(SCALE, BF))
            grads = split_pair(grad_ref[...])
            depth = source.shape[0] // 2
            keys, values = source[pl.ds(0, depth), :], source[pl.ds(depth, depth), :]
            grad_query, grad_key, grad_value = [], [], []
            for head in range(2):
                row = head * HD
                logits = mm(keys, queries[head], NT)
                if bias_ref is not None:
                    logits = logits + bias_ref[:, index : index + 1]
                probs = jnp.exp(logits - logs_all[row : row + 1, :])
                value_part = mm(probs.astype(BF), grads[head], NN)
                grad_probs = mm(values, grads[head], NT)
                if gates is not None:
                    value_part = value_part * gates[head]
                    grad_probs = grad_probs * gates[head]
                grad_logits = (probs * (grad_probs - delta_all[row : row + 1, :])).astype(BF)
                grad_value.append(value_part)
                grad_key.append(mm(grad_logits, queries[head], NN))
                grad_query.append(mm(grad_logits, keys, TN))
            total[...] += jnp.where(low, grad_query[0], grad_query[1])
            out_ref[pl.ds(0, depth), :] = (grad_key[0] + grad_key[1]).astype(BF)
            out_ref[pl.ds(depth, depth), :] = (grad_value[0] + grad_value[1]).astype(BF)

        @pl.when(live_ref[index] == 0)
        def _(out_ref=out_ref):
            out_ref[...] = jnp.zeros_like(out_ref)


def self_backward_kernel(
    live_ref, query_ref, grad_ref, out_ref, log_ref, own_ref, *refs
):
    near_refs, grad_refs = refs[:NEAR_PARTS], list(refs[NEAR_PARTS:-2])
    query_grad_ref, total = refs[-2:]
    set_refs = views(own_ref, near_refs) + grad_refs
    delta = head_sum(grad_ref[...].astype(F32) * out_ref[...])
    backward_sums(live_ref, query_ref, grad_ref, log_ref, delta, None, None, set_refs, total)
    query_grad_ref[...] = total[...] * SCALE


def text_backward_kernel(
    live_ref, gate_ref, query_ref, grad_ref, out_ref, log_ref, bias_ref, *refs
):
    *set_refs, query_grad_ref, gate_grad_ref, total = refs
    low = lanes(query_ref.shape[0]) < HD
    pair = pl.program_id(0)
    gates = (gate_ref[2 * pair], gate_ref[2 * pair + 1])
    dots = head_sum(grad_ref[...].astype(F32) * out_ref[...])
    gate_grad_ref[...] = jnp.broadcast_to(jnp.sum(dots, axis=0, keepdims=True), gate_grad_ref.shape)
    delta = jnp.where(low, gates[0], gates[1]) * dots
    backward_sums(live_ref, query_ref, grad_ref, log_ref, delta, bias_ref, gates, set_refs, total)
    query_grad_ref[...] = total[...] * SCALE


def params(limit=40):
    return pltpu.CompilerParams(vmem_limit_bytes=limit * 2**20)


def whole(kernel, outs, cost, *args):
    shapes = [jax.ShapeDtypeStruct(shape, dtype) for shape, dtype in outs]
    return pl.pallas_call(
        kernel,
        out_shape=shapes if len(shapes) > 1 else shapes[0],
        compiler_params=params(),
        cost_estimate=pl.CostEstimate(flops=cost, bytes_accessed=2 * cost // 10, transcendentals=0),
    )(*args)


def column(rows):
    return pl.BlockSpec((rows, PAIR), lambda pair: (0, pair))


def fixed(shape):
    return pl.BlockSpec(shape, lambda pair: (0, 0))


def prepare_near(pre, gains, cos, sin, sets):
    rows, width = pre[0].shape[0] // sets, gains.shape[1]
    depth = rows * len(pre)

    def block(count, columns):
        return pl.BlockSpec((count, columns), lambda k: (k, 0))

    return pl.pallas_call(
        near_prep_kernel,
        grid=(sets,),
        in_specs=[pl.BlockSpec(gains.shape, lambda k: (0, 0))]
        + [block(depth, PAIR)] * 2
        + [block(rows, 2 * width)] * len(pre),
        out_specs=block(2 * depth, width),
        out_shape=jax.ShapeDtypeStruct((sets * 2 * depth, width), BF),
        compiler_params=params(),
        cost_estimate=pl.CostEstimate(
            flops=40 * sets * depth * width,
            bytes_accessed=12 * sets * depth * width,
            transcendentals=0,
        ),
    )(gains, cos, sin, *pre)


def attend(kernel, scalars, columns, bias, sets, outs, passes, scratch, limit=56):
    rows, width = columns[0].shape
    keys = sets[0].shape[0] // 2
    smem = pl.BlockSpec(memory_space=pltpu.SMEM)
    return pl.pallas_call(
        kernel,
        grid=(width // PAIR,),
        in_specs=[smem] * len(scalars)
        + [column(value.shape[0]) for value in columns]
        + [fixed(value.shape) for value in bias]
        + [column(value.shape[0]) for value in sets],
        out_specs=[column(depth) for depth, _ in outs],
        out_shape=[jax.ShapeDtypeStruct((depth, width), dtype) for depth, dtype in outs],
        scratch_shapes=[pltpu.VMEM((rows, PAIR), F32)] * scratch,
        compiler_params=params(limit),
        cost_estimate=pl.CostEstimate(
            flops=passes * 16 * rows * keys * width,
            bytes_accessed=40 * rows * width,
            transcendentals=4 * rows * keys * width // HD,
        ),
    )(*scalars, *columns, *bias, *sets)


def local(
    tokens,
    caption,
    condition,
    cotangent,
    qkv_weight,
    proj_weight,
    text_weight,
    ffn_weight,
    down_weight,
    ada_weight,
    norm_gains,
    head_gains,
    ada_bias,
    cross_gate,
    group_map,
    grid_width,
    caption_len,
):
    dp_count = lax.axis_size("dp")
    mp_count = lax.axis_size("mp")
    dp_index = lax.axis_index("dp")
    mp_index = lax.axis_index("mp")
    row_count, width = tokens.shape
    seq_len = row_count * mp_count
    local_width = qkv_weight.shape[2]
    local_heads = local_width // HD
    text_len, text_dim = caption.shape[1:]
    units = ffn_weight.shape[2]
    shard = qkv_weight.shape[1]
    weight_scale = 1.0 / math.sqrt(seq_len * dp_count)
    is_odd = (dp_index % 2) == 1
    links = Links()

    qkv_shard = jnp.transpose(qkv_weight, (1, 0, 2)).reshape(shard, 3 * local_width)
    rest_shard = jnp.concatenate(
        [proj_weight.T, jnp.transpose(ffn_weight, (1, 0, 2)).reshape(shard, 2 * units), down_weight.T],
        axis=1,
    )
    qkv_full = lax.all_gather(qkv_shard, "dp", axis=0, tiled=True)
    rest = lax.all_gather(rest_shard, "dp", axis=0, tiled=True)
    cuts = (0, local_width, local_width + 2 * units, local_width + 3 * units)
    proj_full, ffn_full, down_full = [rest[:, low:high] for low, high in zip(cuts[:-1], cuts[1:])]

    text_shard = text_weight.shape[1]
    quarter_rows = text_len // mp_count
    my_rows = lax.dynamic_slice_in_dim(caption[0], mp_index * quarter_rows, quarter_rows, axis=0)
    text_matrix = jnp.transpose(text_weight, (1, 0, 2)).reshape(text_shard, 2 * local_width)
    my_rows = jnp.transpose(my_rows.reshape(quarter_rows, dp_count, text_shard), (1, 0, 2))

    def modulate_all():
        value = jax.nn.silu(condition).astype(BF)
        for bit in all_bits(dp_count):
            (other,) = yield [(value, "dp", swap_pairs("dp", bit))]
            value = in_order((dp_index & bit) != 0, value, other, 0).reshape(2 * bit, width)
        cond_mine = lax.dynamic_slice_in_dim(value, dp_index * shard, shard, axis=1)
        value = mm(cond_mine, ada_weight, NN)
        for bit in all_bits(dp_count):
            (other,) = yield [(value, "dp", swap_pairs("dp", bit))]
            value = value + other
        bias_part = lax.dynamic_slice_in_dim(ada_bias, mp_index * width, width)
        value = (value + bias_part[None, :])[None]
        for bit in all_bits(mp_count):
            (other,) = yield [(value, "mp", swap_pairs("mp", bit))]
            value = in_order((mp_index & bit) != 0, value, other, 0).reshape(2 * bit, dp_count, width)
        return cond_mine, value

    def caption_features():
        value = yield from exchange_blocks(my_rows, dp_index)
        far, near = yield [(value, "mp", swap_pairs("mp", bit)) for bit in (2, 1)]
        (last,) = yield [(far, "mp", swap_pairs("mp", 1))]
        return jnp.concatenate([value, near, far, last], axis=1)

    mod_chain, caption_chain = Chain(modulate_all()), Chain(caption_features())
    token_chain = Chain(send_sets(tokens, is_odd))
    links.finish(mod_chain, caption_chain, token_chain)
    cond_mine, modulation = mod_chain.result
    text_all = caption_chain.result.reshape(dp_count * text_len, text_shard)

    origins = dp_index + set_offsets(is_odd)
    chosen = jnp.arange(dp_count)[None, :] == origins[:, None]

    def looked_up(table):
        return jnp.sum(jnp.where(chosen, table[None, :], 0), axis=1)

    inside = (origins >= 0) & (origins < dp_count)
    first_slot = jnp.sum(jnp.where(jnp.arange(dp_count) == dp_index, group_map, 0))
    grid = jnp.sum(jnp.where(jnp.arange(dp_count) == dp_index, grid_width, 0))
    live = (inside & (looked_up(group_map) == first_slot)).astype(jnp.int32)
    lengths = looked_up(caption_len)

    near_scales = jnp.sum(
        jnp.where(chosen[1:, :, None], modulation[0][None], 0.0), axis=1
    )
    scale_attn, gate_attn, scale_ffn, gate_ffn = [
        lax.dynamic_index_in_dim(modulation, dp_index, 1, False)[k] for k in range(4)
    ]
    gains = [norm_gains[k] for k in range(4)]
    act_rows = tokens.astype(F32)
    first_in, first_pull = jax.vjp(modulate, act_rows, gains[0], scale_attn)
    near_tokens = jnp.stack(token_chain.result[1:]).astype(F32)
    near_in = modulate(near_tokens, gains[0], near_scales[:, None, :]).astype(BF)
    near_sets = near_in.shape[0]

    text_part = mm(text_all, text_matrix, NN).astype(BF)
    text_part = text_part.reshape(dp_count, text_len, 2 * local_width)
    text_sum = Chain(
        scatter_blocks([text_part[..., :local_width], text_part[..., local_width:]], dp_index)
    )
    first_chain = Chain(slots_from_mp(first_in.astype(BF)))
    near_chains = [
        Chain(slots_from_mp(near_in[k : k + 2].reshape(2 * row_count, width)))
        for k in range(0, near_sets, 2)
    ]
    links.stage(text_sum, first_chain, near_chains[0])
    links.stage(text_sum, first_chain, *near_chains[:2])
    first_low = jnp.concatenate(first_chain.result, axis=0)

    blocks = mp_index ^ jnp.arange(mp_count, dtype=jnp.int32)
    token_ids = (blocks[:, None] * row_count + jnp.arange(row_count, dtype=jnp.int32)).reshape(-1)
    text_ids = (blocks[:, None] * quarter_rows + jnp.arange(quarter_rows, dtype=jnp.int32)).reshape(-1)
    positions = ((origins - first_slot)[:, None] * seq_len + token_ids[None, :]).reshape(-1)
    quarter = HD // 4
    lane = jnp.arange(PAIR, dtype=jnp.int32)
    freqs = jnp.exp((lane % quarter).astype(F32) * (-math.log(10000.0) / quarter))
    place = jnp.where((lane % HD < HD // 2)[None, :], (positions // grid)[:, None], (positions % grid)[:, None])
    angles = place.astype(F32) * freqs[None, :]
    cos = jnp.cos(angles)
    sin = jnp.sin(angles) * jnp.where((lane % (2 * quarter)) < quarter, -1.0, 1.0)[None, :]
    local_gains = lax.dynamic_slice_in_dim(head_gains, mp_index * local_width, local_width, axis=1)
    tanh_gate = jnp.tanh(lax.dynamic_slice_in_dim(cross_gate, mp_index * local_heads, local_heads))

    bias = jnp.where(text_ids[None, :] < lengths[:, None], 0.0, NEG).astype(F32)
    bias = jnp.concatenate([bias, bias[:1]], axis=0)

    def project(tie):
        qkv_pre = mm(tie(first_low), qkv_full, NN)
        prepared = whole(
            prep_kernel,
            [((3 * seq_len, local_width), BF)],
            20 * seq_len * 3 * local_width,
            qkv_pre,
            local_gains,
            cos[:seq_len],
            sin[:seq_len],
        )
        return qkv_pre, prepared

    part_sets = near_sets // NEAR_PARTS
    part_rows = part_sets * seq_len

    def project_near(tie, k):
        pre = [mm(tie(slot), qkv_full[:, local_width:], NN) for slot in near_chains[k].result]
        there = slice(seq_len + k * part_rows, seq_len + (k + 1) * part_rows)
        return prepare_near(pre, local_gains, cos[there], sin[there], part_sets)

    (qkv_pre, prepared), near_first = links.stage(
        text_sum, *near_chains, work=lambda tie: (project(tie), project_near(tie, 0))
    )
    query = prepared[:seq_len]
    links.finish(text_sum)
    text_pre = jnp.concatenate(text_sum.result, axis=1)
    text_set = whole(
        text_prep_kernel,
        [((2 * text_len, local_width), BF)],
        20 * text_len * 2 * local_width,
        text_pre,
        local_gains,
    )
    text_sets_chain = Chain(send_sets(text_set, is_odd))
    near_second = links.stage(
        text_sets_chain, *near_chains, work=lambda tie: project_near(tie, 1)
    )
    links.finish(*near_chains)
    near_third = links.stage(text_sets_chain, work=lambda tie: project_near(tie, 2))
    self_sets = [prepared[seq_len:], near_first, near_second, near_third]

    def attend_self(tie):
        return attend(
            self_forward_kernel, [live], [tie(query)], [], self_sets, [(seq_len, F32)] * 2, 2, 2
        )

    out_self, log_self = links.stage(text_sets_chain, work=attend_self)
    text_sets = text_sets_chain.result

    def attend_text(tie):
        attn_low, out_text, log_text = attend(
            text_forward_kernel,
            [live, tanh_gate],
            [tie(query), out_self],
            [bias],
            text_sets,
            [(seq_len, BF), (seq_len, F32), (seq_len, F32)],
            2,
            2,
        )
        return attn_low, out_text, log_text

    attn_low, out_text, log_text = links.stage(work=attend_text)
    attn_rows = sum_to_mp(mm(attn_low, proj_full, NT))
    middle, middle_pull = jax.vjp(gated_add, attn_rows, gains[1], gate_attn, act_rows)
    second_in, second_pull = jax.vjp(modulate, middle, gains[2], scale_ffn)
    second_low = rows_from_mp(second_in.astype(BF))
    ffn_pre = mm(second_low, ffn_full, NN)
    hidden_f, swiglu_pull = jax.vjp(swiglu, ffn_pre[:, :units], ffn_pre[:, units:])
    hidden_low = hidden_f.astype(BF)
    ffn_rows = sum_to_mp(mm(hidden_low, down_full, NT))
    result, result_pull = jax.vjp(gated_add, ffn_rows, gains[3], gate_ffn, middle)


    grad_out = cotangent.astype(F32)
    grad_ffn_rows, grad_gain_four, grad_gate_ffn, grad_middle_a = result_pull(grad_out)
    grad_ffn_all = rows_from_mp(grad_ffn_rows.astype(BF))
    grad_hidden = mm(grad_ffn_all, down_full, NN)
    grad_gate_pre, grad_up_pre = swiglu_pull(grad_hidden)
    grad_pre_low = jnp.concatenate([grad_gate_pre, grad_up_pre], axis=1).astype(BF)
    second_part = mm(grad_pre_low, ffn_full, NT).astype(BF)

    def ffn_backward(tie):
        grad_second = sum_to_mp(second_part)
        terms = [mm(second_low, grad_pre_low, TN), mm(grad_ffn_all, hidden_low, TN)]
        return grad_second, jnp.concatenate([term.astype(BF) for term in terms], axis=1)

    grad_second, ffn_terms = links.stage(work=ffn_backward)
    ffn_sum = lax.psum_scatter(ffn_terms, "dp", scatter_dimension=0, tiled=True)
    grad_middle_b, grad_gain_three, grad_scale_ffn = second_pull(grad_second)
    grad_attn_rows, grad_gain_two, grad_gate_attn, grad_act_a = middle_pull(
        grad_middle_a + grad_middle_b
    )
    grad_attn_all = links.stage(
        work=lambda tie: rows_from_mp(tie(grad_attn_rows.astype(BF)))
    )

    def text_backward(tie):
        grad_attn_low = mm(tie(grad_attn_all), proj_full, NN).astype(BF)
        return grad_attn_low, attend(
            text_backward_kernel,
            [live, tanh_gate],
            [query, grad_attn_low, out_text, log_text],
            [bias.T],
            text_sets,
            [(2 * text_len, BF)] * len(text_sets) + [(seq_len, F32), (8, F32)],
            5,
            1,
        )

    def self_backward(tie):
        return attend(
            self_backward_kernel,
            [live],
            [query, tie(grad_attn_low), out_self, log_self],
            [],
            self_sets,
            [(2 * seq_len, BF)] * (near_sets + 1) + [(seq_len, F32)],
            5,
            1,
        )

    grad_attn_low, text_grads = links.stage(work=text_backward)
    gate_dots = text_grads[-1]
    text_return = Chain(return_sets(text_grads[: len(text_sets)], is_odd))
    self_grads = links.stage(text_return, work=self_backward)
    self_return = Chain(return_sets(self_grads[:-1], is_odd))

    def query_backward(tie):
        grad_query_low, head_query = whole(
            query_back_kernel,
            [((seq_len, local_width), BF), ((8, local_width), F32)],
            20 * seq_len * local_width,
            qkv_pre,
            local_gains,
            cos[:seq_len],
            sin[:seq_len],
            tie(self_grads[-1]),
            text_grads[-2],
        )
        return (
            grad_query_low,
            head_query,
            mm(first_low, grad_query_low, TN).astype(BF),
            mm(grad_attn_all, attn_low, TN).astype(BF),
        )

    grad_query_low, head_query, grad_query_weight, grad_proj = links.stage(
        text_return, self_return, work=query_backward
    )

    def blocks(value):
        return value.reshape(dp_count, shard, local_width)

    query_sum = Chain(scatter_blocks([blocks(grad_query_weight), blocks(grad_proj)], dp_index))
    links.stage(text_return, self_return, query_sum)
    own_text = text_return.result

    def text_rows_backward(tie):
        return whole(
            text_back_kernel,
            [((text_len, 2 * local_width), BF), ((8, local_width), F32)],
            20 * text_len * 2 * local_width,
            text_pre,
            local_gains,
            tie(own_text),
        )

    grad_text_low, head_text = text_rows_backward(lambda value: value)
    text_back = Chain(
        gather_blocks([grad_text_low[:, :local_width], grad_text_low[:, local_width:]], dp_index)
    )
    links.finish_only(self_return, (query_sum, text_back))
    own_self, ffn_sum = lax.optimization_barrier((self_return.result, ffn_sum))

    def key_backward(tie):
        grad_key_low, head_key = whole(
            key_back_kernel,
            [((seq_len, 2 * local_width), BF), ((8, local_width), F32)],
            20 * seq_len * 2 * local_width,
            qkv_pre,
            local_gains,
            cos[:seq_len],
            sin[:seq_len],
            tie(own_self),
        )
        first_part = mm(grad_query_low, qkv_full[:, :local_width], NT) + mm(
            grad_key_low, qkv_full[:, local_width:], NT
        )
        return head_key, mm(first_low, grad_key_low, TN).astype(BF), first_part.astype(BF)

    head_key, grad_key_weight, first_part = links.stage(query_sum, text_back, work=key_backward)
    key_sum = Chain(
        scatter_blocks(
            [blocks(grad_key_weight[:, :local_width]), blocks(grad_key_weight[:, local_width:])],
            dp_index,
        )
    )
    grad_first = links.stage(
        query_sum, text_back, key_sum, work=lambda tie: sum_to_mp(tie(first_part))
    )
    grad_act_b, grad_gain_one, grad_scale_attn = first_pull(grad_first)
    grad_tokens = grad_act_a + grad_act_b
    mod_grads = jnp.stack([grad_scale_attn, grad_gate_attn, grad_scale_ffn, grad_gate_ffn])
    links.finish(text_back)
    text_rows = jnp.concatenate(text_back.result, axis=1)

    def gather_mod_grads(tie):
        mod_sum = sum_all(tie(mod_grads), "mp")
        mine = jnp.arange(mp_count)[:, None] == mp_index
        grad_mod_low = jnp.sum(jnp.where(mine, mod_sum, 0.0), axis=0)[None].astype(BF)
        return grad_mod_low, gather_in_order(grad_mod_low, "dp", dp_index)

    def caption_rows(tie):
        part = mm(tie(text_rows), text_matrix, NT).astype(BF)
        part = part.reshape(dp_count, mp_count, quarter_rows, text_shard)
        part = jnp.transpose(part, (1, 0, 2, 3)).reshape(-1, text_shard)
        return sum_to_mp(part).astype(BF).reshape(dp_count, quarter_rows, text_shard)

    (grad_mod_low, grad_mod_all), caption_mine = links.stage(
        query_sum, key_sum, work=lambda tie: (gather_mod_grads(tie), caption_rows(tie))
    )
    caption_back = Chain(exchange_blocks(caption_mine, dp_index))

    row_grads = jnp.stack([grad_gain_one, grad_gain_two, grad_gain_three, grad_gain_four])
    grad_ada = mm(cond_mine, grad_mod_all, TN) * weight_scale
    cond_part = mm(grad_mod_all, ada_weight, NT)
    zeros = functools.partial(jnp.zeros, dtype=F32)
    cond_rows = lax.dynamic_update_slice_in_dim(
        zeros((dp_count, width)), cond_part, dp_index * shard, 1
    )
    head_local = jnp.concatenate([head_query[:1], head_key[:1], head_text[:1]], axis=0)
    head_rows = lax.dynamic_update_slice_in_dim(
        zeros((3, width)), head_local, mp_index * local_width, 1
    )
    bias_rows = jnp.where(
        jnp.arange(mp_count)[:, None] == mp_index, grad_mod_low.astype(F32), 0.0
    )
    gate_local = gate_dots[0].reshape(local_heads, HD)[:, 0] * (1.0 - tanh_gate * tanh_gate)
    gate_row = lax.dynamic_update_slice_in_dim(
        zeros((1, width)), gate_local[None], mp_index * local_heads, 1
    )
    small = jnp.concatenate([row_grads, head_rows, bias_rows, gate_row, cond_rows], axis=0)
    small = links.stage(
        query_sum, key_sum, caption_back, work=lambda tie: sum_all(sum_all(tie(small), "mp"), "dp")
    )
    links.finish(query_sum, key_sum, caption_back)
    columns = jnp.transpose(caption_back.result, (1, 0, 2)).reshape(quarter_rows, text_dim)
    block = text_dim // mp_count
    grad_caption = jnp.zeros((text_len, block), F32)
    for bit in range(mp_count):
        other = mp_index ^ bit
        piece = lax.dynamic_slice_in_dim(columns, other * block, block, axis=1)
        if bit:
            piece = swap(piece, "mp", bit)
        grad_caption = lax.dynamic_update_slice_in_dim(
            grad_caption, piece.astype(F32), other * quarter_rows, 0
        )
    grad_text = mm(text_all, text_rows, TN) * weight_scale
    ffn_sum = ffn_sum.astype(F32) * weight_scale
    query_sum, proj_sum = [value * weight_scale for value in query_sum.result]
    key_sum, value_sum = [value * weight_scale for value in key_sum.result]
    cond_width = width // mp_count
    cond_sum = lax.dynamic_slice(small[12:], (dp_index, mp_index * cond_width), (1, cond_width))
    cond_cols = lax.dynamic_slice_in_dim(condition, mp_index * cond_width, cond_width, axis=1)
    silu_vals, silu_pull = jax.vjp(jax.nn.silu, cond_cols)
    grad_condition = silu_pull(cond_sum)[0] * (1.0 / math.sqrt(seq_len))
    scaled = small[:12] * weight_scale

    def parted(values, parts):
        return jnp.transpose(values.reshape(values.shape[0], parts, -1), (1, 0, 2))

    return (
        result.astype(BF),
        grad_tokens,
        grad_caption[None],
        grad_condition,
        jnp.stack([query_sum, key_sum, value_sum]),
        proj_sum.T,
        parted(grad_text, 2),
        parted(ffn_sum[:, : 2 * units], 2),
        ffn_sum[:, 2 * units :].T,
        grad_ada,
        scaled[:4],
        scaled[4:7],
        scaled[7:11].reshape(-1),
        scaled[11, :HEADS],
    )


def solution(mesh):
    return jax.shard_map(
        local,
        mesh=mesh,
        in_specs=(
            P(("dp", "mp"), None),
            P("dp", None, None),
            P("dp", None),
            P(("dp", "mp"), None),
            P(None, "dp", "mp"),
            P("mp", "dp"),
            P(None, "dp", "mp"),
            P(None, "dp", "mp"),
            P("mp", "dp"),
            P("dp", "mp"),
            P(),
            P(),
            P(),
            P(),
            P(),
            P(),
            P(),
        ),
        out_specs=(
            P(("dp", "mp"), None),
            P(("dp", "mp"), None),
            P("dp", None, "mp"),
            P("dp", "mp"),
            P(None, "dp", "mp"),
            P("mp", "dp"),
            P(None, "dp", "mp"),
            P(None, "dp", "mp"),
            P("mp", "dp"),
            P("dp", "mp"),
            P(),
            P(),
            P(),
            P(),
        ),
        check_vma=False,
    )
```

time: 905 us -> 866 us (0.957)
  starting transfers between devices: 192 us -> 134 us
  other arithmetic: 47.9 us -> 94 us
  local copies, waits for them, and re-layouts: 87.9 us -> 60.4 us
    ppermute x110 -> x77, starting transfers between devices: 140 us -> 108 us  [stage(): lax.ppermute(value, axis, pairs)]
    unnamed x455 -> x322, local copies, waits for them, and re-layouts: 49.3 us -> 19.7 us
    ppermute x57 -> x37, starting transfers between devices: 51.6 us -> 26.2 us  [swap(): return lax.ppermute(value, axis, [(i, i ^ bit) for i in range(count)])]
    dot_general x21 -> x32, matrix products: 50.3 us -> 66.6 us  [mm(): return lax.dot_general(left, right, dims, preferred_element_type=F32)]
    add x9 -> x24, other arithmetic: 1.18 us -> 17 us  [the longest x16 13.4 us: plus(): return sum((value.astype(F32) for value in values))]
    dot_general x3 -> x0, matrix products: 15 us -> none  [exact(): lax.dot_general(left, right, dims, preferred_element_type=F32, precision=...]
    another operation x0 -> x34, other arithmetic: none -> 12 us  [the longest x29 9.24 us: in_order(): jnp.stack([jnp.where(high, other, own), jnp.where(high, own, other)], axi...]
    convert_element_type x38 -> x23, other arithmetic: 23 us -> 14.7 us  [the longest x11 5.98 us: scatter_blocks(): sent.append((parts[0].astype(BF), 'dp', swap_pairs('dp', bit)))]
  transfers between devices with their start and end apart: 167 -> 117, of which waited for: 72 -> 59; matrix products, arithmetic and copies ran while one was open for 18% -> 20% of each run, Pallas kernels for 6% -> 7%
where the time goes in v2:
time: 866 us; the launch traced here: 856 us
  waiting for transfers between devices  421 us (49%)
  starting transfers between devices  134 us (15%)
  other arithmetic  94 us (11%)
  matrix products  66.6 us (8%)
  Pallas kernels  61.1 us (7%)
  local copies, waits for them, and re-layouts  60.4 us (7%)
  between operations  19 us (2%)
    ppermute x77, waiting for transfers between devices, stage(): lax.ppermute(value, axis, pairs)  316 us
    ppermute x77, starting transfers between devices, stage(): lax.ppermute(value, axis, pairs)  108 us
    ppermute x37, waiting for transfers between devices, swap(): return lax.ppermute(value, axis, [(i, i ^ bit) for i in range(count)])  104 us
    dot_general x32, matrix products, mm(): return lax.dot_general(left, right, dims, preferred_element_type=F32)  66.6 us
    pallas_call x4, Pallas kernels, attend(): pl.pallas_call(kernel, grid=(width // PAIR,), in_specs=[smem] * len(scala...  44 us
    ppermute x37, starting transfers between devices, swap(): return lax.ppermute(value, axis, [(i, i ^ bit) for i in range(count)])  26.2 us
    unnamed x322, local copies, waits for them, and re-layouts  19.7 us
  transfers between devices with their start and end apart: 117, of which 59 were waited for; matrix products, arithmetic and copies ran while one was open for 20% of the time, Pallas kernels for 7%

profile of v2, /device:TPU:0, one launch (start us, length us, event | category | flops | bytes accessed | tf_op | source)
XLA Modules:
  0.0 855.8 jit_solution(16873225167522470880)
XLA Ops:
  46.8 11.9 %collective-permute-done.6 = bf16[2,2,64,512]{3,2,1,0:T(8,128)(2,1)S(1)} collective-permute-done((bf16[2,2,64,512]{3,2,1,0:T(8,128)(2,1)S(1)}, bf16[2,2,64,512]{3,2,1,0:T(8,128)(2,1)S(1)}, u32[]{:S(2)}, u32[]{:S(2)}) %collective-permute-start.6) | collective-permute-done | bytes 262176 | tf_op jit(solution)/shard_map/ppermute | solution.py:65
  59.9 22.1 %collective-permute-done.8 = bf16[128,1536]{1,0:T(8,128)(2,1)} collective-permute-done((bf16[128,1536]{1,0:T(8,128)(2,1)}, bf16[128,1536]{1,0:T(8,128)(2,1)}, u32[]{:S(2)}, u32[]{:S(2)}) %collective-permute-start.8) | collective-permute-done | bytes 393248 | tf_op jit(solution)/shard_map/ppermute | solution.py:65
  90.1 8.6 %collective-permute-done.10 = bf16[2,2,64,512]{3,2,1,0:T(8,128)(2,1)S(1)} collective-permute-done((bf16[2,2,64,512]{3,2,1,0:T(8,128)(2,1)S(1)}, bf16[2,2,64,512]{3,2,1,0:T(8,128)(2,1)S(1)}, u32[]{:S(2)}, u32[]{:S(2)}) %collective-permute-start.10) | collective-permute-done | bytes 262176 | tf_op jit(solution)/shard_map/ppermute | solution.py:65
  119.8 6.2 collective-permute-done.15
  130.2 6.1 collective-permute-done.17
  154.1 8.6 %sine_multiply_fusion = (f32[3584,128]{1,0:T(8,128)}, f32[3584,128]{1,0:T(8,128)}) fusion(f32[128]{0:T(128)S(1)} %copy-done.141, f32[128]{0:T(128)S(1)} %copy-done.142, s32[3584]{0:T(1024)S(1)} %copy-done.125, s32[3584]{0:T(1024)S(1)} %copy-done.126, pred[128]{0:T(512)(128)(4,1)S(1)} %copy-done.143), kind=kLoop, calls=%fused_computation.38 | loop fusion | flops 1835008 | bytes 3699840 | tf_op jit(solution)/shard_map/mul | solution.py:697
  166.8 9.5 %collective-permute-done.20 = bf16[2,2,256,384]{3,2,0,1:T(8,128)(2,1)} collective-permute-done((bf16[2,2,256,384]{3,2,0,1:T(8,128)(2,1)}, bf16[2,2,256,384]{3,2,0,1:T(8,128)(2,1)}, u32[]{:S(2)}, u32[]{:S(2)}) %collective-permute-start.20) | collective-permute-done | bytes 786464 | tf_op jit(solution)/shard_map/ppermute | solution.py:65
  176.3 21.3 %collective-permute-done.21 = bf16[2,2,256,384]{3,2,0,1:T(8,128)(2,1)S(1)} collective-permute-done((bf16[2,2,256,384]{3,2,0,1:T(8,128)(2,1)}, bf16[2,2,256,384]{3,2,0,1:T(8,128)(2,1)S(1)}, u32[]{:S(2)}, u32[]{:S(2)}) %collective-permute-start.21) | collective-permute-done | bytes 786464 | tf_op jit(solution)/shard_map/ppermute | solution.py:65
  207.2 19.0 %collective-permute-done.26 = bf16[2,256,384]{2,1,0:T(8,128)(2,1)} collective-permute-done((bf16[2,256,384]{2,1,0:T(8,128)(2,1)S(1)}, bf16[2,256,384]{2,1,0:T(8,128)(2,1)}, u32[]{:S(2)}, u32[]{:S(2)}) %collective-permute-start.26) | collective-permute-done | bytes 393248 | tf_op jit(solution)/shard_map/ppermute | solution.py:65
  265.6 12.0 %collective-permute-done.33 = bf16[256,384]{1,0:T(8,128)(2,1)} collective-permute-done((bf16[256,384]{1,0:T(8,128)(2,1)}, bf16[256,384]{1,0:T(8,128)(2,1)}, u32[]{:S(2)}, u32[]{:S(2)}) %collective-permute-start.33) | collective-permute-done | bytes 196640 | tf_op jit(solution)/shard_map/ppermute | solution.py:65
  317.0 7.7 shard_map.295
  325.5 6.4 shard_map.296
  338.0 9.7 %collective-permute-done.46 = bf16[128,1536]{1,0:T(8,128)(2,1)S(1)} collective-permute-done((bf16[128,1536]{1,0:T(8,128)(2,1)S(1)}, bf16[128,1536]{1,0:T(8,128)(2,1)S(1)}, u32[]{:S(2)}, u32[]{:S(2)}) %collective-permute-start.46) | collective-permute-done | bytes 393248 | tf_op jit(solution)/shard_map/ppermute | solution.py:31
  350.9 8.9 %collective-permute-done.48 = bf16[128,1536]{1,0:T(8,128)(2,1)S(1)} collective-permute-done((bf16[128,1536]{1,0:T(8,128)(2,1)S(1)}, bf16[128,1536]{1,0:T(8,128)(2,1)S(1)}, u32[]{:S(2)}, u32[]{:S(2)}) %collective-permute-start.48) | collective-permute-done | bytes 393248 | tf_op jit(solution)/shard_map/ppermute | solution.py:31
  370.9 9.7 %collective-permute-done.52 = bf16[128,1536]{1,0:T(8,128)(2,1)S(1)} collective-permute-done((bf16[128,1536]{1,0:T(8,128)(2,1)S(1)}, bf16[128,1536]{1,0:T(8,128)(2,1)S(1)}, u32[]{:S(2)}, u32[]{:S(2)}) %collective-permute-start.52) | collective-permute-done | bytes 393248 | tf_op jit(solution)/shard_map/ppermute | solution.py:31
  384.1 8.9 %collective-permute-done.54 = bf16[128,1536]{1,0:T(8,128)(2,1)S(1)} collective-permute-done((bf16[128,1536]{1,0:T(8,128)(2,1)S(1)}, bf16[128,1536]{1,0:T(8,128)(2,1)S(1)}, u32[]{:S(2)}, u32[]{:S(2)}) %collective-permute-start.54) | collective-permute-done | bytes 393248 | tf_op jit(solution)/shard_map/ppermute | solution.py:31
  430.4 9.2 %collective-permute-done.60 = bf16[128,1536]{1,0:T(8,128)(2,1)} collective-permute-done((bf16[128,1536]{1,0:T(8,128)(2,1)}, bf16[128,1536]{1,0:T(8,128)(2,1)}, u32[]{:S(2)}, u32[]{:S(2)}) %collective-permute-start.60) | collective-permute-done | bytes 393248 | tf_op jit(solution)/shard_map/ppermute | solution.py:31
  446.1 11.9 %shard_map.297 = (bf16[512,384]{1,0:T(8,128)(2,1)}, bf16[512,384]{1,0:T(8,128)(2,1)}, bf16[512,384]{1,0:T(8,128)(2,1)}, bf16[512,384]{1,0:T(8,128)(2,1)}, bf16[5...) custom-call(s32[7]{0:T(128)} %and_convert_fusion.live_ref, ...), custom_call_target="tpu_custom_call" | custom-call | flops 4026531840 | bytes 7864320 | tf_op jit(solution)/shard_map/pallas_call | solution.py:550
  459.5 18.1 %shard_map.298 = (bf16[1024,384]{1,0:T(8,128)(2,1)}, bf16[1024,384]{1,0:T(8,128)(2,1)}, bf16[1024,384]{1,0:T(8,128)(2,1)}, bf16[1024,384]{1,0:T(8,128)(2,1)}, bf...) custom-call(s32[7]{0:T(128)} %and_convert_fusion.live_ref, ...), custom_call_target="tpu_custom_call" | custom-call | flops 8053063680 | bytes 7864320 | tf_op jit(solution)/shard_map/pallas_call | solution.py:550
  477.5 27.1 %collective-permute-done.62 = bf16[512,384]{1,0:T(8,128)(2,1)S(1)} collective-permute-done((bf16[512,384]{1,0:T(8,128)(2,1)}, bf16[512,384]{1,0:T(8,128)(2,1)S(1)}, u32[]{:S(2)}, u32[]{:S(2)}) %collective-permute-start.62) | collective-permute-done | bytes 393248 | tf_op jit(solution)/shard_map/ppermute | solution.py:65
  506.2 7.3 collective-permute-start.63
  527.7 15.8 %collective-permute-done.65 = bf16[1024,384]{1,0:T(8,128)(2,1)S(1)} collective-permute-done((bf16[1024,384]{1,0:T(8,128)(2,1)}, bf16[1024,384]{1,0:T(8,128)(2,1)S(1)}, u32[]{:S(2)}, u32[]{:S(2)}) %collective-permute-start.65) | collective-permute-done | bytes 786464 | tf_op jit(solution)/shard_map/ppermute | solution.py:65
  553.6 12.1 %collective-permute-done.66 = bf16[512,384]{1,0:T(8,128)(2,1)S(1)} collective-permute-done((bf16[512,384]{1,0:T(8,128)(2,1)S(1)}, bf16[512,384]{1,0:T(8,128)(2,1)S(1)}, u32[]{:S(2)}, u32[]{:S(2)}) %collective-permute-start.66) | collective-permute-done | bytes 393248 | tf_op jit(solution)/shard_map/ppermute | solution.py:65
  569.6 24.9 %collective-permute-done.68 = bf16[512,384]{1,0:T(8,128)(2,1)S(1)} collective-permute-done((bf16[512,384]{1,0:T(8,128)(2,1)S(1)}, bf16[512,384]{1,0:T(8,128)(2,1)S(1)}, u32[]{:S(2)}, u32[]{:S(2)}) %collective-permute-start.68) | collective-permute-done | bytes 393248 | tf_op jit(solution)/shard_map/ppermute | solution.py:65
  594.5 10.6 %collective-permute-done.71 = bf16[2,2,192,384]{3,2,0,1:T(8,128)(2,1)S(1)} collective-permute-done((bf16[2,2,192,384]{3,2,0,1:T(8,128)(2,1)S(1)}, bf16[2,2,192,384]{3,2,0,1:T(8,128)(2,1)S(1)}, u32[]{:S(2)}, u32[]{:S(2)}) %collective-permute-start.71) | collective-permute-done | bytes 589856 | tf_op jit(solution)/shard_map/ppermute | solution.py:65
  615.4 6.3 collective-permute-start.75
  627.3 34.0 %collective-permute-done.78 = bf16[256,384]{1,0:T(8,128)(2,1)} collective-permute-done((bf16[256,384]{1,0:T(8,128)(2,1)S(1)}, bf16[256,384]{1,0:T(8,128)(2,1)}, u32[]{:S(2)}, u32[]{:S(2)}) %collective-permute-start.78) | collective-permute-done | bytes 196640 | tf_op jit(solution)/shard_map/ppermute | solution.py:65
  717.0 22.4 %collective-permute-done.86 = bf16[2,2,192,384]{3,2,0,1:T(8,128)(2,1)S(1)} collective-permute-done((bf16[2,2,192,384]{3,2,0,1:T(8,128)(2,1)S(1)}, bf16[2,2,192,384]{3,2,0,1:T(8,128)(2,1)S(1)}, u32[]{:S(2)}, u32[]{:S(2)}) %collective-permute-start.86) | collective-permute-done | bytes 589856 | tf_op jit(solution)/shard_map/ppermute | solution.py:65
  761.5 9.6 %collective-permute-done.100 = bf16[512,512]{1,0:T(8,128)(2,1)S(1)} collective-permute-done((bf16[512,512]{1,0:T(8,128)(2,1)S(1)}, bf16[512,512]{1,0:T(8,128)(2,1)S(1)}, u32[]{:S(2)}, u32[]{:S(2)}) %collective-permute-start.100) | collective-permute-done | bytes 524320 | tf_op jit(solution)/shard_map/ppermute | solution.py:31
  805.4 12.4 %collective-permute-done.108 = f32[20,1536]{1,0:T(8,128)S(1)} collective-permute-done((f32[20,1536]{1,0:T(8,128)S(1)}, f32[20,1536]{1,0:T(8,128)S(1)}, u32[]{:S(2)}, u32[]{:S(2)}) %collective-permute-start.108) | collective-permute-done | bytes 122912 | tf_op jit(solution)/shard_map/ppermute | solution.py:31
  818.8 5.8 collective-permute-done.109
  827.1 9.9 %collective-permute-done.110 = bf16[2,2,64,512]{3,2,1,0:T(8,128)(2,1)S(1)} collective-permute-done((bf16[2,2,64,512]{3,2,1,0:T(8,128)(2,1)S(1)}, bf16[2,2,64,512]{3,2,1,0:T(8,128)(2,1)S(1)}, u32[]{:S(2)}, u32[]{:S(2)}) %collective-permute-start.110) | collective-permute-done | bytes 262176 | tf_op jit(solution)/shard_map/ppermute | solution.py:65
  (820 shorter events, 422.9 us)
Async XLA Ops:
  7.2 236.6 %all-gather.3.cloned.1.call-start = ((), (), s32[]{:S(2)}) async-start(), calls=%async_computation.1 | async-start | bytes 3981312 | tf_op jit(solution)/shard_map/all_gather | solution.py:608
  9.2 322.6 %all-gather.5.cloned.1.call-start = ((), (), s32[]{:S(2)}) async-start(), calls=%async_computation.2 | async-start | bytes 11943936 | tf_op jit(solution)/shard_map/all_gather | solution.py:609
  9.3 28.7 %collective-permute-start.2 = (bf16[128,1536]{1,0:T(8,128)(2,1)}, bf16[128,1536]{1,0:T(8,128)(2,1)}, u32[]{:S(2)}, u32[]{:S(2)}) collective-permute-start(bf16[128,1536]{1,0:T(8,128)(2,1)} %param.19), channel_id=1, source_target_pairs={{0,4},{4,0},{8,12},{12,8},{16,20},{20,16},{24,28},{28,24},{1,5},{5... | collective-permute-start | bytes 1179656 | tf_op jit(solution)/shard_map/ppermute | solution.py:65
  23.0 664.8 %reduce-scatter.2.cloned.1.call-start = ((), (), s32[]{:S(2)}) async-start(), calls=%async_computation.3 | async-start | bytes 10616832 | tf_op jit(solution)/shard_map/reduce_scatter | solution.py:793
  45.5 36.6 %collective-permute-start.8 = (bf16[128,1536]{1,0:T(8,128)(2,1)}, bf16[128,1536]{1,0:T(8,128)(2,1)}, u32[]{:S(2)}, u32[]{:S(2)}) collective-permute-start(bf16[128,1536]{1,0:T(8,128)(2,1)} %collective-permute-done.2), channel_id=1, source_target_pairs={{8,0},{16,8},{24,16},{4,12},{12,20},{20,28},{9,1},{17,9},{25,17},{... | collective-permute-start | bytes 1179656 | tf_op jit(solution)/shard_map/ppermute | solution.py:65
  147.2 29.1 %collective-permute-start.20 = (bf16[2,2,256,384]{3,2,0,1:T(8,128)(2,1)}, bf16[2,2,256,384]{3,2,0,1:T(8,128)(2,1)}, u32[]{:S(2)}, u32[]{:S(2)}) collective-permute-start(bf16[2,2,256,384]{3,2,0,1:T(8,128)(2,1)} %select_bitcast_fusion.5), channel_id=1, source_target_pairs={{0,4},{4,0},{8,12},{12,8},{16,20},{20,16},{24,28},{28,24},{1,5},{5... | collective-permute-start | bytes 2359304 | tf_op jit(solution)/shard_map/ppermute | solution.py:65
  152.1 45.6 %collective-permute-start.21 = (bf16[2,2,256,384]{3,2,0,1:T(8,128)(2,1)}, bf16[2,2,256,384]{3,2,0,1:T(8,128)(2,1)S(1)}, u32[]{:S(2)}, u32[]{:S(2)}) collective-permute-start(bf16[2,2,256,384]{3,2,0,1:T(8,128)(2,1)} %select_bitcast_fusion.4), channel_id=1, source_target_pairs={{0,8},{4,12},{8,0},{12,4},{16,24},{20,28},{24,16},{28,20},{1,9},{5... | collective-permute-start | bytes 2359304 | tf_op jit(solution)/shard_map/ppermute | solution.py:65
  153.5 44.1 %collective-permute-start.24 = (bf16[256,1536]{1,0:T(8,128)(2,1)S(1)}, bf16[256,1536]{1,0:T(8,128)(2,1)}, u32[]{:S(2)}, u32[]{:S(2)}) collective-permute-start(bf16[256,1536]{1,0:T(8,128)(2,1)S(1)} %bitcast.424), channel_id=1, source_target_pairs={{0,2},{1,3},{2,0},{3,1},{4,6},{5,7},{6,4},{7,5},{8,10},{9,11},{10,... | collective-permute-start | bytes 2359304 | tf_op jit(solution)/shard_map/ppermute | solution.py:65
  154.1 44.4 %collective-permute-start.25 = (bf16[256,1536]{1,0:T(8,128)(2,1)S(1)}, bf16[256,1536]{1,0:T(8,128)(2,1)}, u32[]{:S(2)}, u32[]{:S(2)}) collective-permute-start(bf16[256,1536]{1,0:T(8,128)(2,1)S(1)} %bitcast.425), channel_id=1, source_target_pairs={{0,1},{1,0},{2,3},{3,2},{4,5},{5,4},{6,7},{7,6},{8,9},{9,8},{10,11... | collective-permute-start | bytes 2359304 | tf_op jit(solution)/shard_map/ppermute | solution.py:65
  202.4 29.7 %collective-permute-start.29 = (bf16[256,1536]{1,0:T(8,128)(2,1)}, bf16[256,1536]{1,0:T(8,128)(2,1)}, u32[]{:S(2)}, u32[]{:S(2)}) collective-permute-start(bf16[256,1536]{1,0:T(8,128)(2,1)} %collective-permute-done.24), channel_id=1, source_target_pairs={{0,1},{1,0},{2,3},{3,2},{4,5},{5,4},{6,7},{7,6},{8,9},{9,8},{10,11... | collective-permute-start | bytes 2359304 | tf_op jit(solution)/shard_map/ppermute | solution.py:65
  202.4 29.7 %collective-permute-start.30 = (bf16[256,1536]{1,0:T(8,128)(2,1)S(1)}, bf16[256,1536]{1,0:T(8,128)(2,1)}, u32[]{:S(2)}, u32[]{:S(2)}) collective-permute-start(bf16[256,1536]{1,0:T(8,128)(2,1)S(1)} %bitcast.421), channel_id=1, source_target_pairs={{0,2},{1,3},{2,0},{3,1},{4,6},{5,7},{6,4},{7,5},{8,10},{9,11},{10,... | collective-permute-start | bytes 2359304 | tf_op jit(solution)/shard_map/ppermute | solution.py:65
  236.6 29.0 %collective-permute-start.32 = (bf16[256,384]{1,0:T(8,128)(2,1)}, bf16[256,384]{1,0:T(8,128)(2,1)}, u32[]{:S(2)}, u32[]{:S(2)}) collective-permute-start(bf16[256,384]{1,0:T(8,128)(2,1)} %get-tuple-element.302), channel_id=1, source_target_pairs={{0,16},{4,20},{8,24},{12,28},{16,0},{20,4},{24,8},{28,12},{1,17},{... | collective-permute-start | bytes 589832 | tf_op jit(solution)/shard_map/ppermute | solution.py:65
  236.7 41.0 %collective-permute-start.33 = (bf16[256,384]{1,0:T(8,128)(2,1)}, bf16[256,384]{1,0:T(8,128)(2,1)}, u32[]{:S(2)}, u32[]{:S(2)}) collective-permute-start(bf16[256,384]{1,0:T(8,128)(2,1)} %get-tuple-element.303), channel_id=1, source_target_pairs={{0,16},{4,20},{8,24},{12,28},{16,0},{20,4},{24,8},{28,12},{1,17},{... | collective-permute-start | bytes 589832 | tf_op jit(solution)/shard_map/ppermute | solution.py:65
  239.6 38.1 %collective-permute-start.34 = (bf16[256,1536]{1,0:T(8,128)(2,1)}, bf16[256,1536]{1,0:T(8,128)(2,1)}, u32[]{:S(2)}, u32[]{:S(2)}) collective-permute-start(bf16[256,1536]{1,0:T(8,128)(2,1)} %collective-permute-done.30), channel_id=1, source_target_pairs={{0,1},{1,0},{2,3},{3,2},{4,5},{5,4},{6,7},{7,6},{8,9},{9,8},{10,11... | collective-permute-start | bytes 2359304 | tf_op jit(solution)/shard_map/ppermute | solution.py:65
  239.6 38.1 %collective-permute-start.35 = (bf16[256,1536]{1,0:T(8,128)(2,1)}, bf16[256,1536]{1,0:T(8,128)(2,1)}, u32[]{:S(2)}, u32[]{:S(2)}) collective-permute-start(bf16[256,1536]{1,0:T(8,128)(2,1)} %bitcast.57), channel_id=1, source_target_pairs={{0,2},{1,3},{2,0},{3,1},{4,6},{5,7},{6,4},{7,5},{8,10},{9,11},{10,... | collective-permute-start | bytes 2359304 | tf_op jit(solution)/shard_map/ppermute | solution.py:65
  241.0 36.6 %collective-permute-start.36 = (bf16[256,1536]{1,0:T(8,128)(2,1)}, bf16[256,1536]{1,0:T(8,128)(2,1)}, u32[]{:S(2)}, u32[]{:S(2)}) collective-permute-start(bf16[256,1536]{1,0:T(8,128)(2,1)} %bitcast.57), channel_id=1, source_target_pairs={{0,1},{1,0},{2,3},{3,2},{4,5},{5,4},{6,7},{7,6},{8,9},{9,8},{10,11... | collective-permute-start | bytes 2359304 | tf_op jit(solution)/shard_map/ppermute | solution.py:65
  458.0 46.6 %collective-permute-start.62 = (bf16[512,384]{1,0:T(8,128)(2,1)}, bf16[512,384]{1,0:T(8,128)(2,1)S(1)}, u32[]{:S(2)}, u32[]{:S(2)}) collective-permute-start(bf16[512,384]{1,0:T(8,128)(2,1)} %get-tuple-element.371), channel_id=1, source_target_pairs={{8,0},{16,8},{24,16},{4,12},{12,20},{20,28},{9,1},{17,9},{25,17},{... | collective-permute-start | bytes 1179656 | tf_op jit(solution)/shard_map/ppermute | solution.py:65
  504.8 38.7 %collective-permute-start.65 = (bf16[1024,384]{1,0:T(8,128)(2,1)}, bf16[1024,384]{1,0:T(8,128)(2,1)S(1)}, u32[]{:S(2)}, u32[]{:S(2)}) collective-permute-start(bf16[1024,384]{1,0:T(8,128)(2,1)} %get-tuple-element.387), channel_id=1, source_target_pairs={{8,0},{16,8},{24,16},{4,12},{12,20},{20,28},{9,1},{17,9},{25,17},{... | collective-permute-start | bytes 2359304 | tf_op jit(solution)/shard_map/ppermute | solution.py:65
  547.2 58.0 %collective-permute-start.69 = (bf16[1024,384]{1,0:T(8,128)(2,1)S(1)}, bf16[1024,384]{1,0:T(8,128)(2,1)S(1)}, u32[]{:S(2)}, u32[]{:S(2)}) collective-permute-start(bf16[1024,384]{1,0:T(8,128)(2,1)S(1)} %add_convert_fusion.3), channel_id=1, source_target_pairs={{0,4},{4,0},{8,12},{12,8},{16,20},{20,16},{24,28},{28,24},{1,5},{5... | collective-permute-start | bytes 2359304 | tf_op jit(solution)/shard_map/ppermute | solution.py:65
  548.9 56.3 %collective-permute-start.70 = (bf16[1024,384]{1,0:T(8,128)(2,1)S(1)}, bf16[1024,384]{1,0:T(8,128)(2,1)S(1)}, u32[]{:S(2)}, u32[]{:S(2)}) collective-permute-start(bf16[1024,384]{1,0:T(8,128)(2,1)S(1)} %copy-done.149), channel_id=1, source_target_pairs={{0,8},{8,16},{16,24},{12,4},{20,12},{28,20},{1,9},{9,17},{17,25},{... | collective-permute-start | bytes 2359304 | tf_op jit(solution)/shard_map/ppermute | solution.py:65
  553.5 51.7 %collective-permute-start.71 = (bf16[2,2,192,384]{3,2,0,1:T(8,128)(2,1)S(1)}, bf16[2,2,192,384]{3,2,0,1:T(8,128)(2,1)S(1)}, u32[]{:S(2)}, u32[]{:S(2)}) collective-permute-start(bf16[2,2,192,384]{3,2,0,1:T(8,128)(2,1)S(1)} %select_bitcast_fusion.9), channel_id=1, source_target_pairs={{0,4},{4,0},{8,12},{12,8},{16,20},{20,16},{24,28},{28,24},{1,5},{5... | collective-permute-start | bytes 1769480 | tf_op jit(solution)/shard_map/ppermute | solution.py:65
  565.6 39.5 %collective-permute-start.72 = (bf16[2,2,192,384]{3,2,0,1:T(8,128)(2,1)S(1)}, bf16[2,2,192,384]{3,2,0,1:T(8,128)(2,1)S(1)}, u32[]{:S(2)}, u32[]{:S(2)}) collective-permute-start(bf16[2,2,192,384]{3,2,0,1:T(8,128)(2,1)S(1)} %select_bitcast_fusion.8), channel_id=1, source_target_pairs={{0,8},{4,12},{8,0},{12,4},{16,24},{20,28},{24,16},{28,20},{1,9},{5... | collective-permute-start | bytes 1769480 | tf_op jit(solution)/shard_map/ppermute | solution.py:65
  611.7 61.8 %collective-permute-start.73 = (bf16[1024,384]{1,0:T(8,128)(2,1)}, bf16[1024,384]{1,0:T(8,128)(2,1)}, u32[]{:S(2)}, u32[]{:S(2)}) collective-permute-start(bf16[1024,384]{1,0:T(8,128)(2,1)} %add_convert_fusion.2), channel_id=1, source_target_pairs={{0,4},{4,0},{8,12},{12,8},{16,20},{20,16},{24,28},{28,24},{1,5},{5... | collective-permute-start | bytes 2359304 | tf_op jit(solution)/shard_map/ppermute | solution.py:65
  614.1 59.3 %collective-permute-start.74 = (bf16[1024,384]{1,0:T(8,128)(2,1)}, bf16[1024,384]{1,0:T(8,128)(2,1)}, u32[]{:S(2)}, u32[]{:S(2)}) collective-permute-start(bf16[1024,384]{1,0:T(8,128)(2,1)} %get-tuple-element.424), channel_id=1, source_target_pairs={{8,0},{12,4},{16,8},{20,12},{24,16},{28,20},{9,1},{13,5},{17,9},{2... | collective-permute-start | bytes 2359304 | tf_op jit(solution)/shard_map/ppermute | solution.py:65
  615.4 58.1 %collective-permute-start.75 = (bf16[1024,384]{1,0:T(8,128)(2,1)}, bf16[1024,384]{1,0:T(8,128)(2,1)}, u32[]{:S(2)}, u32[]{:S(2)}) collective-permute-start(bf16[1024,384]{1,0:T(8,128)(2,1)} %get-tuple-element.425), channel_id=1, source_target_pairs={{0,8},{4,12},{8,16},{12,20},{16,24},{20,28},{1,9},{5,13},{9,17},{1... | collective-permute-start | bytes 2359304 | tf_op jit(solution)/shard_map/ppermute | solution.py:65
  623.5 37.8 %collective-permute-start.78 = (bf16[256,384]{1,0:T(8,128)(2,1)S(1)}, bf16[256,384]{1,0:T(8,128)(2,1)}, u32[]{:S(2)}, u32[]{:S(2)}) collective-permute-start(bf16[256,384]{1,0:T(8,128)(2,1)S(1)} %copy-done.114), channel_id=1, source_target_pairs={{0,16},{4,20},{8,24},{12,28},{16,0},{20,4},{24,8},{28,12},{1,17},{... | collective-permute-start | bytes 589832 | tf_op jit(solution)/shard_map/ppermute | solution.py:65
  626.4 38.5 %collective-permute-start.79 = (bf16[256,384]{1,0:T(8,128)(2,1)}, bf16[256,384]{1,0:T(8,128)(2,1)}, u32[]{:S(2)}, u32[]{:S(2)}) collective-permute-start(bf16[256,384]{1,0:T(8,128)(2,1)} %get-tuple-element.429), channel_id=1, source_target_pairs={{0,16},{4,20},{8,24},{12,28},{16,0},{20,4},{24,8},{28,12},{1,17},{... | collective-permute-start | bytes 589832 | tf_op jit(solution)/shard_map/ppermute | solution.py:65
  707.5 32.8 %collective-permute-start.84 = (bf16[2,2,256,384]{3,2,0,1:T(8,128)(2,1)S(1)}, bf16[2,2,256,384]{3,2,0,1:T(8,128)(2,1)S(1)}, u32[]{:S(2)}, u32[]{:S(2)}) collective-permute-start(bf16[2,2,256,384]{3,2,0,1:T(8,128)(2,1)S(1)} %pad_maximum_fusion.15), channel_id=1, source_target_pairs={{0,4},{4,0},{8,12},{12,8},{16,20},{20,16},{24,28},{28,24},{1,5},{5... | collective-permute-start | bytes 2359304 | tf_op jit(solution)/shard_map/ppermute | solution.py:65
  708.7 31.6 %collective-permute-start.85 = (bf16[2,2,256,384]{3,2,0,1:T(8,128)(2,1)S(1)}, bf16[2,2,256,384]{3,2,0,1:T(8,128)(2,1)S(1)}, u32[]{:S(2)}, u32[]{:S(2)}) collective-permute-start(bf16[2,2,256,384]{3,2,0,1:T(8,128)(2,1)S(1)} %pad_maximum_fusion.16), channel_id=1, source_target_pairs={{0,8},{4,12},{8,0},{12,4},{16,24},{20,28},{24,16},{28,20},{1,9},{5... | collective-permute-start | bytes 2359304 | tf_op jit(solution)/shard_map/ppermute | solution.py:65
  708.7 30.7 %collective-permute-start.86 = (bf16[2,2,192,384]{3,2,0,1:T(8,128)(2,1)S(1)}, bf16[2,2,192,384]{3,2,0,1:T(8,128)(2,1)S(1)}, u32[]{:S(2)}, u32[]{:S(2)}) collective-permute-start(bf16[2,2,192,384]{3,2,0,1:T(8,128)(2,1)S(1)} %select_bitcast_fusion.7), channel_id=1, source_target_pairs={{0,4},{4,0},{8,12},{12,8},{16,20},{20,16},{24,28},{28,24},{1,5},{5... | collective-permute-start | bytes 1769480 | tf_op jit(solution)/shard_map/ppermute | solution.py:65
  742.7 28.6 %collective-permute-start.91 = (bf16[2,192,384]{2,1,0:T(8,128)(2,1)S(1)}, bf16[2,192,384]{2,1,0:T(8,128)(2,1)S(1)}, u32[]{:S(2)}, u32[]{:S(2)}) collective-permute-start(bf16[2,192,384]{2,1,0:T(8,128)(2,1)S(1)} %fusion.55), channel_id=1, source_target_pairs={{0,8},{4,12},{8,0},{12,4},{16,24},{20,28},{24,16},{28,20},{1,9},{5... | collective-permute-start | bytes 884744 | tf_op jit(solution)/shard_map/ppermute | solution.py:65
  789.1 28.8 %collective-permute-start.103 = (bf16[2,2,64,512]{3,2,0,1:T(8,128)(2,1)S(1)}, bf16[2,2,64,512]{3,2,0,1:T(8,128)(2,1)S(1)}, u32[]{:S(2)}, u32[]{:S(2)}) collective-permute-start(bf16[2,2,64,512]{3,2,0,1:T(8,128)(2,1)S(1)} %select_bitcast_fusion.16), channel_id=1, source_target_pairs={{0,4},{4,0},{8,12},{12,8},{16,20},{20,16},{24,28},{28,24},{1,5},{5... | collective-permute-start | bytes 786440 | tf_op jit(solution)/shard_map/ppermute | solution.py:65
  (242 other events, 2692.7 us)
Sparse Core Ops, SparseCore 0:
  10.2 85.5 all-gather.2
  98.0 182.1 all-gather.4
  424.0 216.1 reduce-scatter.1

commit v3 on v2

--- a/solution.py
+++ b/solution.py
@@ -168,6 +168,13 @@
             [jnp.where(high, other, value), jnp.where(high, value, other)], axis=0
         )
         bit *= 2
+    return value
+
+
+def chain_sum(value, axis):
+    for bit in all_bits(lax.axis_size(axis)):
+        (other,) = yield [(value, axis, swap_pairs(axis, bit))]
+        value = value + other
     return value
 
 
@@ -853,11 +860,7 @@
         text_return, self_return, work=query_backward
     )
 
-    def blocks(value):
-        return value.reshape(dp_count, shard, local_width)
-
-    query_sum = Chain(scatter_blocks([blocks(grad_query_weight), blocks(grad_proj)], dp_index))
-    links.stage(text_return, self_return, query_sum)
+    links.stage(text_return, self_return)
     own_text = text_return.result
 
     def text_rows_backward(tie):
@@ -874,7 +877,7 @@
     text_back = Chain(
         gather_blocks([grad_text_low[:, :local_width], grad_text_low[:, local_width:]], dp_index)
     )
-    links.finish_only(self_return, (query_sum, text_back))
+    links.finish_only(self_return, (text_back,))
     own_self, ffn_sum = lax.optimization_barrier((self_return.result, ffn_sum))
 
     def key_backward(tie):
@@ -891,18 +894,31 @@
         first_part = mm(grad_query_low, qkv_full[:, :local_width], NT) + mm(
             grad_key_low, qkv_full[:, local_width:], NT
         )
-        return head_key, mm(first_low, grad_key_low, TN).astype(BF), first_part.astype(BF)
-
-    head_key, grad_key_weight, first_part = links.stage(query_sum, text_back, work=key_backward)
-    key_sum = Chain(
-        scatter_blocks(
-            [blocks(grad_key_weight[:, :local_width]), blocks(grad_key_weight[:, local_width:])],
-            dp_index,
-        )
-    )
-    grad_first = links.stage(
-        query_sum, text_back, key_sum, work=lambda tie: sum_to_mp(tie(first_part))
-    )
+        return grad_key_low, head_key, first_part.astype(BF)
+
+    def blocks(value):
+        return value.reshape(dp_count, shard, local_width)
+
+    def sum_rows(tie):
+        first_blocks = [first_part[k * row_count : (k + 1) * row_count] for k in range(mp_count)]
+        moved = swap(first_blocks[3], "mp", 1)
+        far_rows = plus(first_blocks[2], moved).astype(BF)
+        grad_first = plus(first_blocks[0], swap(first_blocks[1], "mp", 1), swap(far_rows, "mp", 2))
+        grad_keys = mm(first_low, after(grad_key_low, far_rows), TN).astype(BF)
+        terms = [
+            grad_query_weight,
+            grad_keys[:, :local_width],
+            grad_keys[:, local_width:],
+            grad_proj,
+        ]
+        terms = jnp.stack([blocks(term) for term in terms], axis=1)
+        attn_terms.append(terms.reshape(-1, shard, local_width))
+        return grad_first
+
+    grad_key_low, head_key, first_part = links.stage(text_back, work=key_backward)
+    attn_terms = []
+    grad_first = links.stage(text_back, work=sum_rows)
+    attn_sum = lax.psum_scatter(attn_terms[0], "dp", scatter_dimension=0, tiled=True)
     grad_act_b, grad_gain_one, grad_scale_attn = first_pull(grad_first)
     grad_tokens = grad_act_a + grad_act_b
     mod_grads = jnp.stack([grad_scale_attn, grad_gate_attn, grad_scale_ffn, grad_gate_ffn])
@@ -915,16 +931,12 @@
         grad_mod_low = jnp.sum(jnp.where(mine, mod_sum, 0.0), axis=0)[None].astype(BF)
         return grad_mod_low, gather_in_order(grad_mod_low, "dp", dp_index)
 
-    def caption_rows(tie):
-        part = mm(tie(text_rows), text_matrix, NT).astype(BF)
-        part = part.reshape(dp_count, mp_count, quarter_rows, text_shard)
-        part = jnp.transpose(part, (1, 0, 2, 3)).reshape(-1, text_shard)
-        return sum_to_mp(part).astype(BF).reshape(dp_count, quarter_rows, text_shard)
-
+    caption_part = mm(text_rows, text_matrix, NT).astype(BF)
+    caption_part = caption_part.reshape(dp_count, mp_count, quarter_rows, text_shard)
+    caption_part = jnp.transpose(caption_part, (1, 0, 2, 3)).reshape(-1, text_shard)
     (grad_mod_low, grad_mod_all), caption_mine = links.stage(
-        query_sum, key_sum, work=lambda tie: (gather_mod_grads(tie), caption_rows(tie))
-    )
-    caption_back = Chain(exchange_blocks(caption_mine, dp_index))
+        work=lambda tie: (gather_mod_grads(tie), sum_to_mp(caption_part).astype(BF))
+    )
 
     row_grads = jnp.stack([grad_gain_one, grad_gain_two, grad_gain_three, grad_gain_four])
     grad_ada = mm(cond_mine, grad_mod_all, TN) * weight_scale
@@ -944,26 +956,42 @@
     gate_row = lax.dynamic_update_slice_in_dim(
         zeros((1, width)), gate_local[None], mp_index * local_heads, 1
     )
-    small = jnp.concatenate([row_grads, head_rows, bias_rows, gate_row, cond_rows], axis=0)
-    small = links.stage(
-        query_sum, key_sum, caption_back, work=lambda tie: sum_all(sum_all(tie(small), "mp"), "dp")
-    )
-    links.finish(query_sum, key_sum, caption_back)
-    columns = jnp.transpose(caption_back.result, (1, 0, 2)).reshape(quarter_rows, text_dim)
+    parts = [row_grads, head_rows, bias_rows, gate_row, cond_rows]
+    count = sum(part.shape[0] for part in parts)
+    small, start = 0.0, 0
+    for part in parts:
+        end = start + part.shape[0]
+        small = small + jnp.pad(part, ((start, count - end), (0, 0)))
+        start = end
     block = text_dim // mp_count
+
+    def sum_small():
+        value = yield from chain_sum(small, "mp")
+        return (yield from chain_sum(value, "dp"))
+
+    def send_captions():
+        columns = yield from exchange_blocks(
+            caption_mine.reshape(dp_count, quarter_rows, text_shard), dp_index
+        )
+        columns = jnp.transpose(columns, (1, 0, 2)).reshape(quarter_rows, text_dim)
+        pieces = [
+            lax.dynamic_slice_in_dim(columns, (mp_index ^ k) * block, block, axis=1)
+            for k in range(mp_count)
+        ]
+        moved = yield [(pieces[k], "mp", swap_pairs("mp", k)) for k in range(1, mp_count)]
+        return [pieces[0]] + list(moved)
+
+    small_chain, caption_back = Chain(sum_small()), Chain(send_captions())
+    links.finish(small_chain, caption_back)
+    small = small_chain.result
     grad_caption = jnp.zeros((text_len, block), F32)
-    for bit in range(mp_count):
-        other = mp_index ^ bit
-        piece = lax.dynamic_slice_in_dim(columns, other * block, block, axis=1)
-        if bit:
-            piece = swap(piece, "mp", bit)
+    for k, piece in enumerate(caption_back.result):
         grad_caption = lax.dynamic_update_slice_in_dim(
-            grad_caption, piece.astype(F32), other * quarter_rows, 0
+            grad_caption, piece.astype(F32), (mp_index ^ k) * quarter_rows, 0
         )
     grad_text = mm(text_all, text_rows, TN) * weight_scale
     ffn_sum = ffn_sum.astype(F32) * weight_scale
-    query_sum, proj_sum = [value * weight_scale for value in query_sum.result]
-    key_sum, value_sum = [value * weight_scale for value in key_sum.result]
+    attn_sum = attn_sum.astype(F32) * weight_scale
     cond_width = width // mp_count
     cond_sum = lax.dynamic_slice(small[12:], (dp_index, mp_index * cond_width), (1, cond_width))
     cond_cols = lax.dynamic_slice_in_dim(condition, mp_index * cond_width, cond_width, axis=1)
@@ -979,8 +1007,8 @@
         grad_tokens,
         grad_caption[None],
         grad_condition,
-        jnp.stack([query_sum, key_sum, value_sum]),
-        proj_sum.T,
+        attn_sum[:3],
+        attn_sum[3].T,
         parted(grad_text, 2),
         parted(ffn_sum[:, : 2 * units], 2),
         ffn_sum[:, 2 * units :].T,

time: 866 us -> 826 us (0.954)
  waiting for transfers between devices: 421 us -> 363 us
  Pallas kernels: 61.1 us -> 74.8 us
    ppermute x77 -> x73, waiting for transfers between devices: 316 us -> 287 us  [stage(): lax.ppermute(value, axis, pairs)]
    ppermute x37 -> x29, waiting for transfers between devices: 104 us -> 76 us  [swap(): return lax.ppermute(value, axis, [(i, i ^ bit) for i in range(count)])]
    pallas_call x4, Pallas kernels: 44 us -> 57.7 us  [attend(): pl.pallas_call(kernel, grid=(width // PAIR,), in_specs=[smem] * len(scala...]
    ppermute x37 -> x29, starting transfers between devices: 26.2 us -> 19.9 us  [swap(): return lax.ppermute(value, axis, [(i, i ^ bit) for i in range(count)])]
    ppermute x77 -> x73, starting transfers between devices: 108 us -> 111 us  [stage(): lax.ppermute(value, axis, pairs)]
    unnamed x322 -> x336, local copies, waits for them, and re-layouts: 19.7 us -> 17.7 us
  transfers between devices with their start and end apart: 117 -> 106, of which waited for: 59 -> 52; matrix products, arithmetic and copies ran while one was open for 20% -> 22% of each run, Pallas kernels for 7% -> 9%
where the time goes in v3:
time: 826 us; the launch traced here: 813 us
  waiting for transfers between devices  363 us (44%)
  starting transfers between devices  131 us (16%)
  other arithmetic  97.4 us (12%)
  Pallas kernels  74.8 us (9%)
  matrix products  69 us (8%)
  local copies, waits for them, and re-layouts  58.7 us (7%)
  between operations  19 us (2%)
    ppermute x73, waiting for transfers between devices, stage(): lax.ppermute(value, axis, pairs)  287 us
    ppermute x73, starting transfers between devices, stage(): lax.ppermute(value, axis, pairs)  111 us
    ppermute x29, waiting for transfers between devices, swap(): return lax.ppermute(value, axis, [(i, i ^ bit) for i in range(count)])  76 us
    dot_general x32, matrix products, mm(): return lax.dot_general(left, right, dims, preferred_element_type=F32)  69 us
    pallas_call x4, Pallas kernels, attend(): pl.pallas_call(kernel, grid=(width // PAIR,), in_specs=[smem] * len(scala...  57.7 us
    ppermute x29, starting transfers between devices, swap(): return lax.ppermute(value, axis, [(i, i ^ bit) for i in range(count)])  19.9 us
    unnamed x336, local copies, waits for them, and re-layouts  17.7 us
  transfers between devices with their start and end apart: 106, of which 52 were waited for; matrix products, arithmetic and copies ran while one was open for 22% of the time, Pallas kernels for 9%

profile of v3, /device:TPU:0, one launch (start us, length us, event | category | flops | bytes accessed | tf_op | source)
XLA Modules:
  0.0 812.9 jit_solution(10189649674959783563)
XLA Ops:
  46.8 11.8 %collective-permute-done.6 = bf16[2,2,64,512]{3,2,1,0:T(8,128)(2,1)S(1)} collective-permute-done((bf16[2,2,64,512]{3,2,1,0:T(8,128)(2,1)S(1)}, bf16[2,2,64,512]{3,2,1,0:T(8,128)(2,1)S(1)}, u32[]{:S(2)}, u32[]{:S(2)}) %collective-permute-start.6) | collective-permute-done | bytes 262176 | tf_op jit(solution)/shard_map/ppermute | solution.py:65
  59.9 22.1 %collective-permute-done.8 = bf16[128,1536]{1,0:T(8,128)(2,1)} collective-permute-done((bf16[128,1536]{1,0:T(8,128)(2,1)}, bf16[128,1536]{1,0:T(8,128)(2,1)}, u32[]{:S(2)}, u32[]{:S(2)}) %collective-permute-start.8) | collective-permute-done | bytes 393248 | tf_op jit(solution)/shard_map/ppermute | solution.py:65
  90.3 8.3 %collective-permute-done.10 = bf16[2,2,64,512]{3,2,1,0:T(8,128)(2,1)S(1)} collective-permute-done((bf16[2,2,64,512]{3,2,1,0:T(8,128)(2,1)S(1)}, bf16[2,2,64,512]{3,2,1,0:T(8,128)(2,1)S(1)}, u32[]{:S(2)}, u32[]{:S(2)}) %collective-permute-start.10) | collective-permute-done | bytes 262176 | tf_op jit(solution)/shard_map/ppermute | solution.py:65
  119.7 5.9 collective-permute-done.15
  130.1 5.8 collective-permute-done.17
  153.7 8.6 %sine_multiply_fusion = (f32[3584,128]{1,0:T(8,128)}, f32[3584,128]{1,0:T(8,128)}) fusion(f32[128]{0:T(128)S(1)} %copy-done.147, f32[128]{0:T(128)S(1)} %copy-done.148, s32[3584]{0:T(1024)S(1)} %copy-done.121, s32[3584]{0:T(1024)S(1)} %copy-done.122, pred[128]{0:T(512)(128)(4,1)S(1)} %copy-done.149), kind=kLoop, calls=%fused_computation.40 | loop fusion | flops 1835008 | bytes 3699840 | tf_op jit(solution)/shard_map/mul | solution.py:704
  166.4 9.5 %collective-permute-done.20 = bf16[2,2,256,384]{3,2,0,1:T(8,128)(2,1)} collective-permute-done((bf16[2,2,256,384]{3,2,0,1:T(8,128)(2,1)}, bf16[2,2,256,384]{3,2,0,1:T(8,128)(2,1)}, u32[]{:S(2)}, u32[]{:S(2)}) %collective-permute-start.20) | collective-permute-done | bytes 786464 | tf_op jit(solution)/shard_map/ppermute | solution.py:65
  176.0 21.3 %collective-permute-done.21 = bf16[2,2,256,384]{3,2,0,1:T(8,128)(2,1)S(1)} collective-permute-done((bf16[2,2,256,384]{3,2,0,1:T(8,128)(2,1)}, bf16[2,2,256,384]{3,2,0,1:T(8,128)(2,1)S(1)}, u32[]{:S(2)}, u32[]{:S(2)}) %collective-permute-start.21) | collective-permute-done | bytes 786464 | tf_op jit(solution)/shard_map/ppermute | solution.py:65
  206.8 19.0 %collective-permute-done.26 = bf16[2,256,384]{2,1,0:T(8,128)(2,1)} collective-permute-done((bf16[2,256,384]{2,1,0:T(8,128)(2,1)S(1)}, bf16[2,256,384]{2,1,0:T(8,128)(2,1)}, u32[]{:S(2)}, u32[]{:S(2)}) %collective-permute-start.26) | collective-permute-done | bytes 393248 | tf_op jit(solution)/shard_map/ppermute | solution.py:65
  265.2 12.0 %collective-permute-done.33 = bf16[256,384]{1,0:T(8,128)(2,1)} collective-permute-done((bf16[256,384]{1,0:T(8,128)(2,1)}, bf16[256,384]{1,0:T(8,128)(2,1)}, u32[]{:S(2)}, u32[]{:S(2)}) %collective-permute-start.33) | collective-permute-done | bytes 196640 | tf_op jit(solution)/shard_map/ppermute | solution.py:65
  316.6 10.1 %shard_map.295 = (f32[512,384]{1,0:T(8,128)}, f32[512,384]{1,0:T(8,128)}) custom-call(s32[7]{0:T(128)} %and_convert_fusion.live_ref, bf16[512,384]{1,0:T(8,128)(2,1)} %slice.353.query_ref, bf16[1024,384]{1,0:T(8,128)(2,1)} %slice.358.own_ref, bf16[2048,384]{1,0:T(8,128)(2,1)} %copy-done.13, bf16[2048,384]{1,0:T(8,128)(2,1)} %copy-done.14, ...), custom_call_target="tpu_custom_call" | custom-call | flops 3221225472 | bytes 7864320 | tf_op jit(solution)/shard_map/pallas_call | solution.py:557
  327.5 7.9 shard_map.296
  341.5 9.7 %collective-permute-done.46 = bf16[128,1536]{1,0:T(8,128)(2,1)S(1)} collective-permute-done((bf16[128,1536]{1,0:T(8,128)(2,1)S(1)}, bf16[128,1536]{1,0:T(8,128)(2,1)S(1)}, u32[]{:S(2)}, u32[]{:S(2)}) %collective-permute-start.46) | collective-permute-done | bytes 393248 | tf_op jit(solution)/shard_map/ppermute | solution.py:31
  355.4 8.9 %collective-permute-done.48 = bf16[128,1536]{1,0:T(8,128)(2,1)S(1)} collective-permute-done((bf16[128,1536]{1,0:T(8,128)(2,1)S(1)}, bf16[128,1536]{1,0:T(8,128)(2,1)S(1)}, u32[]{:S(2)}, u32[]{:S(2)}) %collective-permute-start.48) | collective-permute-done | bytes 393248 | tf_op jit(solution)/shard_map/ppermute | solution.py:31
  375.4 9.7 %collective-permute-done.52 = bf16[128,1536]{1,0:T(8,128)(2,1)S(1)} collective-permute-done((bf16[128,1536]{1,0:T(8,128)(2,1)S(1)}, bf16[128,1536]{1,0:T(8,128)(2,1)S(1)}, u32[]{:S(2)}, u32[]{:S(2)}) %collective-permute-start.52) | collective-permute-done | bytes 393248 | tf_op jit(solution)/shard_map/ppermute | solution.py:31
  388.8 8.9 %collective-permute-done.54 = bf16[128,1536]{1,0:T(8,128)(2,1)S(1)} collective-permute-done((bf16[128,1536]{1,0:T(8,128)(2,1)S(1)}, bf16[128,1536]{1,0:T(8,128)(2,1)S(1)}, u32[]{:S(2)}, u32[]{:S(2)}) %collective-permute-start.54) | collective-permute-done | bytes 393248 | tf_op jit(solution)/shard_map/ppermute | solution.py:31
  406.7 5.3 convolution_convert_fusion
  420.8 5.4 collective-permute-done.58
  437.6 9.2 %collective-permute-done.60 = bf16[128,1536]{1,0:T(8,128)(2,1)} collective-permute-done((bf16[128,1536]{1,0:T(8,128)(2,1)}, bf16[128,1536]{1,0:T(8,128)(2,1)}, u32[]{:S(2)}, u32[]{:S(2)}) %collective-permute-start.60) | collective-permute-done | bytes 393248 | tf_op jit(solution)/shard_map/ppermute | solution.py:31
  453.3 15.3 %shard_map.297 = (bf16[512,384]{1,0:T(8,128)(2,1)}, bf16[512,384]{1,0:T(8,128)(2,1)}, bf16[512,384]{1,0:T(8,128)(2,1)}, bf16[512,384]{1,0:T(8,128)(2,1)}, bf16[5...) custom-call(s32[7]{0:T(128)} %and_convert_fusion.live_ref, ...), custom_call_target="tpu_custom_call" | custom-call | flops 4026531840 | bytes 7864320 | tf_op jit(solution)/shard_map/pallas_call | solution.py:557
  470.0 24.4 %shard_map.298 = (bf16[1024,384]{1,0:T(8,128)(2,1)}, bf16[1024,384]{1,0:T(8,128)(2,1)}, bf16[1024,384]{1,0:T(8,128)(2,1)}, bf16[1024,384]{1,0:T(8,128)(2,1)}, bf...) custom-call(s32[7]{0:T(128)} %and_convert_fusion.live_ref, ...), custom_call_target="tpu_custom_call" | custom-call | flops 8053063680 | bytes 7864320 | tf_op jit(solution)/shard_map/pallas_call | solution.py:557
  494.5 7.8 collective-permute-done.62
  503.8 13.0 %collective-permute-start.63 = (bf16[512,384]{1,0:T(8,128)(2,1)S(1)}, bf16[512,384]{1,0:T(8,128)(2,1)S(1)}, u32[]{:S(2)}, u32[]{:S(2)}) collective-permute-start(bf16[512,384]{1,0:T(8,128)(2,1)S(1)} %add_convert_fusion.8), channel_id=1, source_target_pairs={{0,4},{4,0},{8,12},{12,8},{16,20},{20,16},{24,28},{28,24},{1,5},{5... | collective-permute-start | bytes 1179656 | tf_op jit(solution)/shard_map/ppermute | solution.py:65
  525.9 5.7 collective-permute-done.63
  531.6 12.6 %collective-permute-done.65 = bf16[1024,384]{1,0:T(8,128)(2,1)S(1)} collective-permute-done((bf16[1024,384]{1,0:T(8,128)(2,1)}, bf16[1024,384]{1,0:T(8,128)(2,1)S(1)}, u32[]{:S(2)}, u32[]{:S(2)}) %collective-permute-start.65) | collective-permute-done | bytes 786464 | tf_op jit(solution)/shard_map/ppermute | solution.py:65
  555.5 27.6 %collective-permute-done.66 = bf16[512,384]{1,0:T(8,128)(2,1)S(1)} collective-permute-done((bf16[512,384]{1,0:T(8,128)(2,1)S(1)}, bf16[512,384]{1,0:T(8,128)(2,1)S(1)}, u32[]{:S(2)}, u32[]{:S(2)}) %collective-permute-start.66) | collective-permute-done | bytes 393248 | tf_op jit(solution)/shard_map/ppermute | solution.py:65
  591.1 5.9 collective-permute-start.73
  605.5 52.3 %collective-permute-done.74 = bf16[256,384]{1,0:T(8,128)(2,1)} collective-permute-done((bf16[256,384]{1,0:T(8,128)(2,1)S(1)}, bf16[256,384]{1,0:T(8,128)(2,1)}, u32[]{:S(2)}, u32[]{:S(2)}) %collective-permute-start.74) | collective-permute-done | bytes 196640 | tf_op jit(solution)/shard_map/ppermute | solution.py:65
  722.4 8.0 collective-permute-done.90
  742.7 7.4 collective-permute-done.92
  774.5 8.6 %collective-permute-done.97 = f32[20,1536]{1,0:T(8,128)S(1)} collective-permute-done((f32[20,1536]{1,0:T(8,128)S(1)}, f32[20,1536]{1,0:T(8,128)S(1)}, u32[]{:S(2)}, u32[]{:S(2)}) %collective-permute-start.97) | collective-permute-done | bytes 122912 | tf_op jit(solution)/shard_map/ppermute | solution.py:65
  784.6 15.0 %collective-permute-done.101 = f32[20,1536]{1,0:T(8,128)S(1)} collective-permute-done((f32[20,1536]{1,0:T(8,128)S(1)}, f32[20,1536]{1,0:T(8,128)S(1)}, u32[]{:S(2)}, u32[]{:S(2)}) %collective-permute-start.101) | collective-permute-done | bytes 122912 | tf_op jit(solution)/shard_map/ppermute | solution.py:65
  (789 shorter events, 390.9 us)
Async XLA Ops:
  7.2 236.0 %all-gather.3.cloned.1.call-start = ((), (), s32[]{:S(2)}) async-start(), calls=%async_computation.2 | async-start | bytes 3981312 | tf_op jit(solution)/shard_map/all_gather | solution.py:615
  9.2 326.1 %all-gather.5.cloned.1.call-start = ((), (), s32[]{:S(2)}) async-start(), calls=%async_computation.3 | async-start | bytes 11943936 | tf_op jit(solution)/shard_map/all_gather | solution.py:616
  9.3 28.7 %collective-permute-start.2 = (bf16[128,1536]{1,0:T(8,128)(2,1)}, bf16[128,1536]{1,0:T(8,128)(2,1)}, u32[]{:S(2)}, u32[]{:S(2)}) collective-permute-start(bf16[128,1536]{1,0:T(8,128)(2,1)} %param.19), channel_id=1, source_target_pairs={{0,4},{4,0},{8,12},{12,8},{16,20},{20,16},{24,28},{28,24},{1,5},{5... | collective-permute-start | bytes 1179656 | tf_op jit(solution)/shard_map/ppermute | solution.py:65
  12.3 25.7 %collective-permute-start.3 = (bf16[128,1536]{1,0:T(8,128)(2,1)}, bf16[128,1536]{1,0:T(8,128)(2,1)S(1)}, u32[]{:S(2)}, u32[]{:S(2)}) collective-permute-start(bf16[128,1536]{1,0:T(8,128)(2,1)} %param.19), channel_id=1, source_target_pairs={{0,8},{4,12},{8,16},{12,20},{16,24},{20,28},{1,9},{5,13},{9,17},{1... | collective-permute-start | bytes 1179656 | tf_op jit(solution)/shard_map/ppermute | solution.py:65
  23.0 646.0 %reduce-scatter.3.cloned.1.call-start = ((), (), s32[]{:S(2)}) async-start(), calls=%async_computation.4 | async-start | bytes 10616832 | tf_op jit(solution)/shard_map/reduce_scatter | solution.py:800
  45.5 36.6 %collective-permute-start.8 = (bf16[128,1536]{1,0:T(8,128)(2,1)}, bf16[128,1536]{1,0:T(8,128)(2,1)}, u32[]{:S(2)}, u32[]{:S(2)}) collective-permute-start(bf16[128,1536]{1,0:T(8,128)(2,1)} %collective-permute-done.2), channel_id=1, source_target_pairs={{8,0},{16,8},{24,16},{4,12},{12,20},{20,28},{9,1},{17,9},{25,17},{... | collective-permute-start | bytes 1179656 | tf_op jit(solution)/shard_map/ppermute | solution.py:65
  146.8 29.2 %collective-permute-start.20 = (bf16[2,2,256,384]{3,2,0,1:T(8,128)(2,1)}, bf16[2,2,256,384]{3,2,0,1:T(8,128)(2,1)}, u32[]{:S(2)}, u32[]{:S(2)}) collective-permute-start(bf16[2,2,256,384]{3,2,0,1:T(8,128)(2,1)} %select_bitcast_fusion.5), channel_id=1, source_target_pairs={{0,4},{4,0},{8,12},{12,8},{16,20},{20,16},{24,28},{28,24},{1,5},{5... | collective-permute-start | bytes 2359304 | tf_op jit(solution)/shard_map/ppermute | solution.py:65
  151.7 45.6 %collective-permute-start.21 = (bf16[2,2,256,384]{3,2,0,1:T(8,128)(2,1)}, bf16[2,2,256,384]{3,2,0,1:T(8,128)(2,1)S(1)}, u32[]{:S(2)}, u32[]{:S(2)}) collective-permute-start(bf16[2,2,256,384]{3,2,0,1:T(8,128)(2,1)} %select_bitcast_fusion.4), channel_id=1, source_target_pairs={{0,8},{4,12},{8,0},{12,4},{16,24},{20,28},{24,16},{28,20},{1,9},{5... | collective-permute-start | bytes 2359304 | tf_op jit(solution)/shard_map/ppermute | solution.py:65
  153.1 44.1 %collective-permute-start.24 = (bf16[256,1536]{1,0:T(8,128)(2,1)S(1)}, bf16[256,1536]{1,0:T(8,128)(2,1)}, u32[]{:S(2)}, u32[]{:S(2)}) collective-permute-start(bf16[256,1536]{1,0:T(8,128)(2,1)S(1)} %bitcast.352), channel_id=1, source_target_pairs={{0,2},{1,3},{2,0},{3,1},{4,6},{5,7},{6,4},{7,5},{8,10},{9,11},{10,... | collective-permute-start | bytes 2359304 | tf_op jit(solution)/shard_map/ppermute | solution.py:65
  153.7 44.5 %collective-permute-start.25 = (bf16[256,1536]{1,0:T(8,128)(2,1)S(1)}, bf16[256,1536]{1,0:T(8,128)(2,1)}, u32[]{:S(2)}, u32[]{:S(2)}) collective-permute-start(bf16[256,1536]{1,0:T(8,128)(2,1)S(1)} %bitcast.353), channel_id=1, source_target_pairs={{0,1},{1,0},{2,3},{3,2},{4,5},{5,4},{6,7},{7,6},{8,9},{9,8},{10,11... | collective-permute-start | bytes 2359304 | tf_op jit(solution)/shard_map/ppermute | solution.py:65
  202.0 29.8 %collective-permute-start.29 = (bf16[256,1536]{1,0:T(8,128)(2,1)}, bf16[256,1536]{1,0:T(8,128)(2,1)}, u32[]{:S(2)}, u32[]{:S(2)}) collective-permute-start(bf16[256,1536]{1,0:T(8,128)(2,1)} %collective-permute-done.24), channel_id=1, source_target_pairs={{0,1},{1,0},{2,3},{3,2},{4,5},{5,4},{6,7},{7,6},{8,9},{9,8},{10,11... | collective-permute-start | bytes 2359304 | tf_op jit(solution)/shard_map/ppermute | solution.py:65
  202.0 29.8 %collective-permute-start.30 = (bf16[256,1536]{1,0:T(8,128)(2,1)S(1)}, bf16[256,1536]{1,0:T(8,128)(2,1)}, u32[]{:S(2)}, u32[]{:S(2)}) collective-permute-start(bf16[256,1536]{1,0:T(8,128)(2,1)S(1)} %bitcast.349), channel_id=1, source_target_pairs={{0,2},{1,3},{2,0},{3,1},{4,6},{5,7},{6,4},{7,5},{8,10},{9,11},{10,... | collective-permute-start | bytes 2359304 | tf_op jit(solution)/shard_map/ppermute | solution.py:65
  203.0 28.8 %collective-permute-start.31 = (bf16[256,1536]{1,0:T(8,128)(2,1)S(1)}, bf16[256,1536]{1,0:T(8,128)(2,1)}, u32[]{:S(2)}, u32[]{:S(2)}) collective-permute-start(bf16[256,1536]{1,0:T(8,128)(2,1)S(1)} %bitcast.350), channel_id=1, source_target_pairs={{0,1},{1,0},{2,3},{3,2},{4,5},{5,4},{6,7},{7,6},{8,9},{9,8},{10,11... | collective-permute-start | bytes 2359304 | tf_op jit(solution)/shard_map/ppermute | solution.py:65
  236.1 29.1 %collective-permute-start.32 = (bf16[256,384]{1,0:T(8,128)(2,1)}, bf16[256,384]{1,0:T(8,128)(2,1)}, u32[]{:S(2)}, u32[]{:S(2)}) collective-permute-start(bf16[256,384]{1,0:T(8,128)(2,1)} %get-tuple-element.292), channel_id=1, source_target_pairs={{0,16},{4,20},{8,24},{12,28},{16,0},{20,4},{24,8},{28,12},{1,17},{... | collective-permute-start | bytes 589832 | tf_op jit(solution)/shard_map/ppermute | solution.py:65
  236.1 41.1 %collective-permute-start.33 = (bf16[256,384]{1,0:T(8,128)(2,1)}, bf16[256,384]{1,0:T(8,128)(2,1)}, u32[]{:S(2)}, u32[]{:S(2)}) collective-permute-start(bf16[256,384]{1,0:T(8,128)(2,1)} %get-tuple-element.293), channel_id=1, source_target_pairs={{0,16},{4,20},{8,24},{12,28},{16,0},{20,4},{24,8},{28,12},{1,17},{... | collective-permute-start | bytes 589832 | tf_op jit(solution)/shard_map/ppermute | solution.py:65
  239.0 38.2 %collective-permute-start.34 = (bf16[256,1536]{1,0:T(8,128)(2,1)}, bf16[256,1536]{1,0:T(8,128)(2,1)}, u32[]{:S(2)}, u32[]{:S(2)}) collective-permute-start(bf16[256,1536]{1,0:T(8,128)(2,1)} %collective-permute-done.30), channel_id=1, source_target_pairs={{0,1},{1,0},{2,3},{3,2},{4,5},{5,4},{6,7},{7,6},{8,9},{9,8},{10,11... | collective-permute-start | bytes 2359304 | tf_op jit(solution)/shard_map/ppermute | solution.py:65
  239.0 38.2 %collective-permute-start.35 = (bf16[256,1536]{1,0:T(8,128)(2,1)}, bf16[256,1536]{1,0:T(8,128)(2,1)}, u32[]{:S(2)}, u32[]{:S(2)}) collective-permute-start(bf16[256,1536]{1,0:T(8,128)(2,1)} %bitcast.57), channel_id=1, source_target_pairs={{0,2},{1,3},{2,0},{3,1},{4,6},{5,7},{6,4},{7,5},{8,10},{9,11},{10,... | collective-permute-start | bytes 2359304 | tf_op jit(solution)/shard_map/ppermute | solution.py:65
  240.4 36.8 %collective-permute-start.36 = (bf16[256,1536]{1,0:T(8,128)(2,1)}, bf16[256,1536]{1,0:T(8,128)(2,1)}, u32[]{:S(2)}, u32[]{:S(2)}) collective-permute-start(bf16[256,1536]{1,0:T(8,128)(2,1)} %bitcast.57), channel_id=1, source_target_pairs={{0,1},{1,0},{2,3},{3,2},{4,5},{5,4},{6,7},{7,6},{8,9},{9,8},{10,11... | collective-permute-start | bytes 2359304 | tf_op jit(solution)/shard_map/ppermute | solution.py:65
  428.5 374.9 %reduce-scatter.5.cloned.1.call-start = ((), (), s32[]{:S(2)}) async-start(), calls=%async_computation.5 | async-start | bytes 5308416 | tf_op jit(solution)/shard_map/reduce_scatter | solution.py:921
  468.6 33.7 %collective-permute-start.62 = (bf16[512,384]{1,0:T(8,128)(2,1)}, bf16[512,384]{1,0:T(8,128)(2,1)S(1)}, u32[]{:S(2)}, u32[]{:S(2)}) collective-permute-start(bf16[512,384]{1,0:T(8,128)(2,1)} %get-tuple-element.360), channel_id=1, source_target_pairs={{8,0},{16,8},{24,16},{4,12},{12,20},{20,28},{9,1},{17,9},{25,17},{... | collective-permute-start | bytes 1179656 | tf_op jit(solution)/shard_map/ppermute | solution.py:65
  502.4 41.8 %collective-permute-start.65 = (bf16[1024,384]{1,0:T(8,128)(2,1)}, bf16[1024,384]{1,0:T(8,128)(2,1)S(1)}, u32[]{:S(2)}, u32[]{:S(2)}) collective-permute-start(bf16[1024,384]{1,0:T(8,128)(2,1)} %get-tuple-element.379), channel_id=1, source_target_pairs={{8,0},{16,8},{24,16},{4,12},{12,20},{20,28},{9,1},{17,9},{25,17},{... | collective-permute-start | bytes 2359304 | tf_op jit(solution)/shard_map/ppermute | solution.py:65
  503.8 27.7 %collective-permute-start.63 = (bf16[512,384]{1,0:T(8,128)(2,1)S(1)}, bf16[512,384]{1,0:T(8,128)(2,1)S(1)}, u32[]{:S(2)}, u32[]{:S(2)}) collective-permute-start(bf16[512,384]{1,0:T(8,128)(2,1)S(1)} %add_convert_fusion.8), channel_id=1, source_target_pairs={{0,4},{4,0},{8,12},{12,8},{16,20},{20,16},{24,28},{28,24},{1,5},{5... | collective-permute-start | bytes 1179656 | tf_op jit(solution)/shard_map/ppermute | solution.py:65
  544.8 38.3 %collective-permute-start.69 = (bf16[1024,384]{1,0:T(8,128)(2,1)S(1)}, bf16[1024,384]{1,0:T(8,128)(2,1)S(1)}, u32[]{:S(2)}, u32[]{:S(2)}) collective-permute-start(bf16[1024,384]{1,0:T(8,128)(2,1)S(1)} %add_convert_fusion.3), channel_id=1, source_target_pairs={{0,4},{4,0},{8,12},{12,8},{16,20},{20,16},{24,28},{28,24},{1,5},{5... | collective-permute-start | bytes 2359304 | tf_op jit(solution)/shard_map/ppermute | solution.py:65
  545.5 37.6 %collective-permute-start.70 = (bf16[1024,384]{1,0:T(8,128)(2,1)S(1)}, bf16[1024,384]{1,0:T(8,128)(2,1)S(1)}, u32[]{:S(2)}, u32[]{:S(2)}) collective-permute-start(bf16[1024,384]{1,0:T(8,128)(2,1)S(1)} %copy-done.156), channel_id=1, source_target_pairs={{0,8},{8,16},{16,24},{12,4},{20,12},{28,20},{1,9},{9,17},{17,25},{... | collective-permute-start | bytes 2359304 | tf_op jit(solution)/shard_map/ppermute | solution.py:65
  549.5 33.5 %collective-permute-start.66 = (bf16[512,384]{1,0:T(8,128)(2,1)S(1)}, bf16[512,384]{1,0:T(8,128)(2,1)S(1)}, u32[]{:S(2)}, u32[]{:S(2)}) collective-permute-start(bf16[512,384]{1,0:T(8,128)(2,1)S(1)} %add_convert_fusion.7), channel_id=1, source_target_pairs={{0,4},{4,0},{8,12},{12,8},{16,20},{20,16},{24,28},{28,24},{1,5},{5... | collective-permute-start | bytes 1179656 | tf_op jit(solution)/shard_map/ppermute | solution.py:65
  549.6 33.5 %collective-permute-start.67 = (bf16[512,384]{1,0:T(8,128)(2,1)S(1)}, bf16[512,384]{1,0:T(8,128)(2,1)S(1)}, u32[]{:S(2)}, u32[]{:S(2)}) collective-permute-start(bf16[512,384]{1,0:T(8,128)(2,1)S(1)} %get-tuple-element.394), channel_id=1, source_target_pairs={{8,0},{12,4},{16,8},{20,12},{24,16},{28,20},{9,1},{13,5},{17,9},{2... | collective-permute-start | bytes 1179656 | tf_op jit(solution)/shard_map/ppermute | solution.py:65
  550.9 32.2 %collective-permute-start.68 = (bf16[512,384]{1,0:T(8,128)(2,1)S(1)}, bf16[512,384]{1,0:T(8,128)(2,1)S(1)}, u32[]{:S(2)}, u32[]{:S(2)}) collective-permute-start(bf16[512,384]{1,0:T(8,128)(2,1)S(1)} %get-tuple-element.395), channel_id=1, source_target_pairs={{0,8},{4,12},{8,16},{12,20},{16,24},{20,28},{1,9},{5,13},{9,17},{1... | collective-permute-start | bytes 1179656 | tf_op jit(solution)/shard_map/ppermute | solution.py:65
  587.3 74.2 %collective-permute-start.71 = (bf16[1024,384]{1,0:T(8,128)(2,1)}, bf16[1024,384]{1,0:T(8,128)(2,1)}, u32[]{:S(2)}, u32[]{:S(2)}) collective-permute-start(bf16[1024,384]{1,0:T(8,128)(2,1)} %add_convert_fusion.2), channel_id=1, source_target_pairs={{0,4},{4,0},{8,12},{12,8},{16,20},{20,16},{24,28},{28,24},{1,5},{5... | collective-permute-start | bytes 2359304 | tf_op jit(solution)/shard_map/ppermute | solution.py:65
  589.8 71.8 %collective-permute-start.72 = (bf16[1024,384]{1,0:T(8,128)(2,1)}, bf16[1024,384]{1,0:T(8,128)(2,1)}, u32[]{:S(2)}, u32[]{:S(2)}) collective-permute-start(bf16[1024,384]{1,0:T(8,128)(2,1)} %get-tuple-element.408), channel_id=1, source_target_pairs={{8,0},{12,4},{16,8},{20,12},{24,16},{28,20},{9,1},{13,5},{17,9},{2... | collective-permute-start | bytes 2359304 | tf_op jit(solution)/shard_map/ppermute | solution.py:65
  591.1 70.5 %collective-permute-start.73 = (bf16[1024,384]{1,0:T(8,128)(2,1)}, bf16[1024,384]{1,0:T(8,128)(2,1)}, u32[]{:S(2)}, u32[]{:S(2)}) collective-permute-start(bf16[1024,384]{1,0:T(8,128)(2,1)} %get-tuple-element.409), channel_id=1, source_target_pairs={{0,8},{4,12},{8,16},{12,20},{16,24},{20,28},{1,9},{5,13},{9,17},{1... | collective-permute-start | bytes 2359304 | tf_op jit(solution)/shard_map/ppermute | solution.py:65
  602.2 55.6 %collective-permute-start.74 = (bf16[256,384]{1,0:T(8,128)(2,1)S(1)}, bf16[256,384]{1,0:T(8,128)(2,1)}, u32[]{:S(2)}, u32[]{:S(2)}) collective-permute-start(bf16[256,384]{1,0:T(8,128)(2,1)S(1)} %get-tuple-element.410), channel_id=1, source_target_pairs={{0,16},{4,20},{8,24},{12,28},{16,0},{20,4},{24,8},{28,12},{1,17},{... | collective-permute-start | bytes 589832 | tf_op jit(solution)/shard_map/ppermute | solution.py:65
  605.2 56.3 %collective-permute-start.75 = (bf16[256,384]{1,0:T(8,128)(2,1)S(1)}, bf16[256,384]{1,0:T(8,128)(2,1)}, u32[]{:S(2)}, u32[]{:S(2)}) collective-permute-start(bf16[256,384]{1,0:T(8,128)(2,1)S(1)} %get-tuple-element.411), channel_id=1, source_target_pairs={{0,16},{4,20},{8,24},{12,28},{16,0},{20,4},{24,8},{28,12},{1,17},{... | collective-permute-start | bytes 589832 | tf_op jit(solution)/shard_map/ppermute | solution.py:65
  (239 other events, 2639.2 us)
Sparse Core Ops, SparseCore 0:
  10.2 85.5 all-gather.2
  98.0 181.7 all-gather.4
  428.6 223.6 reduce-scatter.2
  695.1 105.8 reduce-scatter.4

commit v4 on v3

--- a/solution.py
+++ b/solution.py
@@ -806,12 +806,24 @@
         work=lambda tie: rows_from_mp(tie(grad_attn_rows.astype(BF)))
     )
 
-    def text_backward(tie):
+    def self_backward(tie):
         grad_attn_low = mm(tie(grad_attn_all), proj_full, NN).astype(BF)
         return grad_attn_low, attend(
+            self_backward_kernel,
+            [live],
+            [query, grad_attn_low, out_self, log_self],
+            [],
+            self_sets,
+            [(2 * seq_len, BF)] * (near_sets + 1) + [(seq_len, F32)],
+            5,
+            1,
+        )
+
+    def text_backward(tie):
+        return attend(
             text_backward_kernel,
             [live, tanh_gate],
-            [query, grad_attn_low, out_text, log_text],
+            [query, tie(grad_attn_low), out_text, log_text],
             [bias.T],
             text_sets,
             [(2 * text_len, BF)] * len(text_sets) + [(seq_len, F32), (8, F32)],
@@ -819,23 +831,11 @@
             1,
         )
 
-    def self_backward(tie):
-        return attend(
-            self_backward_kernel,
-            [live],
-            [query, tie(grad_attn_low), out_self, log_self],
-            [],
-            self_sets,
-            [(2 * seq_len, BF)] * (near_sets + 1) + [(seq_len, F32)],
-            5,
-            1,
-        )
-
-    grad_attn_low, text_grads = links.stage(work=text_backward)
+    grad_attn_low, self_grads = links.stage(work=self_backward)
+    self_return = Chain(return_sets(self_grads[:-1], is_odd))
+    text_grads = links.stage(self_return, work=text_backward)
     gate_dots = text_grads[-1]
     text_return = Chain(return_sets(text_grads[: len(text_sets)], is_odd))
-    self_grads = links.stage(text_return, work=self_backward)
-    self_return = Chain(return_sets(self_grads[:-1], is_odd))
 
     def query_backward(tie):
         grad_query_low, head_query = whole(
@@ -861,24 +861,7 @@
     )
 
     links.stage(text_return, self_return)
-    own_text = text_return.result
-
-    def text_rows_backward(tie):
-        return whole(
-            text_back_kernel,
-            [((text_len, 2 * local_width), BF), ((8, local_width), F32)],
-            20 * text_len * 2 * local_width,
-            text_pre,
-            local_gains,
-            tie(own_text),
-        )
-
-    grad_text_low, head_text = text_rows_backward(lambda value: value)
-    text_back = Chain(
-        gather_blocks([grad_text_low[:, :local_width], grad_text_low[:, local_width:]], dp_index)
-    )
-    links.finish_only(self_return, (text_back,))
-    own_self, ffn_sum = lax.optimization_barrier((self_return.result, ffn_sum))
+    own_self = self_return.result
 
     def key_backward(tie):
         grad_key_low, head_key = whole(
@@ -915,28 +898,31 @@
         attn_terms.append(terms.reshape(-1, shard, local_width))
         return grad_first
 
-    grad_key_low, head_key, first_part = links.stage(text_back, work=key_backward)
+    grad_key_low, head_key, first_part = links.stage(text_return, work=key_backward)
+    grad_text_low, head_text = whole(
+        text_back_kernel,
+        [((text_len, 2 * local_width), BF), ((8, local_width), F32)],
+        20 * text_len * 2 * local_width,
+        text_pre,
+        local_gains,
+        text_return.result,
+    )
+    text_back = Chain(
+        gather_blocks([grad_text_low[:, :local_width], grad_text_low[:, local_width:]], dp_index)
+    )
     attn_terms = []
     grad_first = links.stage(text_back, work=sum_rows)
     attn_sum = lax.psum_scatter(attn_terms[0], "dp", scatter_dimension=0, tiled=True)
     grad_act_b, grad_gain_one, grad_scale_attn = first_pull(grad_first)
     grad_tokens = grad_act_a + grad_act_b
     mod_grads = jnp.stack([grad_scale_attn, grad_gate_attn, grad_scale_ffn, grad_gate_ffn])
-    links.finish(text_back)
-    text_rows = jnp.concatenate(text_back.result, axis=1)
-
     def gather_mod_grads(tie):
         mod_sum = sum_all(tie(mod_grads), "mp")
         mine = jnp.arange(mp_count)[:, None] == mp_index
         grad_mod_low = jnp.sum(jnp.where(mine, mod_sum, 0.0), axis=0)[None].astype(BF)
         return grad_mod_low, gather_in_order(grad_mod_low, "dp", dp_index)
 
-    caption_part = mm(text_rows, text_matrix, NT).astype(BF)
-    caption_part = caption_part.reshape(dp_count, mp_count, quarter_rows, text_shard)
-    caption_part = jnp.transpose(caption_part, (1, 0, 2, 3)).reshape(-1, text_shard)
-    (grad_mod_low, grad_mod_all), caption_mine = links.stage(
-        work=lambda tie: (gather_mod_grads(tie), sum_to_mp(caption_part).astype(BF))
-    )
+    grad_mod_low, grad_mod_all = links.stage(text_back, work=gather_mod_grads)
 
     row_grads = jnp.stack([grad_gain_one, grad_gain_two, grad_gain_three, grad_gain_four])
     grad_ada = mm(cond_mine, grad_mod_all, TN) * weight_scale
@@ -981,7 +967,19 @@
         moved = yield [(pieces[k], "mp", swap_pairs("mp", k)) for k in range(1, mp_count)]
         return [pieces[0]] + list(moved)
 
-    small_chain, caption_back = Chain(sum_small()), Chain(send_captions())
+    small_chain = Chain(sum_small())
+    links.stage(small_chain, text_back)
+    links.finish(text_back)
+    text_rows, ffn_sum = lax.optimization_barrier(
+        (jnp.concatenate(text_back.result, axis=1), ffn_sum)
+    )
+    caption_part = mm(text_rows, text_matrix, NT).astype(BF)
+    caption_part = caption_part.reshape(dp_count, mp_count, quarter_rows, text_shard)
+    caption_part = jnp.transpose(caption_part, (1, 0, 2, 3)).reshape(-1, text_shard)
+    caption_mine = links.stage(
+        small_chain, work=lambda tie: sum_to_mp(caption_part).astype(BF)
+    )
+    caption_back = Chain(send_captions())
     links.finish(small_chain, caption_back)
     small = small_chain.result
     grad_caption = jnp.zeros((text_len, block), F32)

time: 826 us -> 864 us (1.046)
  waiting for transfers between devices: 363 us -> 401 us
    ppermute x73, waiting for transfers between devices: 287 us -> 319 us  [stage(): lax.ppermute(value, axis, pairs)]
    reduce_scatter x1, waiting for transfers between devices: 0.01 us -> 13.5 us  [local(): lax.psum_scatter(attn_terms[0], 'dp', scatter_dimension=0, tiled=True)]
    unnamed x336 -> x324, local copies, waits for them, and re-layouts: 17.7 us -> 19.9 us
  transfers between devices with their start and end apart: 106 -> 106, of which waited for: 52 -> 54; matrix products, arithmetic and copies ran while one was open for 22% -> 21% of each run, Pallas kernels for 9% -> 9%
where the time goes in v4:
time: 864 us; the launch traced here: 854 us
  waiting for transfers between devices  401 us (46%)
  starting transfers between devices  136 us (16%)
  other arithmetic  92.2 us (11%)
  Pallas kernels  74.9 us (9%)
  matrix products  70 us (8%)
  local copies, waits for them, and re-layouts  59.9 us (7%)
  between operations  18.9 us (2%)
    ppermute x73, waiting for transfers between devices, stage(): lax.ppermute(value, axis, pairs)  319 us
    ppermute x73, starting transfers between devices, stage(): lax.ppermute(value, axis, pairs)  116 us
    dot_general x32, matrix products, mm(): return lax.dot_general(left, right, dims, preferred_element_type=F32)  70 us
    ppermute x29, waiting for transfers between devices, swap(): return lax.ppermute(value, axis, [(i, i ^ bit) for i in range(count)])  68.3 us
    pallas_call x4, Pallas kernels, attend(): pl.pallas_call(kernel, grid=(width // PAIR,), in_specs=[smem] * len(scala...  57.8 us
    unnamed x324, local copies, waits for them, and re-layouts  19.9 us
    ppermute x29, starting transfers between devices, swap(): return lax.ppermute(value, axis, [(i, i ^ bit) for i in range(count)])  19.9 us
  transfers between devices with their start and end apart: 106, of which 54 were waited for; matrix products, arithmetic and copies ran while one was open for 21% of the time, Pallas kernels for 9%

profile of v4, /device:TPU:0, one launch (start us, length us, event | category | flops | bytes accessed | tf_op | source)
XLA Modules:
  0.0 853.7 jit_solution(8218310491920243599)
XLA Ops:
  46.8 11.8 %collective-permute-done.6 = bf16[2,2,64,512]{3,2,1,0:T(8,128)(2,1)S(1)} collective-permute-done((bf16[2,2,64,512]{3,2,1,0:T(8,128)(2,1)S(1)}, bf16[2,2,64,512]{3,2,1,0:T(8,128)(2,1)S(1)}, u32[]{:S(2)}, u32[]{:S(2)}) %collective-permute-start.6) | collective-permute-done | bytes 262176 | tf_op jit(solution)/shard_map/ppermute | solution.py:65
  59.9 22.1 %collective-permute-done.8 = bf16[128,1536]{1,0:T(8,128)(2,1)} collective-permute-done((bf16[128,1536]{1,0:T(8,128)(2,1)}, bf16[128,1536]{1,0:T(8,128)(2,1)}, u32[]{:S(2)}, u32[]{:S(2)}) %collective-permute-start.8) | collective-permute-done | bytes 393248 | tf_op jit(solution)/shard_map/ppermute | solution.py:65
  90.3 8.3 collective-permute-done.10
  119.7 5.9 collective-permute-done.15
  130.1 5.8 collective-permute-done.17
  153.8 8.7 %sine_multiply_fusion = (f32[3584,128]{1,0:T(8,128)}, f32[3584,128]{1,0:T(8,128)}) fusion(f32[128]{0:T(128)S(1)} %copy-done.141, f32[128]{0:T(128)S(1)} %copy-done.142, s32[3584]{0:T(1024)S(1)} %copy-done.113, s32[3584]{0:T(1024)S(1)} %copy-done.114, pred[128]{0:T(512)(128)(4,1)S(1)} %copy-done.143), kind=kLoop, calls=%fused_computation.39 | loop fusion | flops 1835008 | bytes 3699840 | tf_op jit(solution)/shard_map/mul | solution.py:704
  166.5 9.6 %collective-permute-done.20 = bf16[2,2,256,384]{3,2,0,1:T(8,128)(2,1)} collective-permute-done((bf16[2,2,256,384]{3,2,0,1:T(8,128)(2,1)}, bf16[2,2,256,384]{3,2,0,1:T(8,128)(2,1)}, u32[]{:S(2)}, u32[]{:S(2)}) %collective-permute-start.20) | collective-permute-done | bytes 786464 | tf_op jit(solution)/shard_map/ppermute | solution.py:65
  176.1 21.4 %collective-permute-done.21 = bf16[2,2,256,384]{3,2,0,1:T(8,128)(2,1)S(1)} collective-permute-done((bf16[2,2,256,384]{3,2,0,1:T(8,128)(2,1)}, bf16[2,2,256,384]{3,2,0,1:T(8,128)(2,1)S(1)}, u32[]{:S(2)}, u32[]{:S(2)}) %collective-permute-start.21) | collective-permute-done | bytes 786464 | tf_op jit(solution)/shard_map/ppermute | solution.py:65
  206.9 18.9 %collective-permute-done.26 = bf16[2,256,384]{2,1,0:T(8,128)(2,1)} collective-permute-done((bf16[2,256,384]{2,1,0:T(8,128)(2,1)S(1)}, bf16[2,256,384]{2,1,0:T(8,128)(2,1)}, u32[]{:S(2)}, u32[]{:S(2)}) %collective-permute-start.26) | collective-permute-done | bytes 393248 | tf_op jit(solution)/shard_map/ppermute | solution.py:65
  265.2 12.0 %collective-permute-done.33 = bf16[256,384]{1,0:T(8,128)(2,1)} collective-permute-done((bf16[256,384]{1,0:T(8,128)(2,1)}, bf16[256,384]{1,0:T(8,128)(2,1)}, u32[]{:S(2)}, u32[]{:S(2)}) %collective-permute-start.33) | collective-permute-done | bytes 196640 | tf_op jit(solution)/shard_map/ppermute | solution.py:65
  316.6 10.1 %shard_map.295 = (f32[512,384]{1,0:T(8,128)}, f32[512,384]{1,0:T(8,128)}) custom-call(s32[7]{0:T(128)} %and_convert_fusion.live_ref, bf16[512,384]{1,0:T(8,128)(2,1)} %slice.353.query_ref, bf16[1024,384]{1,0:T(8,128)(2,1)} %slice.358.own_ref, bf16[2048,384]{1,0:T(8,128)(2,1)} %copy-done.10, bf16[2048,384]{1,0:T(8,128)(2,1)} %copy-done.11, ...), custom_call_target="tpu_custom_call" | custom-call | flops 3221225472 | bytes 7864320 | tf_op jit(solution)/shard_map/pallas_call | solution.py:557
  327.5 8.1 shard_map.296
  341.7 9.7 %collective-permute-done.46 = bf16[128,1536]{1,0:T(8,128)(2,1)S(1)} collective-permute-done((bf16[128,1536]{1,0:T(8,128)(2,1)S(1)}, bf16[128,1536]{1,0:T(8,128)(2,1)S(1)}, u32[]{:S(2)}, u32[]{:S(2)}) %collective-permute-start.46) | collective-permute-done | bytes 393248 | tf_op jit(solution)/shard_map/ppermute | solution.py:31
  355.7 8.8 %collective-permute-done.48 = bf16[128,1536]{1,0:T(8,128)(2,1)S(1)} collective-permute-done((bf16[128,1536]{1,0:T(8,128)(2,1)S(1)}, bf16[128,1536]{1,0:T(8,128)(2,1)S(1)}, u32[]{:S(2)}, u32[]{:S(2)}) %collective-permute-start.48) | collective-permute-done | bytes 393248 | tf_op jit(solution)/shard_map/ppermute | solution.py:31
  375.6 9.7 %collective-permute-done.52 = bf16[128,1536]{1,0:T(8,128)(2,1)S(1)} collective-permute-done((bf16[128,1536]{1,0:T(8,128)(2,1)S(1)}, bf16[128,1536]{1,0:T(8,128)(2,1)S(1)}, u32[]{:S(2)}, u32[]{:S(2)}) %collective-permute-start.52) | collective-permute-done | bytes 393248 | tf_op jit(solution)/shard_map/ppermute | solution.py:31
  389.0 8.8 %collective-permute-done.54 = bf16[128,1536]{1,0:T(8,128)(2,1)S(1)} collective-permute-done((bf16[128,1536]{1,0:T(8,128)(2,1)S(1)}, bf16[128,1536]{1,0:T(8,128)(2,1)S(1)}, u32[]{:S(2)}, u32[]{:S(2)}) %collective-permute-start.54) | collective-permute-done | bytes 393248 | tf_op jit(solution)/shard_map/ppermute | solution.py:31
  420.8 5.4 collective-permute-done.58
  436.8 8.8 %collective-permute-done.60 = bf16[128,1536]{1,0:T(8,128)(2,1)S(1)} collective-permute-done((bf16[128,1536]{1,0:T(8,128)(2,1)S(1)}, bf16[128,1536]{1,0:T(8,128)(2,1)S(1)}, u32[]{:S(2)}, u32[]{:S(2)}) %collective-permute-start.60) | collective-permute-done | bytes 393248 | tf_op jit(solution)/shard_map/ppermute | solution.py:31
  451.7 24.2 %shard_map.297 = (bf16[1024,384]{1,0:T(8,128)(2,1)}, bf16[1024,384]{1,0:T(8,128)(2,1)}, bf16[1024,384]{1,0:T(8,128)(2,1)}, bf16[1024,384]{1,0:T(8,128)(2,1)}, bf...) custom-call(s32[7]{0:T(128)} %and_convert_fusion.live_ref, ...), custom_call_target="tpu_custom_call" | custom-call | flops 8053063680 | bytes 7864320 | tf_op jit(solution)/shard_map/pallas_call | solution.py:557
  478.0 15.4 %shard_map.298 = (bf16[512,384]{1,0:T(8,128)(2,1)}, bf16[512,384]{1,0:T(8,128)(2,1)}, bf16[512,384]{1,0:T(8,128)(2,1)}, bf16[512,384]{1,0:T(8,128)(2,1)}, bf16[5...) custom-call(s32[7]{0:T(128)} %and_convert_fusion.live_ref, ...), custom_call_target="tpu_custom_call" | custom-call | flops 4026531840 | bytes 7864320 | tf_op jit(solution)/shard_map/pallas_call | solution.py:557
  493.4 41.2 %collective-permute-done.62 = bf16[1024,384]{1,0:T(8,128)(2,1)} collective-permute-done((bf16[1024,384]{1,0:T(8,128)(2,1)}, bf16[1024,384]{1,0:T(8,128)(2,1)}, u32[]{:S(2)}, u32[]{:S(2)}) %collective-permute-start.62) | collective-permute-done | bytes 786464 | tf_op jit(solution)/shard_map/ppermute | solution.py:65
  536.1 5.4 collective-permute-start.65
  554.2 14.8 %collective-permute-done.64 = bf16[1024,384]{1,0:T(8,128)(2,1)S(1)} collective-permute-done((bf16[1024,384]{1,0:T(8,128)(2,1)S(1)}, bf16[1024,384]{1,0:T(8,128)(2,1)S(1)}, u32[]{:S(2)}, u32[]{:S(2)}) %collective-permute-start.64) | collective-permute-done | bytes 786464 | tf_op jit(solution)/shard_map/ppermute | solution.py:65
  576.3 5.5 collective-permute-start.70
  589.4 23.9 %collective-permute-done.66 = bf16[512,384]{1,0:T(8,128)(2,1)} collective-permute-done((bf16[512,384]{1,0:T(8,128)(2,1)}, bf16[512,384]{1,0:T(8,128)(2,1)}, u32[]{:S(2)}, u32[]{:S(2)}) %collective-permute-start.66) | collective-permute-done | bytes 393248 | tf_op jit(solution)/shard_map/ppermute | solution.py:65
  613.3 17.2 %collective-permute-done.67 = bf16[512,384]{1,0:T(8,128)(2,1)} collective-permute-done((bf16[512,384]{1,0:T(8,128)(2,1)}, bf16[512,384]{1,0:T(8,128)(2,1)}, u32[]{:S(2)}, u32[]{:S(2)}) %collective-permute-start.67) | collective-permute-done | bytes 393248 | tf_op jit(solution)/shard_map/ppermute | solution.py:65
  633.2 10.8 %collective-permute-start.71 = (bf16[512,384]{1,0:T(8,128)(2,1)S(1)}, bf16[512,384]{1,0:T(8,128)(2,1)S(1)}, u32[]{:S(2)}, u32[]{:S(2)}) collective-permute-start(bf16[512,384]{1,0:T(8,128)(2,1)S(1)} %add_convert_fusion.7), channel_id=1, source_target_pairs={{0,4},{4,0},{8,12},{12,8},{16,20},{20,16},{24,28},{28,24},{1,5},{5... | collective-permute-start | bytes 1179656 | tf_op jit(solution)/shard_map/ppermute | solution.py:65
  645.3 7.5 collective-permute-start.73
  707.0 23.9 %collective-permute-done.79 = bf16[2,256,384]{2,1,0:T(8,128)(2,1)S(1)} collective-permute-done((bf16[2,256,384]{2,1,0:T(8,128)(2,1)S(1)}, bf16[2,256,384]{2,1,0:T(8,128)(2,1)S(1)}, u32[]{:S(2)}, u32[]{:S(2)}) %collective-permute-start.79) | collective-permute-done | bytes 393248 | tf_op jit(solution)/shard_map/ppermute | solution.py:65
  738.9 23.6 %collective-permute-done.87 = bf16[2,2,256,384]{3,2,0,1:T(8,128)(2,1)} collective-permute-done((bf16[2,2,256,384]{3,2,0,1:T(8,128)(2,1)}, bf16[2,2,256,384]{3,2,0,1:T(8,128)(2,1)}, u32[]{:S(2)}, u32[]{:S(2)}) %collective-permute-start.87) | collective-permute-done | bytes 786464 | tf_op jit(solution)/shard_map/ppermute | solution.py:65
  778.5 13.5 %reduce-scatter.5.cloned.1.call-done = bf16[4,192,384]{2,1,0:T(8,128)(2,1)} async-done(((bf16[32,192,384]{2,1,0:T(8,128)(2,1)}), bf16[4,192,384]{2,1,0:T(8,128)(2,1)}) %reduce-scatter.5.cloned.1.call-update) | async-done | bytes 589840 | tf_op jit(solution)/shard_map/reduce_scatter | solution.py:915
  824.2 7.2 collective-permute-done.97
  (778 shorter events, 406.7 us)
Async XLA Ops:
  7.2 236.0 %all-gather.3.cloned.1.call-start = ((), (), s32[]{:S(2)}) async-start(), calls=%async_computation.2 | async-start | bytes 3981312 | tf_op jit(solution)/shard_map/all_gather | solution.py:615
  9.2 326.4 %all-gather.5.cloned.1.call-start = ((), (), s32[]{:S(2)}) async-start(), calls=%async_computation.3 | async-start | bytes 11943936 | tf_op jit(solution)/shard_map/all_gather | solution.py:616
  9.3 28.7 %collective-permute-start.2 = (bf16[128,1536]{1,0:T(8,128)(2,1)}, bf16[128,1536]{1,0:T(8,128)(2,1)}, u32[]{:S(2)}, u32[]{:S(2)}) collective-permute-start(bf16[128,1536]{1,0:T(8,128)(2,1)} %param.19), channel_id=1, source_target_pairs={{0,4},{4,0},{8,12},{12,8},{16,20},{20,16},{24,28},{28,24},{1,5},{5... | collective-permute-start | bytes 1179656 | tf_op jit(solution)/shard_map/ppermute | solution.py:65
  12.3 25.7 %collective-permute-start.3 = (bf16[128,1536]{1,0:T(8,128)(2,1)}, bf16[128,1536]{1,0:T(8,128)(2,1)S(1)}, u32[]{:S(2)}, u32[]{:S(2)}) collective-permute-start(bf16[128,1536]{1,0:T(8,128)(2,1)} %param.19), channel_id=1, source_target_pairs={{0,8},{4,12},{8,16},{12,20},{16,24},{20,28},{1,9},{5,13},{9,17},{1... | collective-permute-start | bytes 1179656 | tf_op jit(solution)/shard_map/ppermute | solution.py:65
  23.0 744.8 %reduce-scatter.3.cloned.1.call-start = ((), (), s32[]{:S(2)}) async-start(), calls=%async_computation.4 | async-start | bytes 10616832 | tf_op jit(solution)/shard_map/reduce_scatter | solution.py:800
  45.5 36.6 %collective-permute-start.8 = (bf16[128,1536]{1,0:T(8,128)(2,1)}, bf16[128,1536]{1,0:T(8,128)(2,1)}, u32[]{:S(2)}, u32[]{:S(2)}) collective-permute-start(bf16[128,1536]{1,0:T(8,128)(2,1)} %collective-permute-done.2), channel_id=1, source_target_pairs={{8,0},{16,8},{24,16},{4,12},{12,20},{20,28},{9,1},{17,9},{25,17},{... | collective-permute-start | bytes 1179656 | tf_op jit(solution)/shard_map/ppermute | solution.py:65
  146.8 29.3 %collective-permute-start.20 = (bf16[2,2,256,384]{3,2,0,1:T(8,128)(2,1)}, bf16[2,2,256,384]{3,2,0,1:T(8,128)(2,1)}, u32[]{:S(2)}, u32[]{:S(2)}) collective-permute-start(bf16[2,2,256,384]{3,2,0,1:T(8,128)(2,1)} %select_bitcast_fusion.5), channel_id=1, source_target_pairs={{0,4},{4,0},{8,12},{12,8},{16,20},{20,16},{24,28},{28,24},{1,5},{5... | collective-permute-start | bytes 2359304 | tf_op jit(solution)/shard_map/ppermute | solution.py:65
  151.7 45.8 %collective-permute-start.21 = (bf16[2,2,256,384]{3,2,0,1:T(8,128)(2,1)}, bf16[2,2,256,384]{3,2,0,1:T(8,128)(2,1)S(1)}, u32[]{:S(2)}, u32[]{:S(2)}) collective-permute-start(bf16[2,2,256,384]{3,2,0,1:T(8,128)(2,1)} %select_bitcast_fusion.4), channel_id=1, source_target_pairs={{0,8},{4,12},{8,0},{12,4},{16,24},{20,28},{24,16},{28,20},{1,9},{5... | collective-permute-start | bytes 2359304 | tf_op jit(solution)/shard_map/ppermute | solution.py:65
  153.2 44.3 %collective-permute-start.24 = (bf16[256,1536]{1,0:T(8,128)(2,1)S(1)}, bf16[256,1536]{1,0:T(8,128)(2,1)}, u32[]{:S(2)}, u32[]{:S(2)}) collective-permute-start(bf16[256,1536]{1,0:T(8,128)(2,1)S(1)} %bitcast.352), channel_id=1, source_target_pairs={{0,2},{1,3},{2,0},{3,1},{4,6},{5,7},{6,4},{7,5},{8,10},{9,11},{10,... | collective-permute-start | bytes 2359304 | tf_op jit(solution)/shard_map/ppermute | solution.py:65
  153.7 44.6 %collective-permute-start.25 = (bf16[256,1536]{1,0:T(8,128)(2,1)S(1)}, bf16[256,1536]{1,0:T(8,128)(2,1)}, u32[]{:S(2)}, u32[]{:S(2)}) collective-permute-start(bf16[256,1536]{1,0:T(8,128)(2,1)S(1)} %bitcast.353), channel_id=1, source_target_pairs={{0,1},{1,0},{2,3},{3,2},{4,5},{5,4},{6,7},{7,6},{8,9},{9,8},{10,11... | collective-permute-start | bytes 2359304 | tf_op jit(solution)/shard_map/ppermute | solution.py:65
  202.2 29.7 %collective-permute-start.29 = (bf16[256,1536]{1,0:T(8,128)(2,1)}, bf16[256,1536]{1,0:T(8,128)(2,1)}, u32[]{:S(2)}, u32[]{:S(2)}) collective-permute-start(bf16[256,1536]{1,0:T(8,128)(2,1)} %collective-permute-done.24), channel_id=1, source_target_pairs={{0,1},{1,0},{2,3},{3,2},{4,5},{5,4},{6,7},{7,6},{8,9},{9,8},{10,11... | collective-permute-start | bytes 2359304 | tf_op jit(solution)/shard_map/ppermute | solution.py:65
  202.2 29.7 %collective-permute-start.30 = (bf16[256,1536]{1,0:T(8,128)(2,1)S(1)}, bf16[256,1536]{1,0:T(8,128)(2,1)}, u32[]{:S(2)}, u32[]{:S(2)}) collective-permute-start(bf16[256,1536]{1,0:T(8,128)(2,1)S(1)} %bitcast.349), channel_id=1, source_target_pairs={{0,2},{1,3},{2,0},{3,1},{4,6},{5,7},{6,4},{7,5},{8,10},{9,11},{10,... | collective-permute-start | bytes 2359304 | tf_op jit(solution)/shard_map/ppermute | solution.py:65
  203.2 28.7 %collective-permute-start.31 = (bf16[256,1536]{1,0:T(8,128)(2,1)S(1)}, bf16[256,1536]{1,0:T(8,128)(2,1)}, u32[]{:S(2)}, u32[]{:S(2)}) collective-permute-start(bf16[256,1536]{1,0:T(8,128)(2,1)S(1)} %bitcast.350), channel_id=1, source_target_pairs={{0,1},{1,0},{2,3},{3,2},{4,5},{5,4},{6,7},{7,6},{8,9},{9,8},{10,11... | collective-permute-start | bytes 2359304 | tf_op jit(solution)/shard_map/ppermute | solution.py:65
  236.1 29.1 %collective-permute-start.32 = (bf16[256,384]{1,0:T(8,128)(2,1)}, bf16[256,384]{1,0:T(8,128)(2,1)}, u32[]{:S(2)}, u32[]{:S(2)}) collective-permute-start(bf16[256,384]{1,0:T(8,128)(2,1)} %get-tuple-element.293), channel_id=1, source_target_pairs={{0,16},{4,20},{8,24},{12,28},{16,0},{20,4},{24,8},{28,12},{1,17},{... | collective-permute-start | bytes 589832 | tf_op jit(solution)/shard_map/ppermute | solution.py:65
  236.1 41.0 %collective-permute-start.33 = (bf16[256,384]{1,0:T(8,128)(2,1)}, bf16[256,384]{1,0:T(8,128)(2,1)}, u32[]{:S(2)}, u32[]{:S(2)}) collective-permute-start(bf16[256,384]{1,0:T(8,128)(2,1)} %get-tuple-element.294), channel_id=1, source_target_pairs={{0,16},{4,20},{8,24},{12,28},{16,0},{20,4},{24,8},{28,12},{1,17},{... | collective-permute-start | bytes 589832 | tf_op jit(solution)/shard_map/ppermute | solution.py:65
  239.1 38.1 %collective-permute-start.34 = (bf16[256,1536]{1,0:T(8,128)(2,1)}, bf16[256,1536]{1,0:T(8,128)(2,1)}, u32[]{:S(2)}, u32[]{:S(2)}) collective-permute-start(bf16[256,1536]{1,0:T(8,128)(2,1)} %collective-permute-done.30), channel_id=1, source_target_pairs={{0,1},{1,0},{2,3},{3,2},{4,5},{5,4},{6,7},{7,6},{8,9},{9,8},{10,11... | collective-permute-start | bytes 2359304 | tf_op jit(solution)/shard_map/ppermute | solution.py:65
  239.1 38.1 %collective-permute-start.35 = (bf16[256,1536]{1,0:T(8,128)(2,1)}, bf16[256,1536]{1,0:T(8,128)(2,1)}, u32[]{:S(2)}, u32[]{:S(2)}) collective-permute-start(bf16[256,1536]{1,0:T(8,128)(2,1)} %bitcast.57), channel_id=1, source_target_pairs={{0,2},{1,3},{2,0},{3,1},{4,6},{5,7},{6,4},{7,5},{8,10},{9,11},{10,... | collective-permute-start | bytes 2359304 | tf_op jit(solution)/shard_map/ppermute | solution.py:65
  240.4 36.8 %collective-permute-start.36 = (bf16[256,1536]{1,0:T(8,128)(2,1)}, bf16[256,1536]{1,0:T(8,128)(2,1)}, u32[]{:S(2)}, u32[]{:S(2)}) collective-permute-start(bf16[256,1536]{1,0:T(8,128)(2,1)} %bitcast.57), channel_id=1, source_target_pairs={{0,1},{1,0},{2,3},{3,2},{4,5},{5,4},{6,7},{7,6},{8,9},{9,8},{10,11... | collective-permute-start | bytes 2359304 | tf_op jit(solution)/shard_map/ppermute | solution.py:65
  428.5 363.5 %reduce-scatter.5.cloned.1.call-start = ((), (), s32[]{:S(2)}) async-start(), calls=%async_computation.5 | async-start | bytes 5308416 | tf_op jit(solution)/shard_map/reduce_scatter | solution.py:915
  475.9 58.7 %collective-permute-start.62 = (bf16[1024,384]{1,0:T(8,128)(2,1)}, bf16[1024,384]{1,0:T(8,128)(2,1)}, u32[]{:S(2)}, u32[]{:S(2)}) collective-permute-start(bf16[1024,384]{1,0:T(8,128)(2,1)} %get-tuple-element.359), channel_id=1, source_target_pairs={{8,0},{16,8},{24,16},{4,12},{12,20},{20,28},{9,1},{17,9},{25,17},{... | collective-permute-start | bytes 2359304 | tf_op jit(solution)/shard_map/ppermute | solution.py:65
  536.0 33.1 %collective-permute-start.64 = (bf16[1024,384]{1,0:T(8,128)(2,1)S(1)}, bf16[1024,384]{1,0:T(8,128)(2,1)S(1)}, u32[]{:S(2)}, u32[]{:S(2)}) collective-permute-start(bf16[1024,384]{1,0:T(8,128)(2,1)S(1)} %add_convert_fusion.3), channel_id=1, source_target_pairs={{0,4},{4,0},{8,12},{12,8},{16,20},{20,16},{24,28},{28,24},{1,5},{5... | collective-permute-start | bytes 2359304 | tf_op jit(solution)/shard_map/ppermute | solution.py:65
  536.1 33.0 %collective-permute-start.65 = (bf16[1024,384]{1,0:T(8,128)(2,1)S(1)}, bf16[1024,384]{1,0:T(8,128)(2,1)S(1)}, u32[]{:S(2)}, u32[]{:S(2)}) collective-permute-start(bf16[1024,384]{1,0:T(8,128)(2,1)S(1)} %copy-done.150), channel_id=1, source_target_pairs={{0,8},{8,16},{16,24},{12,4},{20,12},{28,20},{1,9},{9,17},{17,25},{... | collective-permute-start | bytes 2359304 | tf_op jit(solution)/shard_map/ppermute | solution.py:65
  572.6 57.9 %collective-permute-start.68 = (bf16[1024,384]{1,0:T(8,128)(2,1)}, bf16[1024,384]{1,0:T(8,128)(2,1)}, u32[]{:S(2)}, u32[]{:S(2)}) collective-permute-start(bf16[1024,384]{1,0:T(8,128)(2,1)} %add_convert_fusion.2), channel_id=1, source_target_pairs={{0,4},{4,0},{8,12},{12,8},{16,20},{20,16},{24,28},{28,24},{1,5},{5... | collective-permute-start | bytes 2359304 | tf_op jit(solution)/shard_map/ppermute | solution.py:65
  575.0 55.4 %collective-permute-start.69 = (bf16[1024,384]{1,0:T(8,128)(2,1)}, bf16[1024,384]{1,0:T(8,128)(2,1)}, u32[]{:S(2)}, u32[]{:S(2)}) collective-permute-start(bf16[1024,384]{1,0:T(8,128)(2,1)} %get-tuple-element.398), channel_id=1, source_target_pairs={{8,0},{12,4},{16,8},{20,12},{24,16},{28,20},{9,1},{13,5},{17,9},{2... | collective-permute-start | bytes 2359304 | tf_op jit(solution)/shard_map/ppermute | solution.py:65
  576.3 54.1 %collective-permute-start.70 = (bf16[1024,384]{1,0:T(8,128)(2,1)}, bf16[1024,384]{1,0:T(8,128)(2,1)}, u32[]{:S(2)}, u32[]{:S(2)}) collective-permute-start(bf16[1024,384]{1,0:T(8,128)(2,1)} %get-tuple-element.399), channel_id=1, source_target_pairs={{0,8},{4,12},{8,16},{12,20},{16,24},{20,28},{1,9},{5,13},{9,17},{1... | collective-permute-start | bytes 2359304 | tf_op jit(solution)/shard_map/ppermute | solution.py:65
  581.8 31.5 %collective-permute-start.66 = (bf16[512,384]{1,0:T(8,128)(2,1)}, bf16[512,384]{1,0:T(8,128)(2,1)}, u32[]{:S(2)}, u32[]{:S(2)}) collective-permute-start(bf16[512,384]{1,0:T(8,128)(2,1)} %add_convert_fusion.8), channel_id=1, source_target_pairs={{0,4},{4,0},{8,12},{12,8},{16,20},{20,16},{24,28},{28,24},{1,5},{5... | collective-permute-start | bytes 1179656 | tf_op jit(solution)/shard_map/ppermute | solution.py:65
  581.8 48.7 %collective-permute-start.67 = (bf16[512,384]{1,0:T(8,128)(2,1)}, bf16[512,384]{1,0:T(8,128)(2,1)}, u32[]{:S(2)}, u32[]{:S(2)}) collective-permute-start(bf16[512,384]{1,0:T(8,128)(2,1)} %get-tuple-element.396), channel_id=1, source_target_pairs={{0,8},{8,16},{16,24},{12,4},{20,12},{28,20},{1,9},{9,17},{17,25},{... | collective-permute-start | bytes 1179656 | tf_op jit(solution)/shard_map/ppermute | solution.py:65
  633.2 26.1 %collective-permute-start.71 = (bf16[512,384]{1,0:T(8,128)(2,1)S(1)}, bf16[512,384]{1,0:T(8,128)(2,1)S(1)}, u32[]{:S(2)}, u32[]{:S(2)}) collective-permute-start(bf16[512,384]{1,0:T(8,128)(2,1)S(1)} %add_convert_fusion.7), channel_id=1, source_target_pairs={{0,4},{4,0},{8,12},{12,8},{16,20},{20,16},{24,28},{28,24},{1,5},{5... | collective-permute-start | bytes 1179656 | tf_op jit(solution)/shard_map/ppermute | solution.py:65
  702.7 28.2 %collective-permute-start.79 = (bf16[2,256,384]{2,1,0:T(8,128)(2,1)S(1)}, bf16[2,256,384]{2,1,0:T(8,128)(2,1)S(1)}, u32[]{:S(2)}, u32[]{:S(2)}) collective-permute-start(bf16[2,256,384]{2,1,0:T(8,128)(2,1)S(1)} %pad_maximum_fusion.19), channel_id=1, source_target_pairs={{0,8},{4,12},{8,0},{12,4},{16,24},{20,28},{24,16},{28,20},{1,9},{5... | collective-permute-start | bytes 1179656 | tf_op jit(solution)/shard_map/ppermute | solution.py:65
  705.4 26.2 %collective-permute-start.80 = (bf16[2,256,384]{2,1,0:T(8,128)(2,1)S(1)}, bf16[2,256,384]{2,1,0:T(8,128)(2,1)S(1)}, u32[]{:S(2)}, u32[]{:S(2)}) collective-permute-start(bf16[2,256,384]{2,1,0:T(8,128)(2,1)S(1)} %pad_maximum_fusion.20), channel_id=1, source_target_pairs={{0,4},{4,0},{8,12},{12,8},{16,20},{20,16},{24,28},{28,24},{1,5},{5... | collective-permute-start | bytes 1179656 | tf_op jit(solution)/shard_map/ppermute | solution.py:65
  736.1 26.4 %collective-permute-start.87 = (bf16[2,2,256,384]{3,2,0,1:T(8,128)(2,1)}, bf16[2,2,256,384]{3,2,0,1:T(8,128)(2,1)}, u32[]{:S(2)}, u32[]{:S(2)}) collective-permute-start(bf16[2,2,256,384]{3,2,0,1:T(8,128)(2,1)} %pad_maximum_fusion.15), channel_id=1, source_target_pairs={{0,4},{4,0},{8,12},{12,8},{16,20},{20,16},{24,28},{28,24},{1,5},{5... | collective-permute-start | bytes 2359304 | tf_op jit(solution)/shard_map/ppermute | solution.py:65
  737.3 25.2 %collective-permute-start.88 = (bf16[2,2,256,384]{3,2,0,1:T(8,128)(2,1)S(1)}, bf16[2,2,256,384]{3,2,0,1:T(8,128)(2,1)}, u32[]{:S(2)}, u32[]{:S(2)}) collective-permute-start(bf16[2,2,256,384]{3,2,0,1:T(8,128)(2,1)S(1)} %pad_maximum_fusion.16), channel_id=1, source_target_pairs={{0,8},{4,12},{8,0},{12,4},{16,24},{20,28},{24,16},{28,20},{1,9},{5... | collective-permute-start | bytes 2359304 | tf_op jit(solution)/shard_map/ppermute | solution.py:65
  (233 other events, 2666.0 us)
Sparse Core Ops, SparseCore 0:
  10.2 85.5 all-gather.2
  98.0 181.7 all-gather.4
  428.6 216.0 reduce-scatter.2
  677.0 114.9 reduce-scatter.4

commit v5 on v3

--- a/solution.py
+++ b/solution.py
@@ -169,6 +169,26 @@
         )
         bit *= 2
     return value
+
+
+def to_partners(value, axis):
+    return [(value, axis, swap_pairs(axis, k)) for k in range(1, lax.axis_size(axis))]
+
+
+def placed(own, moved, index):
+    count = len(moved) + 1
+    result = jnp.broadcast_to(own[None], (count,) + own.shape)
+    place = jnp.arange(count).reshape((count,) + (1,) * own.ndim)
+    for k, value in enumerate(moved):
+        result = jnp.where(place == (index ^ (k + 1)), value[None], result)
+    return result
+
+
+def tree_sum(values):
+    values = list(values)
+    while len(values) > 1:
+        values = [one + two for one, two in zip(values[::2], values[1::2])]
+    return values[0]
 
 
 def chain_sum(value, axis):
@@ -625,19 +645,17 @@
 
     def modulate_all():
         value = jax.nn.silu(condition).astype(BF)
-        for bit in all_bits(dp_count):
-            (other,) = yield [(value, "dp", swap_pairs("dp", bit))]
-            value = in_order((dp_index & bit) != 0, value, other, 0).reshape(2 * bit, width)
+        moved = yield to_partners(value, "dp")
+        value = placed(value, moved, dp_index).reshape(dp_count, width)
         cond_mine = lax.dynamic_slice_in_dim(value, dp_index * shard, shard, axis=1)
         value = mm(cond_mine, ada_weight, NN)
         for bit in all_bits(dp_count):
             (other,) = yield [(value, "dp", swap_pairs("dp", bit))]
             value = value + other
         bias_part = lax.dynamic_slice_in_dim(ada_bias, mp_index * width, width)
-        value = (value + bias_part[None, :])[None]
-        for bit in all_bits(mp_count):
-            (other,) = yield [(value, "mp", swap_pairs("mp", bit))]
-            value = in_order((mp_index & bit) != 0, value, other, 0).reshape(2 * bit, dp_count, width)
+        value = value + bias_part[None, :]
+        moved = yield to_partners(value, "mp")
+        value = placed(value, moved, mp_index)
         return cond_mine, value
 
     def caption_features():
@@ -926,7 +944,8 @@
     text_rows = jnp.concatenate(text_back.result, axis=1)
 
     def gather_mod_grads(tie):
-        mod_sum = sum_all(tie(mod_grads), "mp")
+        own = tie(mod_grads)
+        mod_sum = tree_sum([own] + [swap(own, "mp", k) for k in range(1, mp_count)])
         mine = jnp.arange(mp_count)[:, None] == mp_index
         grad_mod_low = jnp.sum(jnp.where(mine, mod_sum, 0.0), axis=0)[None].astype(BF)
         return grad_mod_low, gather_in_order(grad_mod_low, "dp", dp_index)
@@ -966,8 +985,8 @@
     block = text_dim // mp_count
 
     def sum_small():
-        value = yield from chain_sum(small, "mp")
-        return (yield from chain_sum(value, "dp"))
+        moved = yield to_partners(small, "mp")
+        return (yield from chain_sum(tree_sum([small] + list(moved)), "dp"))
 
     def send_captions():
         columns = yield from exchange_blocks(

time: 826 us -> 846 us (1.024)
  Pallas kernels: 74.8 us -> 88.7 us
  starting transfers between devices: 131 us -> 141 us
    ppermute x73 -> x79, starting transfers between devices: 111 us -> 126 us  [stage(): lax.ppermute(value, axis, pairs)]
    pallas_call x4, Pallas kernels: 57.7 us -> 71.6 us  [attend(): pl.pallas_call(kernel, grid=(width // PAIR,), in_specs=[smem] * len(scala...]
    ppermute x29 -> x30, starting transfers between devices: 19.9 us -> 14.7 us  [swap(): return lax.ppermute(value, axis, [(i, i ^ bit) for i in range(count)])]
    unnamed x336 -> x358, local copies, waits for them, and re-layouts: 17.7 us -> 13.9 us
    ppermute x29 -> x30, waiting for transfers between devices: 76 us -> 79.3 us  [swap(): return lax.ppermute(value, axis, [(i, i ^ bit) for i in range(count)])]
    ppermute x73 -> x79, waiting for transfers between devices: 287 us -> 284 us  [stage(): lax.ppermute(value, axis, pairs)]
  transfers between devices with their start and end apart: 106 -> 113, of which waited for: 52 -> 53; matrix products, arithmetic and copies ran while one was open for 22% -> 20% of each run, Pallas kernels for 9% -> 11%
where the time goes in v5:
time: 846 us; the launch traced here: 832 us
  waiting for transfers between devices  370 us (44%)
  starting transfers between devices  141 us (17%)
  other arithmetic  92.4 us (11%)
  Pallas kernels  88.7 us (10%)
  matrix products  68.7 us (8%)
  local copies, waits for them, and re-layouts  52.2 us (6%)
  between operations  19.3 us (2%)
    ppermute x79, waiting for transfers between devices, stage(): lax.ppermute(value, axis, pairs)  284 us
    ppermute x79, starting transfers between devices, stage(): lax.ppermute(value, axis, pairs)  126 us
    ppermute x30, waiting for transfers between devices, swap(): return lax.ppermute(value, axis, [(i, i ^ bit) for i in range(count)])  79.3 us
    pallas_call x4, Pallas kernels, attend(): pl.pallas_call(kernel, grid=(width // PAIR,), in_specs=[smem] * len(scala...  71.6 us
    dot_general x32, matrix products, mm(): return lax.dot_general(left, right, dims, preferred_element_type=F32)  68.7 us
  transfers between devices with their start and end apart: 113, of which 53 were waited for; matrix products, arithmetic and copies ran while one was open for 20% of the time, Pallas kernels for 11%

profile of v5, /device:TPU:0, one launch (start us, length us, event | category | flops | bytes accessed | tf_op | source)
XLA Modules:
  0.0 832.2 jit_solution(15560111898667006854)
XLA Ops:
  39.3 10.2 %collective-permute-done.4 = bf16[1,1536]{1,0:T(2,128)(2,1)S(1)} collective-permute-done((bf16[1,1536]{1,0:T(2,128)(2,1)S(1)}, bf16[1,1536]{1,0:T(2,128)(2,1)S(1)}, u32[]{:S(2)}, u32[]{:S(2)}) %collective-permute-start.4) | collective-permute-done | bytes 3104 | tf_op jit(solution)/shard_map/ppermute | solution.py:65
  69.8 7.5 collective-permute-done.12
  80.4 14.2 %collective-permute-done.14 = bf16[128,1536]{1,0:T(8,128)(2,1)S(1)} collective-permute-done((bf16[128,1536]{1,0:T(8,128)(2,1)}, bf16[128,1536]{1,0:T(8,128)(2,1)S(1)}, u32[]{:S(2)}, u32[]{:S(2)}) %collective-permute-start.14) | collective-permute-done | bytes 393248 | tf_op jit(solution)/shard_map/ppermute | solution.py:65
  99.1 9.5 %collective-permute-done.16 = bf16[2,2,64,512]{3,2,1,0:T(8,128)(2,1)S(1)} collective-permute-done((bf16[2,2,64,512]{3,2,1,0:T(8,128)(2,1)S(1)}, bf16[2,2,64,512]{3,2,1,0:T(8,128)(2,1)S(1)}, u32[]{:S(2)}, u32[]{:S(2)}) %collective-permute-start.16) | collective-permute-done | bytes 262176 | tf_op jit(solution)/shard_map/ppermute | solution.py:65
  114.8 24.2 %collective-permute-start.18 = (f32[8,1536]{1,0:T(8,128)S(1)}, f32[8,1536]{1,0:T(8,128)S(1)}, u32[]{:S(2)}, u32[]{:S(2)}) collective-permute-start(f32[8,1536]{1,0:T(8,128)S(1)} %add.476), channel_id=1, source_target_pairs={{0,16},{4,20},{8,24},{12,28},{16,0},{20,4},{24,8},{28,12},{1,17},{... | collective-permute-start | bytes 147464 | tf_op jit(solution)/shard_map/ppermute | solution.py:65
  139.1 6.3 collective-permute-done.18
  168.1 8.6 %sine_multiply_fusion = (f32[3584,128]{1,0:T(8,128)}, f32[3584,128]{1,0:T(8,128)}) fusion(f32[128]{0:T(128)S(1)} %get-tuple-element.613, f32[128]{0:T(128)S(1)} %copy-done.156, s32[3584]{0:T(1024)S(1)} %add_select_fusion, s32[3584]{0:T(1024)S(1)} %add_select_fusion.1, pred[128]{0:T(512)(128)(4,1)S(1)} %copy-done.157), kind=kLoop, calls=%fused_computation.40 | loop fusion | flops 1835008 | bytes 3699840 | tf_op jit(solution)/shard_map/mul | solution.py:722
  179.9 12.6 %collective-permute-done.25 = bf16[2,2,256,384]{3,2,0,1:T(8,128)(2,1)} collective-permute-done((bf16[2,2,256,384]{3,2,0,1:T(8,128)(2,1)}, bf16[2,2,256,384]{3,2,0,1:T(8,128)(2,1)}, u32[]{:S(2)}, u32[]{:S(2)}) %collective-permute-start.25) | collective-permute-done | bytes 786464 | tf_op jit(solution)/shard_map/ppermute | solution.py:65
  192.5 32.6 %collective-permute-done.26 = bf16[2,2,256,384]{3,2,0,1:T(8,128)(2,1)} collective-permute-done((bf16[2,2,256,384]{3,2,0,1:T(8,128)(2,1)}, bf16[2,2,256,384]{3,2,0,1:T(8,128)(2,1)}, u32[]{:S(2)}, u32[]{:S(2)}) %collective-permute-start.26) | collective-permute-done | bytes 786464 | tf_op jit(solution)/shard_map/ppermute | solution.py:65
  234.1 31.1 %collective-permute-done.31 = bf16[2,256,384]{2,1,0:T(8,128)(2,1)} collective-permute-done((bf16[2,256,384]{2,1,0:T(8,128)(2,1)S(1)}, bf16[2,256,384]{2,1,0:T(8,128)(2,1)}, u32[]{:S(2)}, u32[]{:S(2)}) %collective-permute-start.31) | collective-permute-done | bytes 393248 | tf_op jit(solution)/shard_map/ppermute | solution.py:65
  335.0 5.0 collective-permute-start.48
  342.3 12.6 %shard_map.295 = (f32[512,384]{1,0:T(8,128)}, f32[512,384]{1,0:T(8,128)}) custom-call(s32[7]{0:T(128)} %and_convert_fusion.live_ref, bf16[512,384]{1,0:T(8,128)(2,1)} %slice.353.query_ref, bf16[1024,384]{1,0:T(8,128)(2,1)} %slice.358.own_ref, bf16[2048,384]{1,0:T(8,128)(2,1)} %copy-done.13, bf16[2048,384]{1,0:T(8,128)(2,1)} %copy-done.14, ...), custom_call_target="tpu_custom_call" | custom-call | flops 3221225472 | bytes 7864320 | tf_op jit(solution)/shard_map/pallas_call | solution.py:577
  355.7 9.5 %shard_map.296 = (bf16[512,384]{1,0:T(8,128)(2,1)}, f32[512,384]{1,0:T(8,128)}, f32[512,384]{1,0:T(8,128)}) custom-call(s32[7]{0:T(128)} %and_convert_fusion.live_ref, f32[6]{0:T(128)} %dynamic-slice_tanh_fusion.2.gate_ref, bf16[512,384]{1,0:T(8,128)(2,1)} %slice.353.query_ref, f32[512,384]{1,0:T(8,128)} %get-tuple-element.358.self_ref.out_ref, ...), custom_call_target="tpu_custom_call" | custom-call | flops 1610612736 | bytes 7864320 | tf_op jit(solution)/shard_map/pallas_call | solution.py:577
  370.5 10.4 %collective-permute-done.51 = bf16[128,1536]{1,0:T(8,128)(2,1)S(1)} collective-permute-done((bf16[128,1536]{1,0:T(8,128)(2,1)S(1)}, bf16[128,1536]{1,0:T(8,128)(2,1)S(1)}, u32[]{:S(2)}, u32[]{:S(2)}) %collective-permute-start.51) | collective-permute-done | bytes 393248 | tf_op jit(solution)/shard_map/ppermute | solution.py:31
  384.5 9.6 %collective-permute-done.53 = bf16[128,1536]{1,0:T(8,128)(2,1)S(1)} collective-permute-done((bf16[128,1536]{1,0:T(8,128)(2,1)S(1)}, bf16[128,1536]{1,0:T(8,128)(2,1)S(1)}, u32[]{:S(2)}, u32[]{:S(2)}) %collective-permute-start.53) | collective-permute-done | bytes 393248 | tf_op jit(solution)/shard_map/ppermute | solution.py:31
  404.5 10.4 %collective-permute-done.57 = bf16[128,1536]{1,0:T(8,128)(2,1)S(1)} collective-permute-done((bf16[128,1536]{1,0:T(8,128)(2,1)S(1)}, bf16[128,1536]{1,0:T(8,128)(2,1)S(1)}, u32[]{:S(2)}, u32[]{:S(2)}) %collective-permute-start.57) | collective-permute-done | bytes 393248 | tf_op jit(solution)/shard_map/ppermute | solution.py:31
  417.8 9.6 %collective-permute-done.59 = bf16[128,1536]{1,0:T(8,128)(2,1)S(1)} collective-permute-done((bf16[128,1536]{1,0:T(8,128)(2,1)S(1)}, bf16[128,1536]{1,0:T(8,128)(2,1)S(1)}, u32[]{:S(2)}, u32[]{:S(2)}) %collective-permute-start.59) | collective-permute-done | bytes 393248 | tf_op jit(solution)/shard_map/ppermute | solution.py:31
  436.5 5.3 convolution_convert_fusion
  449.9 6.2 collective-permute-done.63
  466.6 9.9 %collective-permute-done.65 = bf16[128,1536]{1,0:T(8,128)(2,1)} collective-permute-done((bf16[128,1536]{1,0:T(8,128)(2,1)}, bf16[128,1536]{1,0:T(8,128)(2,1)}, u32[]{:S(2)}, u32[]{:S(2)}) %collective-permute-start.65) | collective-permute-done | bytes 393248 | tf_op jit(solution)/shard_map/ppermute | solution.py:31
  483.0 18.9 %shard_map.297 = (bf16[512,384]{1,0:T(8,128)(2,1)}, bf16[512,384]{1,0:T(8,128)(2,1)}, bf16[512,384]{1,0:T(8,128)(2,1)}, bf16[512,384]{1,0:T(8,128)(2,1)}, bf16[5...) custom-call(s32[7]{0:T(128)} %and_convert_fusion.live_ref, ...), custom_call_target="tpu_custom_call" | custom-call | flops 4026531840 | bytes 7864320 | tf_op jit(solution)/shard_map/pallas_call | solution.py:577
  503.3 30.7 %shard_map.298 = (bf16[1024,384]{1,0:T(8,128)(2,1)}, bf16[1024,384]{1,0:T(8,128)(2,1)}, bf16[1024,384]{1,0:T(8,128)(2,1)}, bf16[1024,384]{1,0:T(8,128)(2,1)}, bf...) custom-call(s32[7]{0:T(128)} %and_convert_fusion.live_ref, ...), custom_call_target="tpu_custom_call" | custom-call | flops 8053063680 | bytes 7864320 | tf_op jit(solution)/shard_map/pallas_call | solution.py:577
  549.1 6.2 collective-permute-done.68
  555.3 11.9 %collective-permute-done.70 = bf16[1024,384]{1,0:T(8,128)(2,1)S(1)} collective-permute-done((bf16[1024,384]{1,0:T(8,128)(2,1)}, bf16[1024,384]{1,0:T(8,128)(2,1)S(1)}, u32[]{:S(2)}, u32[]{:S(2)}) %collective-permute-start.70) | collective-permute-done | bytes 786464 | tf_op jit(solution)/shard_map/ppermute | solution.py:65
  578.5 27.5 %collective-permute-done.71 = bf16[512,384]{1,0:T(8,128)(2,1)S(1)} collective-permute-done((bf16[512,384]{1,0:T(8,128)(2,1)S(1)}, bf16[512,384]{1,0:T(8,128)(2,1)S(1)}, u32[]{:S(2)}, u32[]{:S(2)}) %collective-permute-start.71) | collective-permute-done | bytes 393248 | tf_op jit(solution)/shard_map/ppermute | solution.py:65
  614.0 5.7 collective-permute-start.78
  628.1 50.6 %collective-permute-done.79 = bf16[256,384]{1,0:T(8,128)(2,1)} collective-permute-done((bf16[256,384]{1,0:T(8,128)(2,1)S(1)}, bf16[256,384]{1,0:T(8,128)(2,1)}, u32[]{:S(2)}, u32[]{:S(2)}) %collective-permute-start.79) | collective-permute-done | bytes 196640 | tf_op jit(solution)/shard_map/ppermute | solution.py:65
  743.6 8.0 collective-permute-done.96
  774.6 6.0 collective-permute-done.101
  788.9 6.6 collective-permute-done.104
  800.2 12.5 %collective-permute-done.105 = f32[20,1536]{1,0:T(8,128)S(1)} collective-permute-done((f32[20,1536]{1,0:T(8,128)S(1)}, f32[20,1536]{1,0:T(8,128)S(1)}, u32[]{:S(2)}, u32[]{:S(2)}) %collective-permute-start.105) | collective-permute-done | bytes 122912 | tf_op jit(solution)/shard_map/ppermute | solution.py:65
  816.6 6.1 reduce-scatter.5.cloned.1.call-done
  (833 shorter events, 377.0 us)
Async XLA Ops:
  7.2 276.8 %all-gather.3.cloned.1.call-start = ((), (), s32[]{:S(2)}) async-start(), calls=%async_computation.2 | async-start | bytes 3981312 | tf_op jit(solution)/shard_map/all_gather | solution.py:635
  9.3 355.9 %all-gather.5.cloned.1.call-start = ((), (), s32[]{:S(2)}) async-start(), calls=%async_computation.3 | async-start | bytes 11943936 | tf_op jit(solution)/shard_map/all_gather | solution.py:636
  17.6 44.0 %collective-permute-start.8 = (bf16[128,1536]{1,0:T(8,128)(2,1)}, bf16[128,1536]{1,0:T(8,128)(2,1)}, u32[]{:S(2)}, u32[]{:S(2)}) collective-permute-start(bf16[128,1536]{1,0:T(8,128)(2,1)} %param.19), channel_id=1, source_target_pairs={{0,4},{4,0},{8,12},{12,8},{16,20},{20,16},{24,28},{28,24},{1,5},{5... | collective-permute-start | bytes 1179656 | tf_op jit(solution)/shard_map/ppermute | solution.py:65
  21.6 668.6 %reduce-scatter.3.cloned.1.call-start = ((), (), s32[]{:S(2)}) async-start(), calls=%async_computation.4 | async-start | bytes 10616832 | tf_op jit(solution)/shard_map/reduce_scatter | solution.py:818
  30.4 31.3 %collective-permute-start.9 = (bf16[128,1536]{1,0:T(8,128)(2,1)S(1)}, bf16[128,1536]{1,0:T(8,128)(2,1)S(1)}, u32[]{:S(2)}, u32[]{:S(2)}) collective-permute-start(bf16[128,1536]{1,0:T(8,128)(2,1)S(1)} %copy-done.22), channel_id=1, source_target_pairs={{0,8},{4,12},{8,16},{12,20},{16,24},{20,28},{1,9},{5,13},{9,17},{1... | collective-permute-start | bytes 1179656 | tf_op jit(solution)/shard_map/ppermute | solution.py:65
  33.9 27.8 %collective-permute-start.10 = (bf16[128,1536]{1,0:T(8,128)(2,1)S(1)}, bf16[128,1536]{1,0:T(8,128)(2,1)S(1)}, u32[]{:S(2)}, u32[]{:S(2)}) collective-permute-start(bf16[128,1536]{1,0:T(8,128)(2,1)S(1)} %copy-done.22), channel_id=1, source_target_pairs={{8,0},{12,4},{16,8},{20,12},{24,16},{28,20},{9,1},{13,5},{17,9},{2... | collective-permute-start | bytes 1179656 | tf_op jit(solution)/shard_map/ppermute | solution.py:65
  66.2 28.4 %collective-permute-start.14 = (bf16[128,1536]{1,0:T(8,128)(2,1)}, bf16[128,1536]{1,0:T(8,128)(2,1)S(1)}, u32[]{:S(2)}, u32[]{:S(2)}) collective-permute-start(bf16[128,1536]{1,0:T(8,128)(2,1)} %collective-permute-done.8), channel_id=1, source_target_pairs={{8,0},{16,8},{24,16},{4,12},{12,20},{20,28},{9,1},{17,9},{25,17},{... | collective-permute-start | bytes 1179656 | tf_op jit(solution)/shard_map/ppermute | solution.py:65
  113.4 32.0 %collective-permute-start.19 = (bf16[8,64,512]{2,1,0:T(8,128)(2,1)S(1)}, bf16[8,64,512]{2,1,0:T(8,128)(2,1)S(1)}, u32[]{:S(2)}, u32[]{:S(2)}) collective-permute-start(bf16[8,64,512]{2,1,0:T(8,128)(2,1)S(1)} %bitcast.307), channel_id=1, source_target_pairs={{0,2},{1,3},{2,0},{3,1},{4,6},{5,7},{6,4},{7,5},{8,10},{9,11},{10,... | collective-permute-start | bytes 1572872 | tf_op jit(solution)/shard_map/ppermute | solution.py:65
  114.8 30.6 %collective-permute-start.20 = (bf16[8,64,512]{2,1,0:T(8,128)(2,1)S(1)}, bf16[8,64,512]{2,1,0:T(8,128)(2,1)S(1)}, u32[]{:S(2)}, u32[]{:S(2)}) collective-permute-start(bf16[8,64,512]{2,1,0:T(8,128)(2,1)S(1)} %bitcast.308), channel_id=1, source_target_pairs={{0,1},{1,0},{2,3},{3,2},{4,5},{5,4},{6,7},{7,6},{8,9},{9,8},{10,11... | collective-permute-start | bytes 1572872 | tf_op jit(solution)/shard_map/ppermute | solution.py:65
  114.8 30.5 %collective-permute-start.18 = (f32[8,1536]{1,0:T(8,128)S(1)}, f32[8,1536]{1,0:T(8,128)S(1)}, u32[]{:S(2)}, u32[]{:S(2)}) collective-permute-start(f32[8,1536]{1,0:T(8,128)S(1)} %add.476), channel_id=1, source_target_pairs={{0,16},{4,20},{8,24},{12,28},{16,0},{20,4},{24,8},{28,12},{1,17},{... | collective-permute-start | bytes 147464 | tf_op jit(solution)/shard_map/ppermute | solution.py:65
  159.9 32.6 %collective-permute-start.25 = (bf16[2,2,256,384]{3,2,0,1:T(8,128)(2,1)}, bf16[2,2,256,384]{3,2,0,1:T(8,128)(2,1)}, u32[]{:S(2)}, u32[]{:S(2)}) collective-permute-start(bf16[2,2,256,384]{3,2,0,1:T(8,128)(2,1)} %select_bitcast_fusion.5), channel_id=1, source_target_pairs={{0,4},{4,0},{8,12},{12,8},{16,20},{20,16},{24,28},{28,24},{1,5},{5... | collective-permute-start | bytes 2359304 | tf_op jit(solution)/shard_map/ppermute | solution.py:65
  161.5 63.5 %collective-permute-start.26 = (bf16[2,2,256,384]{3,2,0,1:T(8,128)(2,1)}, bf16[2,2,256,384]{3,2,0,1:T(8,128)(2,1)}, u32[]{:S(2)}, u32[]{:S(2)}) collective-permute-start(bf16[2,2,256,384]{3,2,0,1:T(8,128)(2,1)} %select_bitcast_fusion.4), channel_id=1, source_target_pairs={{0,8},{4,12},{8,0},{12,4},{16,24},{20,28},{24,16},{28,20},{1,9},{5... | collective-permute-start | bytes 2359304 | tf_op jit(solution)/shard_map/ppermute | solution.py:65
  166.6 58.4 %collective-permute-start.29 = (bf16[256,1536]{1,0:T(8,128)(2,1)S(1)}, bf16[256,1536]{1,0:T(8,128)(2,1)}, u32[]{:S(2)}, u32[]{:S(2)}) collective-permute-start(bf16[256,1536]{1,0:T(8,128)(2,1)S(1)} %bitcast.323), channel_id=1, source_target_pairs={{0,2},{1,3},{2,0},{3,1},{4,6},{5,7},{6,4},{7,5},{8,10},{9,11},{10,... | collective-permute-start | bytes 2359304 | tf_op jit(solution)/shard_map/ppermute | solution.py:65
  168.1 57.0 %collective-permute-start.30 = (bf16[256,1536]{1,0:T(8,128)(2,1)S(1)}, bf16[256,1536]{1,0:T(8,128)(2,1)}, u32[]{:S(2)}, u32[]{:S(2)}) collective-permute-start(bf16[256,1536]{1,0:T(8,128)(2,1)S(1)} %bitcast.324), channel_id=1, source_target_pairs={{0,1},{1,0},{2,3},{3,2},{4,5},{5,4},{6,7},{7,6},{8,9},{9,8},{10,11... | collective-permute-start | bytes 2359304 | tf_op jit(solution)/shard_map/ppermute | solution.py:65
  230.0 35.2 %collective-permute-start.31 = (bf16[2,256,384]{2,1,0:T(8,128)(2,1)S(1)}, bf16[2,256,384]{2,1,0:T(8,128)(2,1)}, u32[]{:S(2)}, u32[]{:S(2)}) collective-permute-start(bf16[2,256,384]{2,1,0:T(8,128)(2,1)S(1)} %fusion.53), channel_id=1, source_target_pairs={{0,8},{4,12},{8,0},{12,4},{16,24},{20,28},{24,16},{28,20},{1,9},{5... | collective-permute-start | bytes 1179656 | tf_op jit(solution)/shard_map/ppermute | solution.py:65
  230.0 42.4 %collective-permute-start.34 = (bf16[256,1536]{1,0:T(8,128)(2,1)}, bf16[256,1536]{1,0:T(8,128)(2,1)}, u32[]{:S(2)}, u32[]{:S(2)}) collective-permute-start(bf16[256,1536]{1,0:T(8,128)(2,1)} %collective-permute-done.29), channel_id=1, source_target_pairs={{0,1},{1,0},{2,3},{3,2},{4,5},{5,4},{6,7},{7,6},{8,9},{9,8},{10,11... | collective-permute-start | bytes 2359304 | tf_op jit(solution)/shard_map/ppermute | solution.py:65
  230.0 42.4 %collective-permute-start.35 = (bf16[256,1536]{1,0:T(8,128)(2,1)S(1)}, bf16[256,1536]{1,0:T(8,128)(2,1)}, u32[]{:S(2)}, u32[]{:S(2)}) collective-permute-start(bf16[256,1536]{1,0:T(8,128)(2,1)S(1)} %bitcast.320), channel_id=1, source_target_pairs={{0,2},{1,3},{2,0},{3,1},{4,6},{5,7},{6,4},{7,5},{8,10},{9,11},{10,... | collective-permute-start | bytes 2359304 | tf_op jit(solution)/shard_map/ppermute | solution.py:65
  230.2 42.3 %collective-permute-start.36 = (bf16[256,1536]{1,0:T(8,128)(2,1)S(1)}, bf16[256,1536]{1,0:T(8,128)(2,1)}, u32[]{:S(2)}, u32[]{:S(2)}) collective-permute-start(bf16[256,1536]{1,0:T(8,128)(2,1)S(1)} %bitcast.321), channel_id=1, source_target_pairs={{0,1},{1,0},{2,3},{3,2},{4,5},{5,4},{6,7},{7,6},{8,9},{9,8},{10,11... | collective-permute-start | bytes 2359304 | tf_op jit(solution)/shard_map/ppermute | solution.py:65
  234.1 38.3 %collective-permute-start.32 = (bf16[2,256,384]{2,1,0:T(8,128)(2,1)}, bf16[2,256,384]{2,1,0:T(8,128)(2,1)}, u32[]{:S(2)}, u32[]{:S(2)}) collective-permute-start(bf16[2,256,384]{2,1,0:T(8,128)(2,1)} %fusion.54), channel_id=1, source_target_pairs={{0,4},{4,0},{8,12},{12,8},{16,20},{20,16},{24,28},{28,24},{1,5},{5... | collective-permute-start | bytes 1179656 | tf_op jit(solution)/shard_map/ppermute | solution.py:65
  458.3 364.4 %reduce-scatter.5.cloned.1.call-start = ((), (), s32[]{:S(2)}) async-start(), calls=%async_computation.5 | async-start | bytes 5308416 | tf_op jit(solution)/shard_map/reduce_scatter | solution.py:939
  501.9 32.1 %collective-permute-start.67 = (bf16[512,384]{1,0:T(8,128)(2,1)}, bf16[512,384]{1,0:T(8,128)(2,1)S(1)}, u32[]{:S(2)}, u32[]{:S(2)}) collective-permute-start(bf16[512,384]{1,0:T(8,128)(2,1)} %get-tuple-element.377), channel_id=1, source_target_pairs={{8,0},{16,8},{24,16},{4,12},{12,20},{20,28},{9,1},{17,9},{25,17},{... | collective-permute-start | bytes 1179656 | tf_op jit(solution)/shard_map/ppermute | solution.py:65
  534.2 33.0 %collective-permute-start.70 = (bf16[1024,384]{1,0:T(8,128)(2,1)}, bf16[1024,384]{1,0:T(8,128)(2,1)S(1)}, u32[]{:S(2)}, u32[]{:S(2)}) collective-permute-start(bf16[1024,384]{1,0:T(8,128)(2,1)} %get-tuple-element.396), channel_id=1, source_target_pairs={{8,0},{16,8},{24,16},{4,12},{12,20},{20,28},{9,1},{17,9},{25,17},{... | collective-permute-start | bytes 2359304 | tf_op jit(solution)/shard_map/ppermute | solution.py:65
  567.8 38.2 %collective-permute-start.74 = (bf16[1024,384]{1,0:T(8,128)(2,1)S(1)}, bf16[1024,384]{1,0:T(8,128)(2,1)S(1)}, u32[]{:S(2)}, u32[]{:S(2)}) collective-permute-start(bf16[1024,384]{1,0:T(8,128)(2,1)S(1)} %add_convert_fusion.3), channel_id=1, source_target_pairs={{0,4},{4,0},{8,12},{12,8},{16,20},{20,16},{24,28},{28,24},{1,5},{5... | collective-permute-start | bytes 2359304 | tf_op jit(solution)/shard_map/ppermute | solution.py:65
  568.4 37.6 %collective-permute-start.75 = (bf16[1024,384]{1,0:T(8,128)(2,1)S(1)}, bf16[1024,384]{1,0:T(8,128)(2,1)S(1)}, u32[]{:S(2)}, u32[]{:S(2)}) collective-permute-start(bf16[1024,384]{1,0:T(8,128)(2,1)S(1)} %copy-done.167), channel_id=1, source_target_pairs={{0,8},{8,16},{16,24},{12,4},{20,12},{28,20},{1,9},{9,17},{17,25},{... | collective-permute-start | bytes 2359304 | tf_op jit(solution)/shard_map/ppermute | solution.py:65
  572.5 33.4 %collective-permute-start.71 = (bf16[512,384]{1,0:T(8,128)(2,1)S(1)}, bf16[512,384]{1,0:T(8,128)(2,1)S(1)}, u32[]{:S(2)}, u32[]{:S(2)}) collective-permute-start(bf16[512,384]{1,0:T(8,128)(2,1)S(1)} %add_convert_fusion.7), channel_id=1, source_target_pairs={{0,4},{4,0},{8,12},{12,8},{16,20},{20,16},{24,28},{28,24},{1,5},{5... | collective-permute-start | bytes 1179656 | tf_op jit(solution)/shard_map/ppermute | solution.py:65
  572.6 33.4 %collective-permute-start.72 = (bf16[512,384]{1,0:T(8,128)(2,1)S(1)}, bf16[512,384]{1,0:T(8,128)(2,1)S(1)}, u32[]{:S(2)}, u32[]{:S(2)}) collective-permute-start(bf16[512,384]{1,0:T(8,128)(2,1)S(1)} %get-tuple-element.411), channel_id=1, source_target_pairs={{8,0},{12,4},{16,8},{20,12},{24,16},{28,20},{9,1},{13,5},{17,9},{2... | collective-permute-start | bytes 1179656 | tf_op jit(solution)/shard_map/ppermute | solution.py:65
  573.9 32.1 %collective-permute-start.73 = (bf16[512,384]{1,0:T(8,128)(2,1)S(1)}, bf16[512,384]{1,0:T(8,128)(2,1)S(1)}, u32[]{:S(2)}, u32[]{:S(2)}) collective-permute-start(bf16[512,384]{1,0:T(8,128)(2,1)S(1)} %get-tuple-element.412), channel_id=1, source_target_pairs={{0,8},{4,12},{8,16},{12,20},{16,24},{20,28},{1,9},{5,13},{9,17},{1... | collective-permute-start | bytes 1179656 | tf_op jit(solution)/shard_map/ppermute | solution.py:65
  610.2 72.6 %collective-permute-start.76 = (bf16[1024,384]{1,0:T(8,128)(2,1)}, bf16[1024,384]{1,0:T(8,128)(2,1)}, u32[]{:S(2)}, u32[]{:S(2)}) collective-permute-start(bf16[1024,384]{1,0:T(8,128)(2,1)} %add_convert_fusion.2), channel_id=1, source_target_pairs={{0,4},{4,0},{8,12},{12,8},{16,20},{20,16},{24,28},{28,24},{1,5},{5... | collective-permute-start | bytes 2359304 | tf_op jit(solution)/shard_map/ppermute | solution.py:65
  612.7 70.1 %collective-permute-start.77 = (bf16[1024,384]{1,0:T(8,128)(2,1)}, bf16[1024,384]{1,0:T(8,128)(2,1)}, u32[]{:S(2)}, u32[]{:S(2)}) collective-permute-start(bf16[1024,384]{1,0:T(8,128)(2,1)} %get-tuple-element.425), channel_id=1, source_target_pairs={{8,0},{12,4},{16,8},{20,12},{24,16},{28,20},{9,1},{13,5},{17,9},{2... | collective-permute-start | bytes 2359304 | tf_op jit(solution)/shard_map/ppermute | solution.py:65
  614.0 68.9 %collective-permute-start.78 = (bf16[1024,384]{1,0:T(8,128)(2,1)}, bf16[1024,384]{1,0:T(8,128)(2,1)}, u32[]{:S(2)}, u32[]{:S(2)}) collective-permute-start(bf16[1024,384]{1,0:T(8,128)(2,1)} %get-tuple-element.426), channel_id=1, source_target_pairs={{0,8},{4,12},{8,16},{12,20},{16,24},{20,28},{1,9},{5,13},{9,17},{1... | collective-permute-start | bytes 2359304 | tf_op jit(solution)/shard_map/ppermute | solution.py:65
  624.9 53.8 %collective-permute-start.79 = (bf16[256,384]{1,0:T(8,128)(2,1)S(1)}, bf16[256,384]{1,0:T(8,128)(2,1)}, u32[]{:S(2)}, u32[]{:S(2)}) collective-permute-start(bf16[256,384]{1,0:T(8,128)(2,1)S(1)} %get-tuple-element.427), channel_id=1, source_target_pairs={{0,16},{4,20},{8,24},{12,28},{16,0},{20,4},{24,8},{28,12},{1,17},{... | collective-permute-start | bytes 589832 | tf_op jit(solution)/shard_map/ppermute | solution.py:65
  627.4 55.4 %collective-permute-start.80 = (bf16[256,384]{1,0:T(8,128)(2,1)S(1)}, bf16[256,384]{1,0:T(8,128)(2,1)}, u32[]{:S(2)}, u32[]{:S(2)}) collective-permute-start(bf16[256,384]{1,0:T(8,128)(2,1)S(1)} %get-tuple-element.428), channel_id=1, source_target_pairs={{0,16},{4,20},{8,24},{12,28},{16,0},{20,4},{24,8},{28,12},{1,17},{... | collective-permute-start | bytes 589832 | tf_op jit(solution)/shard_map/ppermute | solution.py:65
  (257 other events, 3395.8 us)
Sparse Core Ops, SparseCore 0:
  10.2 84.7 all-gather.2
  97.2 180.8 all-gather.4
  458.4 214.2 reduce-scatter.2
  716.5 106.1 reduce-scatter.4

commit v6 on v3

--- a/solution.py
+++ b/solution.py
@@ -253,7 +253,7 @@
         (low, "dp", shifted(-2)),
         (high, "dp", shifted(2)),
     ]
-    return plus(own, beside, low, high)
+    return [own, beside, low, high]
 
 
 def norm_rows(values, weights):
@@ -355,33 +355,39 @@
         head_ref[0:1, here] = grad_gain
 
 
-def key_back_kernel(pre_ref, gains_ref, cos_ref, sin_ref, set_ref, out_ref, head_ref):
-    rows, width = pre_ref.shape[0], set_ref.shape[1]
+def summed(refs, rows, columns):
+    return sum(ref[rows, columns].astype(F32) for ref in refs)
+
+
+def key_back_kernel(pre_ref, gains_ref, cos_ref, sin_ref, *refs):
+    *set_refs, out_ref, head_ref = refs
+    rows, width = pre_ref.shape[0], set_refs[0].shape[1]
     cos, sin = cos_ref[...], sin_ref[...]
     head_ref[...] = jnp.zeros_like(head_ref)
     for start in range(0, width, PAIR):
         here = pl.ds(start, PAIR)
-        grad = set_ref[pl.ds(0, rows), here]
+        grad = summed(set_refs, pl.ds(0, rows), here)
         grad = grad * cos - partner(grad) * sin
         grad_pre, grad_gain = norm_back(
             pre_ref[:, pl.ds(width + start, PAIR)], gains_ref[1:2, here], grad
         )
         out_ref[:, here] = grad_pre.astype(BF)
         head_ref[0:1, here] = grad_gain
-    out_ref[:, pl.ds(width, width)] = set_ref[pl.ds(rows, rows), :].astype(BF)
-
-
-def text_back_kernel(pre_ref, gains_ref, set_ref, out_ref, head_ref):
-    rows, width = pre_ref.shape[0], set_ref.shape[1]
+        out_ref[:, pl.ds(width + start, PAIR)] = summed(set_refs, pl.ds(rows, rows), here).astype(BF)
+
+
+def text_back_kernel(pre_ref, gains_ref, *refs):
+    *set_refs, out_ref, head_ref = refs
+    rows, width = pre_ref.shape[0], set_refs[0].shape[1]
     head_ref[...] = jnp.zeros_like(head_ref)
     for start in range(0, width, PAIR):
         here = pl.ds(start, PAIR)
         grad_pre, grad_gain = norm_back(
-            pre_ref[:, here], gains_ref[2:3, here], set_ref[pl.ds(0, rows), here]
+            pre_ref[:, here], gains_ref[2:3, here], summed(set_refs, pl.ds(0, rows), here)
         )
         out_ref[:, here] = grad_pre.astype(BF)
         head_ref[0:1, here] = grad_gain
-    out_ref[:, pl.ds(width, width)] = set_ref[pl.ds(rows, rows), :].astype(BF)
+        out_ref[:, pl.ds(width + start, PAIR)] = summed(set_refs, pl.ds(rows, rows), here).astype(BF)
 
 
 def split_pair(values):
@@ -870,7 +876,7 @@
             20 * text_len * 2 * local_width,
             text_pre,
             local_gains,
-            tie(own_text),
+            *own_text,
         )
 
     grad_text_low, head_text = text_rows_backward(lambda value: value)
@@ -889,7 +895,7 @@
             local_gains,
             cos[:seq_len],
             sin[:seq_len],
-            tie(own_self),
+            *own_self,
         )
         first_part = mm(grad_query_low, qkv_full[:, :local_width], NT) + mm(
             grad_key_low, qkv_full[:, local_width:], NT

time: 826 us -> 827 us (level)
  Pallas kernels: 74.8 us -> 90.9 us
    pallas_call x4, Pallas kernels: 57.7 us -> 71.7 us  [attend(): pl.pallas_call(kernel, grid=(width // PAIR,), in_specs=[smem] * len(scala...]
  transfers between devices with their start and end apart: 106 -> 106, of which waited for: 52 -> 52; matrix products, arithmetic and copies ran while one was open for 22% -> 22% of each run, Pallas kernels for 9% -> 11%
where the time goes in v6:
time: 827 us; the launch traced here: 816 us
  waiting for transfers between devices  361 us (44%)
  starting transfers between devices  125 us (15%)
  other arithmetic  92.8 us (11%)
  Pallas kernels  90.9 us (11%)
  matrix products  68.9 us (8%)
  local copies, waits for them, and re-layouts  58.2 us (7%)
  between operations  19.1 us (2%)
    ppermute x73, waiting for transfers between devices, stage(): lax.ppermute(value, axis, pairs)  284 us
    ppermute x73, starting transfers between devices, stage(): lax.ppermute(value, axis, pairs)  105 us
    ppermute x29, waiting for transfers between devices, swap(): return lax.ppermute(value, axis, [(i, i ^ bit) for i in range(count)])  76.7 us
    pallas_call x4, Pallas kernels, attend(): pl.pallas_call(kernel, grid=(width // PAIR,), in_specs=[smem] * len(scala...  71.7 us
    dot_general x32, matrix products, mm(): return lax.dot_general(left, right, dims, preferred_element_type=F32)  68.9 us
    ppermute x29, starting transfers between devices, swap(): return lax.ppermute(value, axis, [(i, i ^ bit) for i in range(count)])  20.2 us
    unnamed x336, local copies, waits for them, and re-layouts  16.9 us
  transfers between devices with their start and end apart: 106, of which 52 were waited for; matrix products, arithmetic and copies ran while one was open for 22% of the time, Pallas kernels for 11%

profile of v6, /device:TPU:0, one launch (start us, length us, event | category | flops | bytes accessed | tf_op | source)
XLA Modules:
  0.0 816.1 jit_solution(10402093041677584166)
XLA Ops:
  46.8 11.9 %collective-permute-done.6 = bf16[2,2,64,512]{3,2,1,0:T(8,128)(2,1)S(1)} collective-permute-done((bf16[2,2,64,512]{3,2,1,0:T(8,128)(2,1)S(1)}, bf16[2,2,64,512]{3,2,1,0:T(8,128)(2,1)S(1)}, u32[]{:S(2)}, u32[]{:S(2)}) %collective-permute-start.6) | collective-permute-done | bytes 262176 | tf_op jit(solution)/shard_map/ppermute | solution.py:65
  60.0 22.1 %collective-permute-done.8 = bf16[128,1536]{1,0:T(8,128)(2,1)} collective-permute-done((bf16[128,1536]{1,0:T(8,128)(2,1)}, bf16[128,1536]{1,0:T(8,128)(2,1)}, u32[]{:S(2)}, u32[]{:S(2)}) %collective-permute-start.8) | collective-permute-done | bytes 393248 | tf_op jit(solution)/shard_map/ppermute | solution.py:65
  90.3 8.3 %collective-permute-done.10 = bf16[2,2,64,512]{3,2,1,0:T(8,128)(2,1)S(1)} collective-permute-done((bf16[2,2,64,512]{3,2,1,0:T(8,128)(2,1)S(1)}, bf16[2,2,64,512]{3,2,1,0:T(8,128)(2,1)S(1)}, u32[]{:S(2)}, u32[]{:S(2)}) %collective-permute-start.10) | collective-permute-done | bytes 262176 | tf_op jit(solution)/shard_map/ppermute | solution.py:65
  108.6 5.1 collective-permute-done.13
  119.7 5.9 collective-permute-done.15
  130.1 5.8 collective-permute-done.17
  153.7 8.6 %sine_multiply_fusion = (f32[3584,128]{1,0:T(8,128)}, f32[3584,128]{1,0:T(8,128)}) fusion(f32[128]{0:T(128)S(1)} %copy-done.147, f32[128]{0:T(128)S(1)} %copy-done.148, s32[3584]{0:T(1024)S(1)} %copy-done.121, s32[3584]{0:T(1024)S(1)} %copy-done.122, pred[128]{0:T(512)(128)(4,1)S(1)} %copy-done.149), kind=kLoop, calls=%fused_computation.40 | loop fusion | flops 1835008 | bytes 3699840 | tf_op jit(solution)/shard_map/mul | solution.py:710
  166.4 9.6 %collective-permute-done.20 = bf16[2,2,256,384]{3,2,0,1:T(8,128)(2,1)} collective-permute-done((bf16[2,2,256,384]{3,2,0,1:T(8,128)(2,1)}, bf16[2,2,256,384]{3,2,0,1:T(8,128)(2,1)}, u32[]{:S(2)}, u32[]{:S(2)}) %collective-permute-start.20) | collective-permute-done | bytes 786464 | tf_op jit(solution)/shard_map/ppermute | solution.py:65
  176.0 21.3 %collective-permute-done.21 = bf16[2,2,256,384]{3,2,0,1:T(8,128)(2,1)S(1)} collective-permute-done((bf16[2,2,256,384]{3,2,0,1:T(8,128)(2,1)}, bf16[2,2,256,384]{3,2,0,1:T(8,128)(2,1)S(1)}, u32[]{:S(2)}, u32[]{:S(2)}) %collective-permute-start.21) | collective-permute-done | bytes 786464 | tf_op jit(solution)/shard_map/ppermute | solution.py:65
  206.9 18.9 %collective-permute-done.26 = bf16[2,256,384]{2,1,0:T(8,128)(2,1)} collective-permute-done((bf16[2,256,384]{2,1,0:T(8,128)(2,1)S(1)}, bf16[2,256,384]{2,1,0:T(8,128)(2,1)}, u32[]{:S(2)}, u32[]{:S(2)}) %collective-permute-start.26) | collective-permute-done | bytes 393248 | tf_op jit(solution)/shard_map/ppermute | solution.py:65
  265.2 12.0 %collective-permute-done.33 = bf16[256,384]{1,0:T(8,128)(2,1)} collective-permute-done((bf16[256,384]{1,0:T(8,128)(2,1)}, bf16[256,384]{1,0:T(8,128)(2,1)}, u32[]{:S(2)}, u32[]{:S(2)}) %collective-permute-start.33) | collective-permute-done | bytes 196640 | tf_op jit(solution)/shard_map/ppermute | solution.py:65
  316.6 12.6 %shard_map.295 = (f32[512,384]{1,0:T(8,128)}, f32[512,384]{1,0:T(8,128)}) custom-call(s32[7]{0:T(128)} %and_convert_fusion.live_ref, bf16[512,384]{1,0:T(8,128)(2,1)} %slice.353.query_ref, bf16[1024,384]{1,0:T(8,128)(2,1)} %slice.358.own_ref, bf16[2048,384]{1,0:T(8,128)(2,1)} %copy-done.11, bf16[2048,384]{1,0:T(8,128)(2,1)} %copy-done.12, ...), custom_call_target="tpu_custom_call" | custom-call | flops 3221225472 | bytes 7864320 | tf_op jit(solution)/shard_map/pallas_call | solution.py:563
  329.9 9.5 %shard_map.296 = (bf16[512,384]{1,0:T(8,128)(2,1)}, f32[512,384]{1,0:T(8,128)}, f32[512,384]{1,0:T(8,128)}) custom-call(s32[7]{0:T(128)} %and_convert_fusion.live_ref, f32[6]{0:T(128)} %dynamic-slice_tanh_fusion.2.gate_ref, bf16[512,384]{1,0:T(8,128)(2,1)} %slice.353.query_ref, f32[512,384]{1,0:T(8,128)} %get-tuple-element.343.self_ref.out_ref, ...), custom_call_target="tpu_custom_call" | custom-call | flops 1610612736 | bytes 7864320 | tf_op jit(solution)/shard_map/pallas_call | solution.py:563
  345.6 9.7 %collective-permute-done.46 = bf16[128,1536]{1,0:T(8,128)(2,1)S(1)} collective-permute-done((bf16[128,1536]{1,0:T(8,128)(2,1)S(1)}, bf16[128,1536]{1,0:T(8,128)(2,1)S(1)}, u32[]{:S(2)}, u32[]{:S(2)}) %collective-permute-start.46) | collective-permute-done | bytes 393248 | tf_op jit(solution)/shard_map/ppermute | solution.py:31
  359.6 8.9 %collective-permute-done.48 = bf16[128,1536]{1,0:T(8,128)(2,1)S(1)} collective-permute-done((bf16[128,1536]{1,0:T(8,128)(2,1)S(1)}, bf16[128,1536]{1,0:T(8,128)(2,1)S(1)}, u32[]{:S(2)}, u32[]{:S(2)}) %collective-permute-start.48) | collective-permute-done | bytes 393248 | tf_op jit(solution)/shard_map/ppermute | solution.py:31
  379.6 9.7 %collective-permute-done.52 = bf16[128,1536]{1,0:T(8,128)(2,1)S(1)} collective-permute-done((bf16[128,1536]{1,0:T(8,128)(2,1)S(1)}, bf16[128,1536]{1,0:T(8,128)(2,1)S(1)}, u32[]{:S(2)}, u32[]{:S(2)}) %collective-permute-start.52) | collective-permute-done | bytes 393248 | tf_op jit(solution)/shard_map/ppermute | solution.py:31
  392.9 8.9 %collective-permute-done.54 = bf16[128,1536]{1,0:T(8,128)(2,1)S(1)} collective-permute-done((bf16[128,1536]{1,0:T(8,128)(2,1)S(1)}, bf16[128,1536]{1,0:T(8,128)(2,1)S(1)}, u32[]{:S(2)}, u32[]{:S(2)}) %collective-permute-start.54) | collective-permute-done | bytes 393248 | tf_op jit(solution)/shard_map/ppermute | solution.py:31
  410.8 5.3 convolution_convert_fusion
  424.9 5.4 collective-permute-done.58
  441.7 9.2 %collective-permute-done.60 = bf16[128,1536]{1,0:T(8,128)(2,1)} collective-permute-done((bf16[128,1536]{1,0:T(8,128)(2,1)}, bf16[128,1536]{1,0:T(8,128)(2,1)}, u32[]{:S(2)}, u32[]{:S(2)}) %collective-permute-start.60) | collective-permute-done | bytes 393248 | tf_op jit(solution)/shard_map/ppermute | solution.py:31
  457.4 18.9 %shard_map.297 = (bf16[512,384]{1,0:T(8,128)(2,1)}, bf16[512,384]{1,0:T(8,128)(2,1)}, bf16[512,384]{1,0:T(8,128)(2,1)}, bf16[512,384]{1,0:T(8,128)(2,1)}, bf16[5...) custom-call(s32[7]{0:T(128)} %and_convert_fusion.live_ref, ...), custom_call_target="tpu_custom_call" | custom-call | flops 4026531840 | bytes 7864320 | tf_op jit(solution)/shard_map/pallas_call | solution.py:563
  477.7 30.7 %shard_map.298 = (bf16[1024,384]{1,0:T(8,128)(2,1)}, bf16[1024,384]{1,0:T(8,128)(2,1)}, bf16[1024,384]{1,0:T(8,128)(2,1)}, bf16[1024,384]{1,0:T(8,128)(2,1)}, bf...) custom-call(s32[7]{0:T(128)} %and_convert_fusion.live_ref, ...), custom_call_target="tpu_custom_call" | custom-call | flops 8053063680 | bytes 7864320 | tf_op jit(solution)/shard_map/pallas_call | solution.py:563
  510.0 7.0 collective-permute-start.63
  530.1 15.6 %collective-permute-done.65 = bf16[1024,384]{1,0:T(8,128)(2,1)S(1)} collective-permute-done((bf16[1024,384]{1,0:T(8,128)(2,1)}, bf16[1024,384]{1,0:T(8,128)(2,1)S(1)}, u32[]{:S(2)}, u32[]{:S(2)}) %collective-permute-start.65) | collective-permute-done | bytes 786464 | tf_op jit(solution)/shard_map/ppermute | solution.py:65
  557.0 28.9 %collective-permute-done.66.refs_1_ = bf16[512,384]{1,0:T(8,128)(2,1)S(1)} collective-permute-done((bf16[512,384]{1,0:T(8,128)(2,1)S(1)}, bf16[512,384]{1,0:T(8,128)(2,1)S(1)}, u32[]{:S(2)}, u32[]{:S(2)}) %collective-permute-start.66) | collective-permute-done | bytes 393248 | tf_op jit(solution)/shard_map/ppermute | solution.py:65
  592.0 5.7 collective-permute-start.73
  606.2 54.3 %collective-permute-done.74 = bf16[256,384]{1,0:T(8,128)(2,1)} collective-permute-done((bf16[256,384]{1,0:T(8,128)(2,1)S(1)}, bf16[256,384]{1,0:T(8,128)(2,1)}, u32[]{:S(2)}, u32[]{:S(2)}) %collective-permute-start.74) | collective-permute-done | bytes 196640 | tf_op jit(solution)/shard_map/ppermute | solution.py:65
  725.7 8.8 %collective-permute-done.90 = bf16[512,512]{1,0:T(8,128)(2,1)S(1)} collective-permute-done((bf16[512,512]{1,0:T(8,128)(2,1)S(1)}, bf16[512,512]{1,0:T(8,128)(2,1)S(1)}, u32[]{:S(2)}, u32[]{:S(2)}) %collective-permute-start.90) | collective-permute-done | bytes 524320 | tf_op jit(solution)/shard_map/ppermute | solution.py:31
  746.5 7.1 collective-permute-done.92
  767.8 6.0 collective-permute-done.96
  778.3 5.5 collective-permute-done.97
  784.5 18.2 %collective-permute-done.101 = f32[20,1536]{1,0:T(8,128)S(1)} collective-permute-done((f32[20,1536]{1,0:T(8,128)S(1)}, f32[20,1536]{1,0:T(8,128)S(1)}, u32[]{:S(2)}, u32[]{:S(2)}) %collective-permute-start.101) | collective-permute-done | bytes 122912 | tf_op jit(solution)/shard_map/ppermute | solution.py:65
  (786 shorter events, 381.5 us)
Async XLA Ops:
  7.2 235.9 %all-gather.3.cloned.1.call-start = ((), (), s32[]{:S(2)}) async-start(), calls=%async_computation.2 | async-start | bytes 3981312 | tf_op jit(solution)/shard_map/all_gather | solution.py:621
  9.2 330.2 %all-gather.5.cloned.1.call-start = ((), (), s32[]{:S(2)}) async-start(), calls=%async_computation.3 | async-start | bytes 11943936 | tf_op jit(solution)/shard_map/all_gather | solution.py:622
  9.3 28.7 %collective-permute-start.2 = (bf16[128,1536]{1,0:T(8,128)(2,1)}, bf16[128,1536]{1,0:T(8,128)(2,1)}, u32[]{:S(2)}, u32[]{:S(2)}) collective-permute-start(bf16[128,1536]{1,0:T(8,128)(2,1)} %param.19), channel_id=1, source_target_pairs={{0,4},{4,0},{8,12},{12,8},{16,20},{20,16},{24,28},{28,24},{1,5},{5... | collective-permute-start | bytes 1179656 | tf_op jit(solution)/shard_map/ppermute | solution.py:65
  12.3 25.7 %collective-permute-start.3 = (bf16[128,1536]{1,0:T(8,128)(2,1)}, bf16[128,1536]{1,0:T(8,128)(2,1)S(1)}, u32[]{:S(2)}, u32[]{:S(2)}) collective-permute-start(bf16[128,1536]{1,0:T(8,128)(2,1)} %param.19), channel_id=1, source_target_pairs={{0,8},{4,12},{8,16},{12,20},{16,24},{20,28},{1,9},{5,13},{9,17},{1... | collective-permute-start | bytes 1179656 | tf_op jit(solution)/shard_map/ppermute | solution.py:65
  23.0 646.5 %reduce-scatter.3.cloned.1.call-start = ((), (), s32[]{:S(2)}) async-start(), calls=%async_computation.4 | async-start | bytes 10616832 | tf_op jit(solution)/shard_map/reduce_scatter | solution.py:806
  45.5 36.6 %collective-permute-start.8 = (bf16[128,1536]{1,0:T(8,128)(2,1)}, bf16[128,1536]{1,0:T(8,128)(2,1)}, u32[]{:S(2)}, u32[]{:S(2)}) collective-permute-start(bf16[128,1536]{1,0:T(8,128)(2,1)} %collective-permute-done.2), channel_id=1, source_target_pairs={{8,0},{16,8},{24,16},{4,12},{12,20},{20,28},{9,1},{17,9},{25,17},{... | collective-permute-start | bytes 1179656 | tf_op jit(solution)/shard_map/ppermute | solution.py:65
  146.8 29.2 %collective-permute-start.20 = (bf16[2,2,256,384]{3,2,0,1:T(8,128)(2,1)}, bf16[2,2,256,384]{3,2,0,1:T(8,128)(2,1)}, u32[]{:S(2)}, u32[]{:S(2)}) collective-permute-start(bf16[2,2,256,384]{3,2,0,1:T(8,128)(2,1)} %select_bitcast_fusion.5), channel_id=1, source_target_pairs={{0,4},{4,0},{8,12},{12,8},{16,20},{20,16},{24,28},{28,24},{1,5},{5... | collective-permute-start | bytes 2359304 | tf_op jit(solution)/shard_map/ppermute | solution.py:65
  151.7 45.7 %collective-permute-start.21 = (bf16[2,2,256,384]{3,2,0,1:T(8,128)(2,1)}, bf16[2,2,256,384]{3,2,0,1:T(8,128)(2,1)S(1)}, u32[]{:S(2)}, u32[]{:S(2)}) collective-permute-start(bf16[2,2,256,384]{3,2,0,1:T(8,128)(2,1)} %select_bitcast_fusion.4), channel_id=1, source_target_pairs={{0,8},{4,12},{8,0},{12,4},{16,24},{20,28},{24,16},{28,20},{1,9},{5... | collective-permute-start | bytes 2359304 | tf_op jit(solution)/shard_map/ppermute | solution.py:65
  153.1 44.2 %collective-permute-start.24 = (bf16[256,1536]{1,0:T(8,128)(2,1)S(1)}, bf16[256,1536]{1,0:T(8,128)(2,1)}, u32[]{:S(2)}, u32[]{:S(2)}) collective-permute-start(bf16[256,1536]{1,0:T(8,128)(2,1)S(1)} %bitcast.352), channel_id=1, source_target_pairs={{0,2},{1,3},{2,0},{3,1},{4,6},{5,7},{6,4},{7,5},{8,10},{9,11},{10,... | collective-permute-start | bytes 2359304 | tf_op jit(solution)/shard_map/ppermute | solution.py:65
  153.7 44.5 %collective-permute-start.25 = (bf16[256,1536]{1,0:T(8,128)(2,1)S(1)}, bf16[256,1536]{1,0:T(8,128)(2,1)}, u32[]{:S(2)}, u32[]{:S(2)}) collective-permute-start(bf16[256,1536]{1,0:T(8,128)(2,1)S(1)} %bitcast.353), channel_id=1, source_target_pairs={{0,1},{1,0},{2,3},{3,2},{4,5},{5,4},{6,7},{7,6},{8,9},{9,8},{10,11... | collective-permute-start | bytes 2359304 | tf_op jit(solution)/shard_map/ppermute | solution.py:65
  202.1 29.8 %collective-permute-start.29 = (bf16[256,1536]{1,0:T(8,128)(2,1)}, bf16[256,1536]{1,0:T(8,128)(2,1)}, u32[]{:S(2)}, u32[]{:S(2)}) collective-permute-start(bf16[256,1536]{1,0:T(8,128)(2,1)} %collective-permute-done.24), channel_id=1, source_target_pairs={{0,1},{1,0},{2,3},{3,2},{4,5},{5,4},{6,7},{7,6},{8,9},{9,8},{10,11... | collective-permute-start | bytes 2359304 | tf_op jit(solution)/shard_map/ppermute | solution.py:65
  202.1 29.8 %collective-permute-start.30 = (bf16[256,1536]{1,0:T(8,128)(2,1)S(1)}, bf16[256,1536]{1,0:T(8,128)(2,1)}, u32[]{:S(2)}, u32[]{:S(2)}) collective-permute-start(bf16[256,1536]{1,0:T(8,128)(2,1)S(1)} %bitcast.349), channel_id=1, source_target_pairs={{0,2},{1,3},{2,0},{3,1},{4,6},{5,7},{6,4},{7,5},{8,10},{9,11},{10,... | collective-permute-start | bytes 2359304 | tf_op jit(solution)/shard_map/ppermute | solution.py:65
  203.1 28.7 %collective-permute-start.31 = (bf16[256,1536]{1,0:T(8,128)(2,1)S(1)}, bf16[256,1536]{1,0:T(8,128)(2,1)}, u32[]{:S(2)}, u32[]{:S(2)}) collective-permute-start(bf16[256,1536]{1,0:T(8,128)(2,1)S(1)} %bitcast.350), channel_id=1, source_target_pairs={{0,1},{1,0},{2,3},{3,2},{4,5},{5,4},{6,7},{7,6},{8,9},{9,8},{10,11... | collective-permute-start | bytes 2359304 | tf_op jit(solution)/shard_map/ppermute | solution.py:65
  206.9 24.9 %collective-permute-start.27 = (bf16[2,256,384]{2,1,0:T(8,128)(2,1)}, bf16[2,256,384]{2,1,0:T(8,128)(2,1)}, u32[]{:S(2)}, u32[]{:S(2)}) collective-permute-start(bf16[2,256,384]{2,1,0:T(8,128)(2,1)} %fusion.54), channel_id=1, source_target_pairs={{0,4},{4,0},{8,12},{12,8},{16,20},{20,16},{24,28},{28,24},{1,5},{5... | collective-permute-start | bytes 1179656 | tf_op jit(solution)/shard_map/ppermute | solution.py:65
  236.1 29.1 %collective-permute-start.32 = (bf16[256,384]{1,0:T(8,128)(2,1)}, bf16[256,384]{1,0:T(8,128)(2,1)}, u32[]{:S(2)}, u32[]{:S(2)}) collective-permute-start(bf16[256,384]{1,0:T(8,128)(2,1)} %get-tuple-element.294), channel_id=1, source_target_pairs={{0,16},{4,20},{8,24},{12,28},{16,0},{20,4},{24,8},{28,12},{1,17},{... | collective-permute-start | bytes 589832 | tf_op jit(solution)/shard_map/ppermute | solution.py:65
  236.1 41.1 %collective-permute-start.33 = (bf16[256,384]{1,0:T(8,128)(2,1)}, bf16[256,384]{1,0:T(8,128)(2,1)}, u32[]{:S(2)}, u32[]{:S(2)}) collective-permute-start(bf16[256,384]{1,0:T(8,128)(2,1)} %get-tuple-element.295), channel_id=1, source_target_pairs={{0,16},{4,20},{8,24},{12,28},{16,0},{20,4},{24,8},{28,12},{1,17},{... | collective-permute-start | bytes 589832 | tf_op jit(solution)/shard_map/ppermute | solution.py:65
  239.0 38.2 %collective-permute-start.34 = (bf16[256,1536]{1,0:T(8,128)(2,1)}, bf16[256,1536]{1,0:T(8,128)(2,1)}, u32[]{:S(2)}, u32[]{:S(2)}) collective-permute-start(bf16[256,1536]{1,0:T(8,128)(2,1)} %collective-permute-done.30), channel_id=1, source_target_pairs={{0,1},{1,0},{2,3},{3,2},{4,5},{5,4},{6,7},{7,6},{8,9},{9,8},{10,11... | collective-permute-start | bytes 2359304 | tf_op jit(solution)/shard_map/ppermute | solution.py:65
  239.0 38.2 %collective-permute-start.35 = (bf16[256,1536]{1,0:T(8,128)(2,1)}, bf16[256,1536]{1,0:T(8,128)(2,1)}, u32[]{:S(2)}, u32[]{:S(2)}) collective-permute-start(bf16[256,1536]{1,0:T(8,128)(2,1)} %bitcast.57), channel_id=1, source_target_pairs={{0,2},{1,3},{2,0},{3,1},{4,6},{5,7},{6,4},{7,5},{8,10},{9,11},{10,... | collective-permute-start | bytes 2359304 | tf_op jit(solution)/shard_map/ppermute | solution.py:65
  240.4 36.8 %collective-permute-start.36 = (bf16[256,1536]{1,0:T(8,128)(2,1)}, bf16[256,1536]{1,0:T(8,128)(2,1)}, u32[]{:S(2)}, u32[]{:S(2)}) collective-permute-start(bf16[256,1536]{1,0:T(8,128)(2,1)} %bitcast.57), channel_id=1, source_target_pairs={{0,1},{1,0},{2,3},{3,2},{4,5},{5,4},{6,7},{7,6},{8,9},{9,8},{10,11... | collective-permute-start | bytes 2359304 | tf_op jit(solution)/shard_map/ppermute | solution.py:65
  432.6 373.9 %reduce-scatter.5.cloned.1.call-start = ((), (), s32[]{:S(2)}) async-start(), calls=%async_computation.5 | async-start | bytes 5308416 | tf_op jit(solution)/shard_map/reduce_scatter | solution.py:927
  476.3 32.2 %collective-permute-start.62 = (bf16[512,384]{1,0:T(8,128)(2,1)}, bf16[512,384]{1,0:T(8,128)(2,1)S(1)}, u32[]{:S(2)}, u32[]{:S(2)}) collective-permute-start(bf16[512,384]{1,0:T(8,128)(2,1)} %get-tuple-element.362), channel_id=1, source_target_pairs={{8,0},{16,8},{24,16},{4,12},{12,20},{20,28},{9,1},{17,9},{25,17},{... | collective-permute-start | bytes 1179656 | tf_op jit(solution)/shard_map/ppermute | solution.py:65
  508.6 37.1 %collective-permute-start.65 = (bf16[1024,384]{1,0:T(8,128)(2,1)}, bf16[1024,384]{1,0:T(8,128)(2,1)S(1)}, u32[]{:S(2)}, u32[]{:S(2)}) collective-permute-start(bf16[1024,384]{1,0:T(8,128)(2,1)} %get-tuple-element.381), channel_id=1, source_target_pairs={{8,0},{16,8},{24,16},{4,12},{12,20},{20,28},{9,1},{17,9},{25,17},{... | collective-permute-start | bytes 2359304 | tf_op jit(solution)/shard_map/ppermute | solution.py:65
  546.3 39.6 %collective-permute-start.69 = (bf16[1024,384]{1,0:T(8,128)(2,1)S(1)}, bf16[1024,384]{1,0:T(8,128)(2,1)S(1)}, u32[]{:S(2)}, u32[]{:S(2)}) collective-permute-start(bf16[1024,384]{1,0:T(8,128)(2,1)S(1)} %add_convert_fusion.3), channel_id=1, source_target_pairs={{0,4},{4,0},{8,12},{12,8},{16,20},{20,16},{24,28},{28,24},{1,5},{5... | collective-permute-start | bytes 2359304 | tf_op jit(solution)/shard_map/ppermute | solution.py:65
  547.0 39.0 %collective-permute-start.70 = (bf16[1024,384]{1,0:T(8,128)(2,1)S(1)}, bf16[1024,384]{1,0:T(8,128)(2,1)S(1)}, u32[]{:S(2)}, u32[]{:S(2)}) collective-permute-start(bf16[1024,384]{1,0:T(8,128)(2,1)S(1)} %copy-done.156), channel_id=1, source_target_pairs={{0,8},{8,16},{16,24},{12,4},{20,12},{28,20},{1,9},{9,17},{17,25},{... | collective-permute-start | bytes 2359304 | tf_op jit(solution)/shard_map/ppermute | solution.py:65
  551.1 34.9 %collective-permute-start.66 = (bf16[512,384]{1,0:T(8,128)(2,1)S(1)}, bf16[512,384]{1,0:T(8,128)(2,1)S(1)}, u32[]{:S(2)}, u32[]{:S(2)}) collective-permute-start(bf16[512,384]{1,0:T(8,128)(2,1)S(1)} %add_convert_fusion.7), channel_id=1, source_target_pairs={{0,4},{4,0},{8,12},{12,8},{16,20},{20,16},{24,28},{28,24},{1,5},{5... | collective-permute-start | bytes 1179656 | tf_op jit(solution)/shard_map/ppermute | solution.py:65
  551.1 34.8 %collective-permute-start.67 = (bf16[512,384]{1,0:T(8,128)(2,1)S(1)}, bf16[512,384]{1,0:T(8,128)(2,1)S(1)}, u32[]{:S(2)}, u32[]{:S(2)}) collective-permute-start(bf16[512,384]{1,0:T(8,128)(2,1)S(1)} %get-tuple-element.396), channel_id=1, source_target_pairs={{8,0},{12,4},{16,8},{20,12},{24,16},{28,20},{9,1},{13,5},{17,9},{2... | collective-permute-start | bytes 1179656 | tf_op jit(solution)/shard_map/ppermute | solution.py:65
  552.4 33.5 %collective-permute-start.68 = (bf16[512,384]{1,0:T(8,128)(2,1)S(1)}, bf16[512,384]{1,0:T(8,128)(2,1)S(1)}, u32[]{:S(2)}, u32[]{:S(2)}) collective-permute-start(bf16[512,384]{1,0:T(8,128)(2,1)S(1)} %get-tuple-element.397), channel_id=1, source_target_pairs={{0,8},{4,12},{8,16},{12,20},{16,24},{20,28},{1,9},{5,13},{9,17},{1... | collective-permute-start | bytes 1179656 | tf_op jit(solution)/shard_map/ppermute | solution.py:65
  589.3 75.2 %collective-permute-start.71 = (bf16[1024,384]{1,0:T(8,128)(2,1)}, bf16[1024,384]{1,0:T(8,128)(2,1)}, u32[]{:S(2)}, u32[]{:S(2)}) collective-permute-start(bf16[1024,384]{1,0:T(8,128)(2,1)} %add_convert_fusion.2), channel_id=1, source_target_pairs={{0,4},{4,0},{8,12},{12,8},{16,20},{20,16},{24,28},{28,24},{1,5},{5... | collective-permute-start | bytes 2359304 | tf_op jit(solution)/shard_map/ppermute | solution.py:65
  590.7 73.8 %collective-permute-start.72 = (bf16[1024,384]{1,0:T(8,128)(2,1)}, bf16[1024,384]{1,0:T(8,128)(2,1)}, u32[]{:S(2)}, u32[]{:S(2)}) collective-permute-start(bf16[1024,384]{1,0:T(8,128)(2,1)} %get-tuple-element.410), channel_id=1, source_target_pairs={{8,0},{12,4},{16,8},{20,12},{24,16},{28,20},{9,1},{13,5},{17,9},{2... | collective-permute-start | bytes 2359304 | tf_op jit(solution)/shard_map/ppermute | solution.py:65
  592.0 72.5 %collective-permute-start.73 = (bf16[1024,384]{1,0:T(8,128)(2,1)}, bf16[1024,384]{1,0:T(8,128)(2,1)}, u32[]{:S(2)}, u32[]{:S(2)}) collective-permute-start(bf16[1024,384]{1,0:T(8,128)(2,1)} %get-tuple-element.411), channel_id=1, source_target_pairs={{0,8},{4,12},{8,16},{12,20},{16,24},{20,28},{1,9},{5,13},{9,17},{1... | collective-permute-start | bytes 2359304 | tf_op jit(solution)/shard_map/ppermute | solution.py:65
  602.9 57.7 %collective-permute-start.74 = (bf16[256,384]{1,0:T(8,128)(2,1)S(1)}, bf16[256,384]{1,0:T(8,128)(2,1)}, u32[]{:S(2)}, u32[]{:S(2)}) collective-permute-start(bf16[256,384]{1,0:T(8,128)(2,1)S(1)} %get-tuple-element.412), channel_id=1, source_target_pairs={{0,16},{4,20},{8,24},{12,28},{16,0},{20,4},{24,8},{28,12},{1,17},{... | collective-permute-start | bytes 589832 | tf_op jit(solution)/shard_map/ppermute | solution.py:65
  606.0 58.5 %collective-permute-start.75 = (bf16[256,384]{1,0:T(8,128)(2,1)S(1)}, bf16[256,384]{1,0:T(8,128)(2,1)}, u32[]{:S(2)}, u32[]{:S(2)}) collective-permute-start(bf16[256,384]{1,0:T(8,128)(2,1)S(1)} %get-tuple-element.413), channel_id=1, source_target_pairs={{0,16},{4,20},{8,24},{12,28},{16,0},{20,4},{24,8},{28,12},{1,17},{... | collective-permute-start | bytes 589832 | tf_op jit(solution)/shard_map/ppermute | solution.py:65
  (238 other events, 2644.9 us)
Sparse Core Ops, SparseCore 0:
  10.2 85.5 all-gather.2
  98.0 181.7 all-gather.4
  432.7 224.9 reduce-scatter.2
  698.4 107.0 reduce-scatter.4
